TPU v7x, 32 devices: a whole 2x2x4 slice. The times are simulated.
32 devices in a mesh: layer: 2 (over core), feat: 16 (over z, y, x).
Axes of the slice: x: 2, y: 2, z: 4, core: 2. Of those that a mesh axis runs over, the one named last changes fastest.
Arguments:
- source: float32 [2, 64, 2048], P('layer', 'feat'), may hold values from -6 to 6
- w_enc: bfloat16 [2, 2048, 24576], P('layer', None, 'feat'), may hold values from -0.125 to 0.125
- b_enc: float32 [2, 24576], P('layer', 'feat'), may hold values from -3 to 3
- threshold: float32 [2, 24576], P('layer', 'feat'), may hold values from 0.2 to 2
- dec_self: bfloat16 [2, 24576, 2048], P('layer', 'feat'), may hold values from -0.0390625 to 0.0390625
- dec_next: bfloat16 [2, 24576, 2048], P('layer', 'feat'), may hold values from -0.0390625 to 0.0390625
- target: float32 [2, 64, 2048], P('layer', 'feat'), may hold values from -3 to 3
Outputs:
- residual: float32 [2, 64, 2048], P('layer', 'feat')
All inputs are finite; a program needn't handle non-finite values.
Results may differ from a plain program's by a relative error of at most 0.0038.
Values may be sent and summed in bfloat16 or wider, within the bound.
No kernel may reach another device: no remote copies, remote signals or barrier semaphores. Data moves between devices by JAX's collectives and lax.ppermute only.
A program may use at most 64 MiB of HBM per device.

v0:
```python
import jax
import jax.numpy as jnp
from jax import lax
from jax.sharding import PartitionSpec as P


def passed_along(value, axis, steps):
    count = lax.axis_size(axis)
    first, last = (max(0, -steps), min(count, count - steps))
    return lax.ppermute(value, axis, [(source, source + steps) for source in range(first, last)])


def body(source, w_enc, b_enc, threshold, dec_self, dec_next, target):
    rows = source[0]
    scale = lax.rsqrt(jnp.mean(rows * rows, axis=1, keepdims=True) + 1e-05)
    normed = (rows * scale).astype(jnp.bfloat16)
    encoder = w_enc[0]
    bias = b_enc[0]
    limits = threshold[0]
    own_dec = dec_self[0]
    after_dec = dec_next[0]
    pre = (
        jnp.dot(
            lax.all_gather(normed, "feat", axis=0, tiled=True),
            encoder,
            preferred_element_type=jnp.float32,
        )
        + bias
    )
    codes = (pre * jax.nn.sigmoid((pre - limits) / 0.1)).astype(jnp.bfloat16)
    whole_next = jnp.dot(codes, after_dec, preferred_element_type=jnp.float32)
    arrived = passed_along(whole_next, "layer", 1)
    recon = lax.psum_scatter(
        jnp.dot(codes, own_dec, preferred_element_type=jnp.float32) + arrived,
        "feat",
        scatter_dimension=0,
        tiled=True,
    )
    return (recon - target[0])[None]


def solution(mesh):
    return jax.shard_map(
        body,
        mesh=mesh,
        in_specs=(
            P("layer", "feat", None),
            P("layer", None, "feat"),
            P("layer", "feat"),
            P("layer", "feat"),
            P("layer", "feat", None),
            P("layer", "feat", None),
            P("layer", "feat", None),
        ),
        out_specs=P("layer", "feat", None),
        check_vma=False,
    )
```

profile of v0, /device:TPU:0, one launch (start us, length us, event | category | flops | bytes accessed | tf_op | source)
XLA Modules:
  0.0 179.7 jit_solution(11442511106023310841)
XLA Ops:
  6.5 0.0 all-reduce.3.cloned.1.call-start
  6.5 0.9 fusion.15
  7.4 0.8 fusion.17
  8.3 43.8 %all-gather = bf16[16,4,2048]{2,1,0:T(4,128)(2,1)S(1)} all-gather(bf16[1,4,2048]{2,1,0:T(4,128)(2,1)S(1)} %fusion.17), channel_id=1, replica_groups=mesh['layer'=2,'feat'=16] {'feat'}, dimensions={0}, use_global_device_ids=true | all-gather | bytes 278528 | tf_op jit(solution)/shard_map/all_gather | solution.py:24
  52.0 0.0 slice-start
  52.0 0.1 reshape.9
  52.1 0.9 reduce
  53.0 0.7 reduce.1
  53.7 0.0 slice-start.1
  53.7 4.2 %multiply_convert_fusion = bf16[64,1536]{1,0:T(8,128)(2,1)S(1)} fusion(bf16[64,2048]{1,0:T(8,128)(2,1)S(1)} %reshape.9, bf16[1,2048,1536]{2,1,0:T(8,128)(2,1)} %param.8, f32[1536]{0:T(1024)S(1)} %reduce.1, f32[1536]{0:T(1024)S(1)} %reduce), kind=kOutput, calls=%fused_computation.8 | convolution fusion | flops 403439616 | bytes 6762496 | tf_op jit(solution)/shard_map/dot_general | solution.py:23
  57.9 0.0 copy-start.1
  57.9 0.0 copy-start
  57.9 4.0 %fusion = f32[64,2048]{1,0:T(8,128)S(1)} fusion(bf16[64,1536]{1,0:T(8,128)(2,1)S(1)} %multiply_convert_fusion, bf16[1,1536,2048]{2,1,0:T(8,128)(2,1)} %param.12), kind=kOutput, calls=%fused_computation | convolution fusion | flops 402653184 | bytes 7012352 | tf_op jit(solution)/shard_map/dot_general | solution.py:31
  61.9 1.3 collective-permute-start
  63.3 1.5 collective-permute-done
  64.8 0.0 slice-done
  64.8 0.0 slice-done.1
  64.8 2.1 %fusion.9 = f32[64,2048]{1,0:T(8,128)} fusion(f32[64,2048]{1,0:T(8,128)S(1)} %collective-permute-done, bf16[64,1536]{1,0:T(8,128)(2,1)S(1)} %multiply_convert_fusion, bf16[1,1536,2048]{2,1,0:T(8,128)(2,1)S(1)} %bitcast.35), kind=kOutput, calls=%fused_computation.7 | convolution fusion | flops 402784256 | bytes 7536640 | tf_op jit(solution)/shard_map/dot_general | solution.py:34
  66.8 0.0 all-reduce.3.cloned.1.call-update
  66.9 0.0 copy-done.1
  66.9 0.6 dynamic-slice
  68.1 103.3 %all-reduce.3.cloned.1.call-done = f32[64,2048]{1,0:T(8,128)} async-done(((f32[64,2048]{1,0:T(8,128)}), f32[64,2048]{1,0:T(8,128)}) %all-reduce.3.cloned.1.call-update) | async-done | bytes 524304
  171.4 0.0 copy-done
  171.4 1.5 fusion.14
  (2 shorter events, 0.0 us)
Async XLA Ops:
  6.5 164.9 %all-reduce.3.cloned.1.call-start = ((), (), s32[]{:S(2)}) async-start(), calls=%async_computation | async-start | bytes 1048576
  52.0 12.7 %slice-start = ((s8[6291456]{0:T(1024)(128)(4,1)}), s8[2097152]{0:T(1024)(128)(4,1)S(1)}, s32[]{:S(2)}) async-start(s8[6291456]{0:T(1024)(128)(4,1)} %bitcast.34), calls=%async_computation.1 | async-start | bytes 4194304
  53.7 11.1 %slice-start.1 = ((s8[6291456]{0:T(1024)(128)(4,1)}), s8[4194304]{0:T(1024)(128)(4,1)S(1)}, s32[]{:S(2)}) async-start(s8[6291456]{0:T(1024)(128)(4,1)} %bitcast.34), calls=%async_computation.2 | async-start | bytes 8388608
  57.9 9.0 %copy-start.1 = (u32[32]{0:T(128)S(1)}, u32[32]{0:T(128)}, u32[]{:S(2)}) copy-start(u32[32]{0:T(128)} %constant.21) | copy-start | bytes 388
  57.9 113.6 %copy-start = (f32[1,4,2048]{2,1,0:T(4,128)S(1)}, f32[1,4,2048]{2,1,0:T(4,128)}, u32[]{:S(2)}) copy-start(f32[1,4,2048]{2,1,0:T(4,128)} %param.13) | copy-start | bytes 98308
  61.9 2.8 %collective-permute-start = (f32[64,2048]{1,0:T(8,128)S(1)}, f32[64,2048]{1,0:T(8,128)S(1)}, u32[]{:S(2)}, u32[]{:S(2)}) collective-permute-start(f32[64,2048]{1,0:T(8,128)S(1)} %fusion), channel_id=1, source_target_pairs={{0,16},{1,17},{2,18},{3,19},{4,20},{5,21},{6,22},{7,23},{8,24},{9,... | collective-permute-start | bytes 1572872 | tf_op jit(solution)/shard_map/ppermute | solution.py:10
Sparse Core Ops, SparseCore 0:
  67.0 104.4 all-reduce.2
where the time goes:
time: 180 us
  waiting for transfers between devices  105 us (58%)
  blocking collectives  43.8 us (24%)
  between operations  14.1 us (8%)
  matrix products  10.3 us (6%)
  other arithmetic  4.76 us (3%)
    unnamed x2, waiting for transfers between devices  103 us
    all_gather x1, blocking collectives, body(): lax.all_gather(normed, 'feat', axis=0, tiled=True)  43.8 us
    dot_general x1, matrix products, body(): jnp.dot(lax.all_gather(normed, 'feat', axis=0, tiled=True), encoder, pref...  4.18 us
    dot_general x1, matrix products, body(): whole_next = jnp.dot(codes, after_dec, preferred_element_type=jnp.float32)  4.04 us
  transfers between devices with their start and end apart: 2, of which 2 were waited for; matrix products, arithmetic and copies ran while one was open for 0% of the time, Pallas kernels for 0%

commit v1 on v0

v1 whole, which is shorter than its diff:
```python
import jax
import jax.numpy as jnp
from jax import lax
from jax.sharding import PartitionSpec as P


def body(source, w_enc, b_enc, threshold, dec_self, dec_next, target):
    feats = lax.axis_size("feat")
    layers = lax.axis_size("layer")
    rows = source[0]
    block, depth = rows.shape
    scale = lax.rsqrt(jnp.mean(rows * rows, axis=1, keepdims=True) + 1e-05)
    normed = (rows * scale).astype(jnp.bfloat16)
    spread = jnp.broadcast_to(normed[None], (feats, block, depth))
    gathered = lax.all_to_all(spread, "feat", 0, 0).reshape(feats * block, depth)
    pre = jnp.dot(gathered, w_enc[0], preferred_element_type=jnp.float32) + b_enc[0]
    codes = (pre * jax.nn.sigmoid((pre - threshold[0]) / 0.1)).astype(jnp.bfloat16)
    whole_next = jnp.dot(codes, dec_next[0], preferred_element_type=jnp.float32)
    ring = [(i, (i + 1) % layers) for i in range(layers)]
    arrived = lax.ppermute(whole_next.astype(jnp.bfloat16), "layer", ring)
    arrived = jnp.where(lax.axis_index("layer") > 0, arrived, jnp.zeros_like(arrived))
    own = jnp.dot(codes, dec_self[0], preferred_element_type=jnp.float32)
    part = (own + arrived.astype(jnp.float32)).astype(jnp.bfloat16)
    shares = lax.all_to_all(part.reshape(feats, block, depth), "feat", 0, 0)
    recon = jnp.sum(shares.astype(jnp.float32), axis=0)
    return (recon - target[0])[None]


def solution(mesh):
    return jax.shard_map(
        body,
        mesh=mesh,
        in_specs=(
            P("layer", "feat", None),
            P("layer", None, "feat"),
            P("layer", "feat"),
            P("layer", "feat"),
            P("layer", "feat", None),
            P("layer", "feat", None),
            P("layer", "feat", None),
        ),
        out_specs=P("layer", "feat", None),
        check_vma=False,
    )
```

time: 180 us -> 47.1 us (0.26)
  waiting for transfers between devices: 105 us -> 9.95 us
  blocking collectives: 43.8 us -> 13.5 us
  between operations: 14.1 us -> 0.08 us
  starting transfers between devices: 1.32 us -> 8.38 us
    unnamed x2 -> x0, waiting for transfers between devices: 103 us -> none
    all_gather x1 -> x0, blocking collectives: 43.8 us -> none  [body(): lax.all_gather(normed, 'feat', axis=0, tiled=True)]
    all_to_all x0 -> x1, blocking collectives: none -> 13.5 us  [body(): shares = lax.all_to_all(part.reshape(feats, block, depth), 'feat', 0, 0)]
    all_to_all x0 -> x1, waiting for transfers between devices: none -> 8.43 us  [body(): lax.all_to_all(spread, 'feat', 0, 0).reshape(feats * block, depth)]
    all_to_all x0 -> x1, starting transfers between devices: none -> 8.31 us  [body(): lax.all_to_all(spread, 'feat', 0, 0).reshape(feats * block, depth)]
  transfers between devices with their start and end apart: 2 -> 2, of which waited for: 2 -> 2; matrix products, arithmetic and copies ran while one was open for 0% -> 3% of each run, Pallas kernels for 0% -> 0%
where the time goes in v1:
time: 47.1 us; the launch traced here: 46.6 us
  blocking collectives  13.5 us (29%)
  waiting for transfers between devices  9.95 us (21%)
  matrix products  9.41 us (20%)
  starting transfers between devices  8.38 us (18%)
  other arithmetic  3.91 us (8%)
  local copies, waits for them, and re-layouts  1.38 us (3%)
    all_to_all x1, blocking collectives, body(): shares = lax.all_to_all(part.reshape(feats, block, depth), 'feat', 0, 0)  13.5 us
    all_to_all x1, waiting for transfers between devices, body(): lax.all_to_all(spread, 'feat', 0, 0).reshape(feats * block, depth)  8.43 us
    all_to_all x1, starting transfers between devices, body(): lax.all_to_all(spread, 'feat', 0, 0).reshape(feats * block, depth)  8.31 us
    dot_general x1, matrix products, body(): jnp.dot(gathered, w_enc[0], preferred_element_type=jnp.float32) + b_enc[0]  4.17 us
    dot_general x1, matrix products, body(): own = jnp.dot(codes, dec_self[0], preferred_element_type=jnp.float32)  3.99 us
    ppermute x1, waiting for transfers between devices, body(): arrived = lax.ppermute(whole_next.astype(jnp.bfloat16), 'layer', ring)  1.52 us
    unnamed x2, other arithmetic  1.43 us
    dot_general x1, matrix products, body(): whole_next = jnp.dot(codes, dec_next[0], preferred_element_type=jnp.float32)  1.24 us
  transfers between devices with their start and end apart: 2, of which 2 were waited for; matrix products, arithmetic and copies ran while one was open for 3% of the time, Pallas kernels for 0%

profile of v1, /device:TPU:0, one launch (start us, length us, event | category | flops | bytes accessed | tf_op | source)
XLA Modules:
  0.0 46.6 jit_solution(18160875215459267481)
XLA Ops:
  0.0 0.9 %multiply_reduce_fusion = f32[4]{0:T(128)S(1)} fusion(f32[1,4,2048]{2,1,0:T(4,128)} %param.7), kind=kLoop, calls=%fused_computation.13 | loop fusion | flops 16380 | bytes 32784 | tf_op jit(solution)/shard_map/reduce_sum | solution.py:12
  0.9 0.8 %fusion.14 = bf16[4,2048]{1,0:T(4,128)(2,1)S(1)} fusion(f32[1,4,2048]{2,1,0:T(4,128)} %param.7, f32[4]{0:T(128)S(1)} %add_rsqrt_fusion), kind=kLoop, calls=%fused_computation.14 | loop fusion | flops 16384 | bytes 49168 | tf_op jit(solution)/shard_map/broadcast_in_dim | solution.py:14
  1.7 0.8 %broadcast_in_dim.14 = bf16[16,4,2048]{2,1,0:T(4,128)(2,1)} broadcast(bf16[4,2048]{1,0:T(4,128)(2,1)S(1)} %fusion.14), dimensions={1,2} | broadcast | bytes 278528 | tf_op jit(solution)/shard_map/broadcast_in_dim | solution.py:14
  2.5 8.3 %all-to-all-start = ((bf16[16,4,2048]{2,1,0:T(4,128)(2,1)}), bf16[16,4,2048]{2,1,0:T(4,128)(2,1)S(1)}, u32[]{:S(2)}, u32[]{:S(2)}) async-start(bf16[16,4,2048]{2,1,0:T(4,128)(2,1)} %broadcast_in_dim.14), calls=%async_computation | async-start | bytes 524288 | tf_op jit(solution)/shard_map/all_to_all | solution.py:15
  10.9 0.7 %reduce.1 = f32[1536]{0:T(1024)S(1)} reduce(f32[1,1536]{1,0:T(1,128)} %param.9, f32[]{:T(128)} %constant.29), dimensions={0}, to_apply=%param.9.reduce_sub_computation | reduce | bytes 12292 | tf_op args[2]
  11.6 0.7 %reduce.2 = f32[1536]{0:T(1024)S(1)} reduce(f32[1,1536]{1,0:T(1,128)} %param.10, f32[]{:T(128)} %constant.29), dimensions={0}, to_apply=%param.10.reduce_sub_computation | reduce | bytes 12292 | tf_op args[3]
  12.3 8.4 %all-to-all-done = bf16[16,4,2048]{2,1,0:T(4,128)(2,1)S(1)} async-done(((bf16[16,4,2048]{2,1,0:T(4,128)(2,1)}), bf16[16,4,2048]{2,1,0:T(4,128)(2,1)S(1)}, u32[]{:S(2)}, u32[]{:S(2)}) %all-to-all-start) | async-done | bytes 262176 | tf_op jit(solution)/shard_map/all_to_all | solution.py:15
  20.7 0.1 reshape.23
  20.8 0.0 copy-start
  20.8 4.2 %multiply_convert_fusion = bf16[64,1536]{1,0:T(8,128)(2,1)S(1)} fusion(bf16[64,2048]{1,0:T(8,128)(2,1)S(1)} %reshape.23, bf16[1,2048,1536]{2,1,0:T(8,128)(2,1)} %param.8, f32[1536]{0:T(1024)S(1)} %reduce.2, f32[1536]{0:T(1024)S(1)} %reduce.1), kind=kOutput, calls=%fused_computation.10 | convolution fusion | flops 403439616 | bytes 6762496 | tf_op jit(solution)/shard_map/dot_general | solution.py:16
  25.0 0.4 copy-done
  25.4 0.0 copy-start.1
  25.4 1.2 %fusion.9 = bf16[64,2048]{1,0:T(8,128)(2,1)S(1)} fusion(bf16[64,1536]{1,0:T(8,128)(2,1)S(1)} %multiply_convert_fusion, bf16[1,1536,2048]{2,1,0:T(8,128)(2,1)S(1)} %copy-done), kind=kOutput, calls=%fused_computation.7 | convolution fusion | flops 402784256 | bytes 6750208 | tf_op jit(solution)/shard_map/dot_general | solution.py:18
  26.6 0.1 collective-permute-start
  26.7 1.5 %collective-permute-done = bf16[64,2048]{1,0:T(8,128)(2,1)S(1)} collective-permute-done((bf16[64,2048]{1,0:T(8,128)(2,1)S(1)}, bf16[64,2048]{1,0:T(8,128)(2,1)S(1)}, u32[]{:S(2)}, u32[]{:S(2)}) %collective-permute-start) | collective-permute-done | bytes 262176 | tf_op jit(solution)/shard_map/ppermute | solution.py:20
  28.2 4.0 %add_convert_fusion = bf16[64,2048]{1,0:T(8,128)(2,1)S(1)} fusion(bf16[64,2048]{1,0:T(8,128)(2,1)S(1)} %collective-permute-done, pred[]{:T(512)S(6)} %gt.3, bf16[64,1536]{1,0:T(8,128)(2,1)S(1)} %multiply_convert_fusion, bf16[1,1536,2048]{2,1,0:T(8,128)(2,1)} %param.11), kind=kOutput, calls=%fused_computation.9 | convolution fusion | flops 403177472 | bytes 7012353 | tf_op jit(solution)/shard_map/dot_general | solution.py:22
  32.2 0.1 reshape.24
  32.4 13.5 %all_to_all.10 = bf16[16,4,2048]{2,1,0:T(4,128)(2,1)S(1)} all-to-all(bf16[16,4,2048]{2,1,0:T(4,128)(2,1)S(1)} %reshape.24), channel_id=1, replica_groups=mesh['layer'=2,'feat'=16] {'feat'}, dimensions={0} | all-to-all | bytes 524288 | tf_op jit(solution)/shard_map/all_to_all | solution.py:24
  45.9 0.1 convert_reduce_fusion
  46.0 0.0 copy-done.1
  46.0 0.6 %bitcast_subtract_fusion = f32[1,4,2048]{2,1,0:T(4,128)} fusion(f32[1,4,2048]{2,1,0:T(4,128)S(1)} %copy-done.1, f32[4,2048]{1,0:T(4,128)S(1)} %convert_reduce_fusion), kind=kLoop, calls=%fused_computation.11 | loop fusion | flops 8192 | bytes 98304 | tf_op jit(solution)/shard_map/sub | solution.py:26
  (1 shorter events, 0.0 us)
Async XLA Ops:
  2.5 18.2 %all-to-all-start = ((bf16[16,4,2048]{2,1,0:T(4,128)(2,1)}), bf16[16,4,2048]{2,1,0:T(4,128)(2,1)S(1)}, u32[]{:S(2)}, u32[]{:S(2)}) async-start(bf16[16,4,2048]{2,1,0:T(4,128)(2,1)} %broadcast_in_dim.14), calls=%async_computation | async-start | bytes 524288 | tf_op jit(solution)/shard_map/all_to_all | solution.py:15
  20.8 4.6 %copy-start = (bf16[1,1536,2048]{2,1,0:T(8,128)(2,1)S(1)}, bf16[1,1536,2048]{2,1,0:T(8,128)(2,1)}, u32[]{:S(2)}) copy-start(bf16[1,1536,2048]{2,1,0:T(8,128)(2,1)} %param.12) | copy-start | bytes 18874372
  25.4 20.6 %copy-start.1 = (f32[1,4,2048]{2,1,0:T(4,128)S(1)}, f32[1,4,2048]{2,1,0:T(4,128)}, u32[]{:S(2)}) copy-start(f32[1,4,2048]{2,1,0:T(4,128)} %param.13) | copy-start | bytes 98308
  26.6 1.6 %collective-permute-start = (bf16[64,2048]{1,0:T(8,128)(2,1)S(1)}, bf16[64,2048]{1,0:T(8,128)(2,1)S(1)}, u32[]{:S(2)}, u32[]{:S(2)}) collective-permute-start(bf16[64,2048]{1,0:T(8,128)(2,1)S(1)} %fusion.9), channel_id=1, source_target_pairs={{0,16},{16,0},{1,17},{17,1},{2,18},{18,2},{3,19},{19,3},{4,20},{20... | collective-permute-start | bytes 786440 | tf_op jit(solution)/shard_map/ppermute | solution.py:20

commit v2 on v1

v2 whole, which is shorter than its diff:
```python
import jax
import jax.numpy as jnp
from jax import lax
from jax.experimental import pallas as pl
from jax.experimental.pallas import tpu as pltpu
from jax.sharding import PartitionSpec as P

VMEM = pl.BlockSpec(memory_space=pltpu.VMEM)
GRANT = 8 * 2**20


def call(kernel, out_shape, args, flops=0, moved=2**18):
    return pl.pallas_call(
        kernel,
        out_shape=out_shape,
        in_specs=[VMEM] * len(args),
        out_specs=jax.tree.map(lambda _: VMEM, out_shape),
        compiler_params=pltpu.CompilerParams(vmem_limit_bytes=GRANT),
        cost_estimate=pl.CostEstimate(flops=flops, bytes_accessed=moved, transcendentals=0),
    )(*args)


def spread_kernel(rows_ref, out_ref):
    rows = rows_ref[0]
    scale = lax.rsqrt(jnp.mean(rows * rows, axis=1, keepdims=True) + 1e-05)
    normed = (rows * scale).astype(jnp.bfloat16)
    out_ref[...] = jnp.broadcast_to(normed[None], out_ref.shape)


def encode_kernel(rows_ref, enc_ref, bias_ref, limit_ref, after_ref, codes_ref, carried_ref):
    rows = rows_ref[...].reshape(-1, rows_ref.shape[-1])
    pre = jnp.dot(rows, enc_ref[0], preferred_element_type=jnp.float32) + bias_ref[...]
    codes = (pre * jax.nn.sigmoid((pre - limit_ref[...]) / 0.1)).astype(jnp.bfloat16)
    codes_ref[...] = codes
    last = lax.axis_index("layer") == lax.axis_size("layer") - 1

    @pl.when(last)
    def _():
        carried_ref[...] = jnp.zeros_like(carried_ref)

    @pl.when(jnp.logical_not(last))
    def _():
        carried = jnp.dot(codes, after_ref[0], preferred_element_type=jnp.float32)
        carried_ref[...] = carried.astype(jnp.bfloat16)


def decode_kernel(codes_ref, dec_ref, own_ref):
    own_ref[...] = jnp.dot(codes_ref[...], dec_ref[0], preferred_element_type=jnp.float32)


def join_kernel(own_ref, arrived_ref, part_ref):
    part = own_ref[...] + arrived_ref[...].astype(jnp.float32)
    part_ref[...] = part.astype(jnp.bfloat16).reshape(part_ref.shape)


def finish_kernel(shares_ref, target_ref, out_ref):
    out_ref[0] = jnp.sum(shares_ref[...].astype(jnp.float32), axis=0) - target_ref[0]


def body(source, w_enc, b_enc, threshold, dec_self, dec_next, target):
    feats = lax.axis_size("feat")
    layers = lax.axis_size("layer")
    _, block, depth = source.shape
    width = w_enc.shape[2]
    rows = feats * block
    work = 2 * rows * depth * width
    half, full = jnp.bfloat16, jnp.float32
    shape = jax.ShapeDtypeStruct
    spread = call(spread_kernel, shape((feats, block, depth), half), (source,), 2**36, 2**27)
    gathered = lax.all_to_all(spread, "feat", 0, 0)
    codes, carried = call(
        encode_kernel,
        (shape((rows, width), half), shape((rows, depth), half)),
        (gathered, w_enc, b_enc, threshold, dec_next),
        2 * work,
    )
    arrived = lax.ppermute(carried, "layer", [(i, (i + 1) % layers) for i in range(layers)])
    own = call(decode_kernel, shape((rows, depth), full), (codes, dec_self), work)
    part = call(join_kernel, shape((feats, block, depth), half), (own, arrived))
    shares = lax.all_to_all(part, "feat", 0, 0)
    return call(finish_kernel, shape(target.shape, full), (shares, target))


def solution(mesh):
    return jax.shard_map(
        body,
        mesh=mesh,
        in_specs=(
            P("layer", "feat", None),
            P("layer", None, "feat"),
            P("layer", "feat"),
            P("layer", "feat"),
            P("layer", "feat", None),
            P("layer", "feat", None),
            P("layer", "feat", None),
        ),
        out_specs=P("layer", "feat", None),
        check_vma=False,
    )
```

time: 47.1 us -> 38 us (0.81)
  blocking collectives: 13.5 us -> 31.8 us
  waiting for transfers between devices: 9.95 us -> 0.07 us
  matrix products: 9.41 us -> 0 us
  starting transfers between devices: 8.38 us -> 0.07 us
  Pallas kernels: 0 us -> 4.53 us
  other arithmetic: 3.91 us -> 0 us
    all_to_all x1 -> x2, blocking collectives: 13.5 us -> 31.8 us  [the longest x1 18.3 us: body(): gathered = lax.all_to_all(spread, 'feat', 0, 0)]
    dot_general x3 -> x0, matrix products: 9.41 us -> none  [the longest x1 4.17 us: body(): jnp.dot(gathered, w_enc[0], preferred_element_type=jnp.float32) + b_enc[0]]
    all_to_all x1 -> x0, waiting for transfers between devices: 8.43 us -> none  [body(): lax.all_to_all(spread, 'feat', 0, 0).reshape(feats * block, depth)]
    all_to_all x1 -> x0, starting transfers between devices: 8.31 us -> none  [body(): lax.all_to_all(spread, 'feat', 0, 0).reshape(feats * block, depth)]
    pallas_call x0 -> x5, Pallas kernels: none -> 4.53 us  [call(): pl.pallas_call(kernel, out_shape=out_shape, in_specs=[VMEM] * len(args),...]
    ppermute x1, waiting for transfers between devices: 1.52 us -> 0.07 us  [body(): lax.ppermute(carried, 'layer', [(i, (i + 1) % layers) for i in range(laye...]
    unnamed x2 -> x0, other arithmetic: 1.43 us -> none
    reduce_sum x2 -> x0, other arithmetic: 1.01 us -> none  [the longest x1 0.89 us: body(): scale = lax.rsqrt(jnp.mean(rows * rows, axis=1, keepdims=True) + 1e-05)]
  transfers between devices with their start and end apart: 2 -> 1, of which waited for: 2 -> 1; matrix products, arithmetic and copies ran while one was open for 3% -> 0% of each run, Pallas kernels for 0% -> 3%
where the time goes in v2:
time: 38 us; the launch traced here: 37.8 us
  blocking collectives  31.8 us (84%)
  Pallas kernels  4.53 us (12%)
  local copies, waits for them, and re-layouts  1.18 us (3%)
    all_to_all x1, blocking collectives, body(): gathered = lax.all_to_all(spread, 'feat', 0, 0)  18.3 us
    all_to_all x1, blocking collectives, body(): shares = lax.all_to_all(part, 'feat', 0, 0)  13.6 us
    pallas_call x5, Pallas kernels, call(): pl.pallas_call(kernel, out_shape=out_shape, in_specs=[VMEM] * len(args),...  4.53 us
    unnamed x14, local copies, waits for them, and re-layouts  1.18 us
  transfers between devices with their start and end apart: 1, of which 1 were waited for; matrix products, arithmetic and copies ran while one was open for 0% of the time, Pallas kernels for 3%

profile of v2, /device:TPU:0, one launch (start us, length us, event | category | flops | bytes accessed | tf_op | source)
XLA Modules:
  0.0 37.8 jit_solution(5455686406651617945)
XLA Ops:
  0.0 0.0 copy-start.1
  0.0 0.0 copy-start.5
  0.0 0.0 copy-start.4
  0.0 0.0 copy-start
  0.0 0.0 copy-start.6
  0.0 0.9 %copy-done.6 = f32[1,4,2048]{2,1,0:T(4,128)S(1)} copy-done((f32[1,4,2048]{2,1,0:T(4,128)S(1)}, f32[1,4,2048]{2,1,0:T(4,128)}, u32[]{:S(2)}) %copy-start.6) | copy-done | bytes 32792
  0.9 0.1 shard_map.73
  1.0 18.3 %all_to_all.10.rows_ref = bf16[16,4,2048]{2,1,0:T(4,128)(2,1)S(1)} all-to-all(bf16[16,4,2048]{2,1,0:T(4,128)(2,1)S(1)} %shard_map.73), channel_id=1, replica_groups=mesh['layer'=2,'feat'=16] {'feat'}, dimensions={0} | all-to-all | bytes 524288 | tf_op jit(solution)/shard_map/all_to_all | solution.py:70
  19.3 0.0 copy-done.1
  19.3 0.0 copy-done.5
  19.3 0.0 copy-done.4
  19.3 0.0 copy-done
  19.3 0.0 copy-start.2
  19.3 2.4 %shard_map.74 = (bf16[64,1536]{1,0:T(8,128)(2,1)S(1)}, bf16[64,2048]{1,0:T(8,128)(2,1)S(1)}) custom-call(bf16[16,4,2048]{2,1,0:T(4,128)(2,1)S(1)} %all_to_all.10.rows_ref, bf16[1,2048,1536]{2,1,0:T(8,128)(2,1)S(1)} %copy-done, f32[1,1536]{1,0:T(1,128)S(1)} %copy-done.4, f32[1,1536]{1,0:T(1,128)S(1)} %copy-done.5, bf16[1,1536,2048]{2,1,0:T(8,128)(2,1)S(1)} %copy-done.1), custom_call_target="tpu_custom_call" | custom-call | flops 805306368 | bytes 262144 | tf_op jit(solution)/shard_map/pallas_call | solution.py:13
  21.8 0.0 copy-start.3
  21.8 0.1 collective-permute-start
  21.9 0.3 copy-done.2
  22.1 1.2 %shard_map.75.own_ref = f32[64,2048]{1,0:T(8,128)S(1)} custom-call(bf16[64,1536]{1,0:T(8,128)(2,1)S(1)} %get-tuple-element.7.codes_ref, bf16[1,1536,2048]{2,1,0:T(8,128)(2,1)S(1)} %copy-done.2), custom_call_target="tpu_custom_call" | custom-call | flops 402653184 | bytes 262144 | tf_op jit(solution)/shard_map/pallas_call | solution.py:13
  23.3 0.1 collective-permute-done.arrived_ref
  23.4 0.1 shard_map.76
  23.4 13.6 %all_to_all.11.shares_ref = bf16[16,4,2048]{2,1,0:T(4,128)(2,1)S(1)} all-to-all(bf16[16,4,2048]{2,1,0:T(4,128)(2,1)S(1)} %shard_map.76), channel_id=1, replica_groups=mesh['layer'=2,'feat'=16] {'feat'}, dimensions={0} | all-to-all | bytes 524288 | tf_op jit(solution)/shard_map/all_to_all | solution.py:80
  37.0 0.0 copy-done.3
  37.0 0.7 %shard_map.77 = f32[1,4,2048]{2,1,0:T(4,128)} custom-call(bf16[16,4,2048]{2,1,0:T(4,128)(2,1)S(1)} %all_to_all.11.shares_ref, f32[1,4,2048]{2,1,0:T(4,128)S(1)} %copy-done.3), custom_call_target="tpu_custom_call" | custom-call | bytes 262144 | tf_op jit(solution)/shard_map/pallas_call | solution.py:13
Async XLA Ops:
  0.0 19.3 %copy-start.1 = (bf16[1,1536,2048]{2,1,0:T(8,128)(2,1)S(1)}, bf16[1,1536,2048]{2,1,0:T(8,128)(2,1)}, u32[]{:S(2)}) copy-start(bf16[1,1536,2048]{2,1,0:T(8,128)(2,1)} %after_ref.1) | copy-start | bytes 18874372
  0.0 19.3 %copy-start.5 = (f32[1,1536]{1,0:T(1,128)S(1)}, f32[1,1536]{1,0:T(1,128)}, u32[]{:S(2)}) copy-start(f32[1,1536]{1,0:T(1,128)} %limit_ref.1) | copy-start | bytes 18436
  0.0 19.3 %copy-start.4 = (f32[1,1536]{1,0:T(1,128)S(1)}, f32[1,1536]{1,0:T(1,128)}, u32[]{:S(2)}) copy-start(f32[1,1536]{1,0:T(1,128)} %bias_ref.1) | copy-start | bytes 18436
  0.0 19.3 %copy-start = (bf16[1,2048,1536]{2,1,0:T(8,128)(2,1)S(1)}, bf16[1,2048,1536]{2,1,0:T(8,128)(2,1)}, u32[]{:S(2)}) copy-start(bf16[1,2048,1536]{2,1,0:T(8,128)(2,1)} %enc_ref.1) | copy-start | bytes 18874372
  0.0 0.9 %copy-start.6 = (f32[1,4,2048]{2,1,0:T(4,128)S(1)}, f32[1,4,2048]{2,1,0:T(4,128)}, u32[]{:S(2)}) copy-start(f32[1,4,2048]{2,1,0:T(4,128)} %rows_ref.1) | copy-start | bytes 98308
  19.3 2.8 %copy-start.2 = (bf16[1,1536,2048]{2,1,0:T(8,128)(2,1)S(1)}, bf16[1,1536,2048]{2,1,0:T(8,128)(2,1)}, u32[]{:S(2)}) copy-start(bf16[1,1536,2048]{2,1,0:T(8,128)(2,1)} %dec_ref.1) | copy-start | bytes 18874372
  21.8 15.3 %copy-start.3 = (f32[1,4,2048]{2,1,0:T(4,128)S(1)}, f32[1,4,2048]{2,1,0:T(4,128)}, u32[]{:S(2)}) copy-start(f32[1,4,2048]{2,1,0:T(4,128)} %target_ref.1) | copy-start | bytes 98308
  21.8 1.6 %collective-permute-start = (bf16[64,2048]{1,0:T(8,128)(2,1)S(1)}, bf16[64,2048]{1,0:T(8,128)(2,1)S(1)}, u32[]{:S(2)}, u32[]{:S(2)}) collective-permute-start(bf16[64,2048]{1,0:T(8,128)(2,1)S(1)} %get-tuple-element.8), channel_id=1, source_target_pairs={{0,16},{16,0},{1,17},{17,1},{2,18},{18,2},{3,19},{19,3},{4,20},{20... | collective-permute-start | bytes 786440 | tf_op jit(solution)/shard_map/ppermute | solution.py:77

commit v3 on v2

v3 whole, which is shorter than its diff:
```python
import jax
import jax.numpy as jnp
from jax import lax
from jax.experimental import pallas as pl
from jax.experimental.pallas import tpu as pltpu
from jax.sharding import PartitionSpec as P

VMEM = pl.BlockSpec(memory_space=pltpu.VMEM)
GRANT = 8 * 2**20
RADIX = 4


def call(kernel, out_shape, args, flops=0, moved=2**18):
    return pl.pallas_call(
        kernel,
        out_shape=out_shape,
        in_specs=[VMEM] * len(args),
        out_specs=jax.tree.map(lambda _: VMEM, out_shape),
        compiler_params=pltpu.CompilerParams(vmem_limit_bytes=GRANT),
        cost_estimate=pl.CostEstimate(flops=flops, bytes_accessed=moved, transcendentals=0),
    )(*args)


def normalise_kernel(rows_ref, out_ref):
    rows = rows_ref[0]
    scale = lax.rsqrt(jnp.mean(rows * rows, axis=1, keepdims=True) + 1e-05)
    out_ref[...] = (rows * scale).astype(jnp.bfloat16)


def stack_kernel(*refs):
    *block_refs, out_ref = refs
    whole = jnp.concatenate([ref[...].astype(jnp.float32) for ref in block_refs], axis=0)
    out_ref[...] = whole.astype(jnp.bfloat16)


def encode_kernel(*refs):
    *block_refs, enc_ref, bias_ref, limit_ref, codes_ref = refs
    rows = jnp.concatenate([ref[...] for ref in block_refs], axis=0)
    pre = jnp.dot(rows, enc_ref[0], preferred_element_type=jnp.float32) + bias_ref[...]
    codes_ref[...] = (pre * jax.nn.sigmoid((pre - limit_ref[...]) / 0.1)).astype(jnp.bfloat16)


def decode_kernel(codes_ref, dec_ref, own_ref):
    own_ref[...] = jnp.dot(codes_ref[...], dec_ref[0], preferred_element_type=jnp.float32)


def cut(total, part_refs):
    size = part_refs[0].shape[0]
    for i, part_ref in enumerate(part_refs):
        part_ref[...] = total[i * size : (i + 1) * size].astype(jnp.bfloat16)


def join_kernel(own_ref, before_ref, dec_ref, *part_refs):
    first = lax.axis_index("layer") == 0

    @pl.when(first)
    def _():
        cut(own_ref[...], part_refs)

    @pl.when(jnp.logical_not(first))
    def _():
        carried = jnp.dot(before_ref[...], dec_ref[0], preferred_element_type=jnp.float32)
        cut(own_ref[...] + carried, part_refs)


def added(block_refs):
    return sum(ref[...].astype(jnp.float32) for ref in block_refs)


def split_kernel(count, *refs):
    cut(added(refs[:count]), refs[count:])


def finish_kernel(*refs):
    *block_refs, target_ref, out_ref = refs
    out_ref[0] = added(block_refs) - target_ref[0]


def digits(count):
    assert count & (count - 1) == 0
    found, stride = [], 1
    while stride < count:
        radix = min(RADIX, count // stride)
        found.append((stride, radix))
        stride *= radix
    return found or [(1, 1)]


def body(source, w_enc, b_enc, threshold, dec_self, dec_next, target):
    feats = lax.axis_size("feat")
    layers = lax.axis_size("layer")
    _, block, depth = source.shape
    width = w_enc.shape[2]
    rows = feats * block
    work = 2 * rows * depth * width
    half, full = jnp.bfloat16, jnp.float32
    shape = jax.ShapeDtypeStruct
    steps = digits(feats)

    def swap(value, flip):
        return lax.ppermute(value, "feat", [(i, i ^ flip) for i in range(feats)])

    def onward(value):
        return lax.ppermute(value, "layer", [(i, (i + 1) % layers) for i in range(layers)])

    arrived_dec = onward(dec_next)

    line = call(normalise_kernel, shape((block, depth), half), (source,), 2**36, 2**27)
    for at, (stride, radix) in enumerate(reversed(steps)):
        blocks = [line] + [swap(line, stride * j) for j in range(1, radix)]
        if at < len(steps) - 1:
            line = call(stack_kernel, shape((radix * line.shape[0], depth), half), blocks, 2**34)

    codes = call(encode_kernel, shape((rows, width), half), (*blocks, w_enc, b_enc, threshold), work)
    before = onward(codes)
    own = call(decode_kernel, shape((rows, depth), full), (codes, dec_self), work)

    size = rows // steps[0][1]
    parts = call(join_kernel, (shape((size, depth), half),) * steps[0][1], (own, before, arrived_dec), work)
    for at, (stride, radix) in enumerate(steps):
        blocks = [parts[0]] + [swap(parts[j], stride * j) for j in reversed(range(1, radix))]
        if at < len(steps) - 1:
            following = steps[at + 1][1]
            size //= following
            kernel = lambda *refs, count=radix: split_kernel(count, *refs)
            parts = call(kernel, (shape((size, depth), half),) * following, blocks)
    return call(finish_kernel, shape(target.shape, full), (*blocks, target))


def solution(mesh):
    return jax.shard_map(
        body,
        mesh=mesh,
        in_specs=(
            P("layer", "feat", None),
            P("layer", None, "feat"),
            P("layer", "feat"),
            P("layer", "feat"),
            P("layer", "feat", None),
            P("layer", "feat", None),
            P("layer", "feat", None),
        ),
        out_specs=P("layer", "feat", None),
        check_vma=False,
    )
```

time: 38 us -> 35.3 us (0.929)
  blocking collectives: 31.8 us -> 0 us
  starting transfers between devices: 0.07 us -> 17.4 us
  waiting for transfers between devices: 0.07 us -> 13.6 us
  Pallas kernels: 4.53 us -> 3.23 us
  local copies, waits for them, and re-layouts: 1.18 us -> 0.79 us
    all_to_all x2 -> x0, blocking collectives: 31.8 us -> none  [the longest x1 18.3 us: body(): gathered = lax.all_to_all(spread, 'feat', 0, 0)]
    ppermute x1 -> x14, starting transfers between devices: 0.07 us -> 17.4 us  [the longest x12 16.9 us: swap(): return lax.ppermute(value, 'feat', [(i, i ^ flip) for i in range(feats)])]
    ppermute x1 -> x14, waiting for transfers between devices: 0.07 us -> 13.6 us  [the longest x12 13.4 us: swap(): return lax.ppermute(value, 'feat', [(i, i ^ flip) for i in range(feats)])]
    pallas_call x5 -> x7, Pallas kernels: 4.53 us -> 3.23 us  [call(): pl.pallas_call(kernel, out_shape=out_shape, in_specs=[VMEM] * len(args),...]
    unnamed x14 -> x12, local copies, waits for them, and re-layouts: 1.18 us -> 0.79 us
  transfers between devices with their start and end apart: 1 -> 14, of which waited for: 1 -> 11; matrix products, arithmetic and copies ran while one was open for 0% -> 0% of each run, Pallas kernels for 3% -> 7%
where the time goes in v3:
time: 35.3 us; the launch traced here: 35.1 us
  starting transfers between devices  17.4 us (49%)
  waiting for transfers between devices  13.6 us (39%)
  Pallas kernels  3.23 us (9%)
  local copies, waits for them, and re-layouts  0.79 us (2%)
    ppermute x12, starting transfers between devices, swap(): return lax.ppermute(value, 'feat', [(i, i ^ flip) for i in range(feats)])  16.9 us
    ppermute x12, waiting for transfers between devices, swap(): return lax.ppermute(value, 'feat', [(i, i ^ flip) for i in range(feats)])  13.4 us
    pallas_call x7, Pallas kernels, call(): pl.pallas_call(kernel, out_shape=out_shape, in_specs=[VMEM] * len(args),...  3.23 us
    unnamed x12, local copies, waits for them, and re-layouts  0.79 us
  transfers between devices with their start and end apart: 14, of which 11 were waited for; matrix products, arithmetic and copies ran while one was open for 0% of the time, Pallas kernels for 7%

profile of v3, /device:TPU:0, one launch (start us, length us, event | category | flops | bytes accessed | tf_op | source)
XLA Modules:
  0.0 35.1 jit_solution(2197049825428939417)
XLA Ops:
  0.0 0.5 %collective-permute-start.7 = (bf16[1,1536,2048]{2,1,0:T(8,128)(2,1)}, bf16[1,1536,2048]{2,1,0:T(8,128)(2,1)S(1)}, u32[]{:S(2)}, u32[]{:S(2)}) collective-permute-start(bf16[1,1536,2048]{2,1,0:T(8,128)(2,1)} %param.12), channel_id=1, source_target_pairs={{0,16},{16,0},{1,17},{17,1},{2,18},{18,2},{3,19},{19,3},{4,20},{20... | collective-permute-start | bytes 18874376 | tf_op jit(solution)/shard_map/ppermute | solution.py:104
  0.5 0.8 %copy-done.5 = f32[1,4,2048]{2,1,0:T(4,128)S(1)} copy-done((f32[1,4,2048]{2,1,0:T(4,128)S(1)}, f32[1,4,2048]{2,1,0:T(4,128)}, u32[]{:S(2)}) %copy-start.5) | copy-done | bytes 32792
  1.3 4.7 %collective-permute-start.2 = (bf16[4,2048]{1,0:T(4,128)(2,1)S(1)}, bf16[4,2048]{1,0:T(4,128)(2,1)S(1)}, u32[]{:S(2)}, u32[]{:S(2)}) collective-permute-start(bf16[4,2048]{1,0:T(4,128)(2,1)S(1)} %shard_map.73.refs_0_), channel_id=1, source_target_pairs={{0,12},{1,13},{2,14},{3,15},{4,8},{5,9},{6,10},{7,11},{8,4},{9,5},... | collective-permute-start | bytes 49160 | tf_op jit(solution)/shard_map/ppermute | solution.py:101
  6.0 0.6 %collective-permute-start = (bf16[4,2048]{1,0:T(4,128)(2,1)S(1)}, bf16[4,2048]{1,0:T(4,128)(2,1)S(1)}, u32[]{:S(2)}, u32[]{:S(2)}) collective-permute-start(bf16[4,2048]{1,0:T(4,128)(2,1)S(1)} %shard_map.73.refs_0_), channel_id=1, source_target_pairs={{0,4},{1,5},{2,6},{3,7},{4,0},{5,1},{6,2},{7,3},{8,12},{9,13},{10,... | collective-permute-start | bytes 49160 | tf_op jit(solution)/shard_map/ppermute | solution.py:101
  6.7 1.1 %collective-permute-done.2.refs_3_ = bf16[4,2048]{1,0:T(4,128)(2,1)S(1)} collective-permute-done((bf16[4,2048]{1,0:T(4,128)(2,1)S(1)}, bf16[4,2048]{1,0:T(4,128)(2,1)S(1)}, u32[]{:S(2)}, u32[]{:S(2)}) %collective-permute-start.2) | collective-permute-done | bytes 16416 | tf_op jit(solution)/shard_map/ppermute | solution.py:101
  7.7 2.9 %collective-permute-done.1.refs_2_ = bf16[4,2048]{1,0:T(4,128)(2,1)S(1)} collective-permute-done((bf16[4,2048]{1,0:T(4,128)(2,1)S(1)}, bf16[4,2048]{1,0:T(4,128)(2,1)S(1)}, u32[]{:S(2)}, u32[]{:S(2)}) %collective-permute-start.1) | collective-permute-done | bytes 16416 | tf_op jit(solution)/shard_map/ppermute | solution.py:101
  10.7 2.5 %collective-permute-start.5 = (bf16[16,2048]{1,0:T(8,128)(2,1)S(1)}, bf16[16,2048]{1,0:T(8,128)(2,1)S(1)}, u32[]{:S(2)}, u32[]{:S(2)}) collective-permute-start(bf16[16,2048]{1,0:T(8,128)(2,1)S(1)} %shard_map.74.refs_0_), channel_id=1, source_target_pairs={{0,3},{1,2},{2,1},{3,0},{4,7},{5,6},{6,5},{7,4},{8,11},{9,10},{10,... | collective-permute-start | bytes 196616 | tf_op jit(solution)/shard_map/ppermute | solution.py:101
  13.2 0.5 %collective-permute-start.4 = (bf16[16,2048]{1,0:T(8,128)(2,1)S(1)}, bf16[16,2048]{1,0:T(8,128)(2,1)S(1)}, u32[]{:S(2)}, u32[]{:S(2)}) collective-permute-start(bf16[16,2048]{1,0:T(8,128)(2,1)S(1)} %shard_map.74.refs_0_), channel_id=1, source_target_pairs={{0,2},{1,3},{2,0},{3,1},{4,6},{5,7},{6,4},{7,5},{8,10},{9,11},{10,... | collective-permute-start | bytes 196616 | tf_op jit(solution)/shard_map/ppermute | solution.py:101
  13.7 0.5 %collective-permute-start.3 = (bf16[16,2048]{1,0:T(8,128)(2,1)S(1)}, bf16[16,2048]{1,0:T(8,128)(2,1)S(1)}, u32[]{:S(2)}, u32[]{:S(2)}) collective-permute-start(bf16[16,2048]{1,0:T(8,128)(2,1)S(1)} %shard_map.74.refs_0_), channel_id=1, source_target_pairs={{0,1},{1,0},{2,3},{3,2},{4,5},{5,4},{6,7},{7,6},{8,9},{9,8},{10,11... | collective-permute-start | bytes 196616 | tf_op jit(solution)/shard_map/ppermute | solution.py:101
  14.2 1.9 %collective-permute-done.5.refs_3_ = bf16[16,2048]{1,0:T(8,128)(2,1)S(1)} collective-permute-done((bf16[16,2048]{1,0:T(8,128)(2,1)S(1)}, bf16[16,2048]{1,0:T(8,128)(2,1)S(1)}, u32[]{:S(2)}, u32[]{:S(2)}) %collective-permute-start.5) | collective-permute-done | bytes 65568 | tf_op jit(solution)/shard_map/ppermute | solution.py:101
  16.1 1.4 %collective-permute-done.4.refs_2_ = bf16[16,2048]{1,0:T(8,128)(2,1)S(1)} collective-permute-done((bf16[16,2048]{1,0:T(8,128)(2,1)S(1)}, bf16[16,2048]{1,0:T(8,128)(2,1)S(1)}, u32[]{:S(2)}, u32[]{:S(2)}) %collective-permute-start.4) | collective-permute-done | bytes 65568 | tf_op jit(solution)/shard_map/ppermute | solution.py:101
  17.5 0.5 %collective-permute-done.3.refs_1_ = bf16[16,2048]{1,0:T(8,128)(2,1)S(1)} collective-permute-done((bf16[16,2048]{1,0:T(8,128)(2,1)S(1)}, bf16[16,2048]{1,0:T(8,128)(2,1)S(1)}, u32[]{:S(2)}, u32[]{:S(2)}) %collective-permute-start.3) | collective-permute-done | bytes 65568 | tf_op jit(solution)/shard_map/ppermute | solution.py:101
  18.0 1.2 %shard_map.75.codes_ref = bf16[64,1536]{1,0:T(8,128)(2,1)S(1)} custom-call(bf16[16,2048]{1,0:T(8,128)(2,1)S(1)} %shard_map.74.refs_0_, bf16[16,2048]{1,0:T(8,128)(2,1)S(1)} %collective-permute-done.3.refs_1_, bf16[16,2048]{1,0:T(8,128)(2,1)S(1)} %collective-permute-done.4.refs_2_, bf16[16,2048]{1,0:T(8,128)(2,1)S(1)} %collective-permute-done.5.refs_3_, ...), custom_call_target="tpu_custom_call" | custom-call | flops 402653184 | bytes 262144 | tf_op jit(solution)/shard_map/pallas_call | solution.py:14
  19.3 1.2 %shard_map.76.own_ref = f32[64,2048]{1,0:T(8,128)S(1)} custom-call(bf16[64,1536]{1,0:T(8,128)(2,1)S(1)} %shard_map.75.codes_ref, bf16[1,1536,2048]{2,1,0:T(8,128)(2,1)S(1)} %copy-done.1), custom_call_target="tpu_custom_call" | custom-call | flops 402653184 | bytes 262144 | tf_op jit(solution)/shard_map/pallas_call | solution.py:14
  20.8 1.6 %collective-permute-start.8 = (bf16[16,2048]{1,0:T(8,128)(2,1)S(1)}, bf16[16,2048]{1,0:T(8,128)(2,1)S(1)}, u32[]{:S(2)}, u32[]{:S(2)}) collective-permute-start(bf16[16,2048]{1,0:T(8,128)(2,1)S(1)} %get-tuple-element.14), channel_id=1, source_target_pairs={{0,3},{1,2},{2,1},{3,0},{4,7},{5,6},{6,5},{7,4},{8,11},{9,10},{10,... | collective-permute-start | bytes 196616 | tf_op jit(solution)/shard_map/ppermute | solution.py:101
  22.3 0.5 %collective-permute-start.9 = (bf16[16,2048]{1,0:T(8,128)(2,1)S(1)}, bf16[16,2048]{1,0:T(8,128)(2,1)S(1)}, u32[]{:S(2)}, u32[]{:S(2)}) collective-permute-start(bf16[16,2048]{1,0:T(8,128)(2,1)S(1)} %get-tuple-element.15), channel_id=1, source_target_pairs={{0,2},{1,3},{2,0},{3,1},{4,6},{5,7},{6,4},{7,5},{8,10},{9,11},{10,... | collective-permute-start | bytes 196616 | tf_op jit(solution)/shard_map/ppermute | solution.py:101
  22.8 1.5 %collective-permute-start.10 = (bf16[16,2048]{1,0:T(8,128)(2,1)S(1)}, bf16[16,2048]{1,0:T(8,128)(2,1)S(1)}, u32[]{:S(2)}, u32[]{:S(2)}) collective-permute-start(bf16[16,2048]{1,0:T(8,128)(2,1)S(1)} %get-tuple-element.16), channel_id=1, source_target_pairs={{0,1},{1,0},{2,3},{3,2},{4,5},{5,4},{6,7},{7,6},{8,9},{9,8},{10,11... | collective-permute-start | bytes 196616 | tf_op jit(solution)/shard_map/ppermute | solution.py:101
  24.3 2.0 %collective-permute-done.8.refs_1_ = bf16[16,2048]{1,0:T(8,128)(2,1)S(1)} collective-permute-done((bf16[16,2048]{1,0:T(8,128)(2,1)S(1)}, bf16[16,2048]{1,0:T(8,128)(2,1)S(1)}, u32[]{:S(2)}, u32[]{:S(2)}) %collective-permute-start.8) | collective-permute-done | bytes 65568 | tf_op jit(solution)/shard_map/ppermute | solution.py:101
  26.3 1.8 %collective-permute-done.9.refs_2_ = bf16[16,2048]{1,0:T(8,128)(2,1)S(1)} collective-permute-done((bf16[16,2048]{1,0:T(8,128)(2,1)S(1)}, bf16[16,2048]{1,0:T(8,128)(2,1)S(1)}, u32[]{:S(2)}, u32[]{:S(2)}) %collective-permute-start.9) | collective-permute-done | bytes 65568 | tf_op jit(solution)/shard_map/ppermute | solution.py:101
  28.1 1.5 %collective-permute-start.11 = (bf16[4,2048]{1,0:T(4,128)(2,1)S(1)}, bf16[4,2048]{1,0:T(4,128)(2,1)S(1)}, u32[]{:S(2)}, u32[]{:S(2)}) collective-permute-start(bf16[4,2048]{1,0:T(4,128)(2,1)S(1)} %get-tuple-element.18), channel_id=1, source_target_pairs={{0,12},{1,13},{2,14},{3,15},{4,8},{5,9},{6,10},{7,11},{8,4},{9,5},... | collective-permute-start | bytes 49160 | tf_op jit(solution)/shard_map/ppermute | solution.py:101
  29.7 0.6 %collective-permute-start.12 = (bf16[4,2048]{1,0:T(4,128)(2,1)S(1)}, bf16[4,2048]{1,0:T(4,128)(2,1)S(1)}, u32[]{:S(2)}, u32[]{:S(2)}) collective-permute-start(bf16[4,2048]{1,0:T(4,128)(2,1)S(1)} %get-tuple-element.19), channel_id=1, source_target_pairs={{0,8},{1,9},{2,10},{3,11},{4,12},{5,13},{6,14},{7,15},{8,0},{9,1},... | collective-permute-start | bytes 49160 | tf_op jit(solution)/shard_map/ppermute | solution.py:101
  30.3 2.3 %collective-permute-start.13 = (bf16[4,2048]{1,0:T(4,128)(2,1)S(1)}, bf16[4,2048]{1,0:T(4,128)(2,1)S(1)}, u32[]{:S(2)}, u32[]{:S(2)}) collective-permute-start(bf16[4,2048]{1,0:T(4,128)(2,1)S(1)} %get-tuple-element.20), channel_id=1, source_target_pairs={{0,4},{1,5},{2,6},{3,7},{4,0},{5,1},{6,2},{7,3},{8,12},{9,13},{10,... | collective-permute-start | bytes 49160 | tf_op jit(solution)/shard_map/ppermute | solution.py:101
  32.6 1.3 %collective-permute-done.11.refs_1_ = bf16[4,2048]{1,0:T(4,128)(2,1)S(1)} collective-permute-done((bf16[4,2048]{1,0:T(4,128)(2,1)S(1)}, bf16[4,2048]{1,0:T(4,128)(2,1)S(1)}, u32[]{:S(2)}, u32[]{:S(2)}) %collective-permute-start.11) | collective-permute-done | bytes 16416 | tf_op jit(solution)/shard_map/ppermute | solution.py:101
  34.5 0.6 %shard_map.79 = f32[1,4,2048]{2,1,0:T(4,128)} custom-call(bf16[4,2048]{1,0:T(4,128)(2,1)S(1)} %get-tuple-element.17.refs_0_, bf16[4,2048]{1,0:T(4,128)(2,1)S(1)} %collective-permute-done.11.refs_1_, bf16[4,2048]{1,0:T(4,128)(2,1)S(1)} %collective-permute-done.12.refs_2_, bf16[4,2048]{1,0:T(4,128)(2,1)S(1)} %collective-permute-done.13.refs_3_, ...), custom_call_target="tpu_custom_call" | custom-call | bytes 262144 | tf_op jit(solution)/shard_map/pallas_call | solution.py:14
  (23 shorter events, 1.1 us)
Async XLA Ops:
  0.0 20.7 %collective-permute-start.7 = (bf16[1,1536,2048]{2,1,0:T(8,128)(2,1)}, bf16[1,1536,2048]{2,1,0:T(8,128)(2,1)S(1)}, u32[]{:S(2)}, u32[]{:S(2)}) collective-permute-start(bf16[1,1536,2048]{2,1,0:T(8,128)(2,1)} %param.12), channel_id=1, source_target_pairs={{0,16},{16,0},{1,17},{17,1},{2,18},{18,2},{3,19},{19,3},{4,20},{20... | collective-permute-start | bytes 18874376 | tf_op jit(solution)/shard_map/ppermute | solution.py:104
  0.5 0.8 %copy-start.5 = (f32[1,4,2048]{2,1,0:T(4,128)S(1)}, f32[1,4,2048]{2,1,0:T(4,128)}, u32[]{:S(2)}) copy-start(f32[1,4,2048]{2,1,0:T(4,128)} %rows_ref.1) | copy-start | bytes 98308
  1.3 16.7 %copy-start = (bf16[1,2048,1536]{2,1,0:T(8,128)(2,1)S(1)}, bf16[1,2048,1536]{2,1,0:T(8,128)(2,1)}, u32[]{:S(2)}) copy-start(bf16[1,2048,1536]{2,1,0:T(8,128)(2,1)} %refs_4_.2) | copy-start | bytes 18874372
  1.3 16.7 %copy-start.3 = (f32[1,1536]{1,0:T(1,128)S(1)}, f32[1,1536]{1,0:T(1,128)}, u32[]{:S(2)}) copy-start(f32[1,1536]{1,0:T(1,128)} %refs_5_.1) | copy-start | bytes 18436
  1.3 16.6 %copy-start.4 = (f32[1,1536]{1,0:T(1,128)S(1)}, f32[1,1536]{1,0:T(1,128)}, u32[]{:S(2)}) copy-start(f32[1,1536]{1,0:T(1,128)} %refs_6_.1) | copy-start | bytes 18436
  1.3 6.4 %collective-permute-start.2 = (bf16[4,2048]{1,0:T(4,128)(2,1)S(1)}, bf16[4,2048]{1,0:T(4,128)(2,1)S(1)}, u32[]{:S(2)}, u32[]{:S(2)}) collective-permute-start(bf16[4,2048]{1,0:T(4,128)(2,1)S(1)} %shard_map.73.refs_0_), channel_id=1, source_target_pairs={{0,12},{1,13},{2,14},{3,15},{4,8},{5,9},{6,10},{7,11},{8,4},{9,5},... | collective-permute-start | bytes 49160 | tf_op jit(solution)/shard_map/ppermute | solution.py:101
  6.0 4.6 %collective-permute-start.1 = (bf16[4,2048]{1,0:T(4,128)(2,1)S(1)}, bf16[4,2048]{1,0:T(4,128)(2,1)S(1)}, u32[]{:S(2)}, u32[]{:S(2)}) collective-permute-start(bf16[4,2048]{1,0:T(4,128)(2,1)S(1)} %shard_map.73.refs_0_), channel_id=1, source_target_pairs={{0,8},{1,9},{2,10},{3,11},{4,12},{5,13},{6,14},{7,15},{8,0},{9,1},... | collective-permute-start | bytes 49160 | tf_op jit(solution)/shard_map/ppermute | solution.py:101
  6.0 4.6 %collective-permute-start = (bf16[4,2048]{1,0:T(4,128)(2,1)S(1)}, bf16[4,2048]{1,0:T(4,128)(2,1)S(1)}, u32[]{:S(2)}, u32[]{:S(2)}) collective-permute-start(bf16[4,2048]{1,0:T(4,128)(2,1)S(1)} %shard_map.73.refs_0_), channel_id=1, source_target_pairs={{0,4},{1,5},{2,6},{3,7},{4,0},{5,1},{6,2},{7,3},{8,12},{9,13},{10,... | collective-permute-start | bytes 49160 | tf_op jit(solution)/shard_map/ppermute | solution.py:101
  10.7 8.6 %copy-start.1 = (bf16[1,1536,2048]{2,1,0:T(8,128)(2,1)S(1)}, bf16[1,1536,2048]{2,1,0:T(8,128)(2,1)}, u32[]{:S(2)}) copy-start(bf16[1,1536,2048]{2,1,0:T(8,128)(2,1)} %dec_ref.1) | copy-start | bytes 18874372
  10.7 5.4 %collective-permute-start.5 = (bf16[16,2048]{1,0:T(8,128)(2,1)S(1)}, bf16[16,2048]{1,0:T(8,128)(2,1)S(1)}, u32[]{:S(2)}, u32[]{:S(2)}) collective-permute-start(bf16[16,2048]{1,0:T(8,128)(2,1)S(1)} %shard_map.74.refs_0_), channel_id=1, source_target_pairs={{0,3},{1,2},{2,1},{3,0},{4,7},{5,6},{6,5},{7,4},{8,11},{9,10},{10,... | collective-permute-start | bytes 196616 | tf_op jit(solution)/shard_map/ppermute | solution.py:101
  13.2 4.3 %collective-permute-start.4 = (bf16[16,2048]{1,0:T(8,128)(2,1)S(1)}, bf16[16,2048]{1,0:T(8,128)(2,1)S(1)}, u32[]{:S(2)}, u32[]{:S(2)}) collective-permute-start(bf16[16,2048]{1,0:T(8,128)(2,1)S(1)} %shard_map.74.refs_0_), channel_id=1, source_target_pairs={{0,2},{1,3},{2,0},{3,1},{4,6},{5,7},{6,4},{7,5},{8,10},{9,11},{10,... | collective-permute-start | bytes 196616 | tf_op jit(solution)/shard_map/ppermute | solution.py:101
  13.7 4.3 %collective-permute-start.3 = (bf16[16,2048]{1,0:T(8,128)(2,1)S(1)}, bf16[16,2048]{1,0:T(8,128)(2,1)S(1)}, u32[]{:S(2)}, u32[]{:S(2)}) collective-permute-start(bf16[16,2048]{1,0:T(8,128)(2,1)S(1)} %shard_map.74.refs_0_), channel_id=1, source_target_pairs={{0,1},{1,0},{2,3},{3,2},{4,5},{5,4},{6,7},{7,6},{8,9},{9,8},{10,11... | collective-permute-start | bytes 196616 | tf_op jit(solution)/shard_map/ppermute | solution.py:101
  19.2 15.3 %copy-start.2 = (f32[1,4,2048]{2,1,0:T(4,128)S(1)}, f32[1,4,2048]{2,1,0:T(4,128)}, u32[]{:S(2)}) copy-start(f32[1,4,2048]{2,1,0:T(4,128)} %refs_4_.3) | copy-start | bytes 98308
  19.2 1.5 %collective-permute-start.6 = (bf16[64,1536]{1,0:T(8,128)(2,1)S(1)}, bf16[64,1536]{1,0:T(8,128)(2,1)S(1)}, u32[]{:S(2)}, u32[]{:S(2)}) collective-permute-start(bf16[64,1536]{1,0:T(8,128)(2,1)S(1)} %shard_map.75.codes_ref), channel_id=1, source_target_pairs={{0,16},{16,0},{1,17},{17,1},{2,18},{18,2},{3,19},{19,3},{4,20},{20... | collective-permute-start | bytes 589832 | tf_op jit(solution)/shard_map/ppermute | solution.py:104
  20.8 5.5 %collective-permute-start.8 = (bf16[16,2048]{1,0:T(8,128)(2,1)S(1)}, bf16[16,2048]{1,0:T(8,128)(2,1)S(1)}, u32[]{:S(2)}, u32[]{:S(2)}) collective-permute-start(bf16[16,2048]{1,0:T(8,128)(2,1)S(1)} %get-tuple-element.14), channel_id=1, source_target_pairs={{0,3},{1,2},{2,1},{3,0},{4,7},{5,6},{6,5},{7,4},{8,11},{9,10},{10,... | collective-permute-start | bytes 196616 | tf_op jit(solution)/shard_map/ppermute | solution.py:101
  22.3 5.8 %collective-permute-start.9 = (bf16[16,2048]{1,0:T(8,128)(2,1)S(1)}, bf16[16,2048]{1,0:T(8,128)(2,1)S(1)}, u32[]{:S(2)}, u32[]{:S(2)}) collective-permute-start(bf16[16,2048]{1,0:T(8,128)(2,1)S(1)} %get-tuple-element.15), channel_id=1, source_target_pairs={{0,2},{1,3},{2,0},{3,1},{4,6},{5,7},{6,4},{7,5},{8,10},{9,11},{10,... | collective-permute-start | bytes 196616 | tf_op jit(solution)/shard_map/ppermute | solution.py:101
  22.8 5.3 %collective-permute-start.10 = (bf16[16,2048]{1,0:T(8,128)(2,1)S(1)}, bf16[16,2048]{1,0:T(8,128)(2,1)S(1)}, u32[]{:S(2)}, u32[]{:S(2)}) collective-permute-start(bf16[16,2048]{1,0:T(8,128)(2,1)S(1)} %get-tuple-element.16), channel_id=1, source_target_pairs={{0,1},{1,0},{2,3},{3,2},{4,5},{5,4},{6,7},{7,6},{8,9},{9,8},{10,11... | collective-permute-start | bytes 196616 | tf_op jit(solution)/shard_map/ppermute | solution.py:101
  28.1 5.8 %collective-permute-start.11 = (bf16[4,2048]{1,0:T(4,128)(2,1)S(1)}, bf16[4,2048]{1,0:T(4,128)(2,1)S(1)}, u32[]{:S(2)}, u32[]{:S(2)}) collective-permute-start(bf16[4,2048]{1,0:T(4,128)(2,1)S(1)} %get-tuple-element.18), channel_id=1, source_target_pairs={{0,12},{1,13},{2,14},{3,15},{4,8},{5,9},{6,10},{7,11},{8,4},{9,5},... | collective-permute-start | bytes 49160 | tf_op jit(solution)/shard_map/ppermute | solution.py:101
  29.7 4.7 %collective-permute-start.12 = (bf16[4,2048]{1,0:T(4,128)(2,1)S(1)}, bf16[4,2048]{1,0:T(4,128)(2,1)S(1)}, u32[]{:S(2)}, u32[]{:S(2)}) collective-permute-start(bf16[4,2048]{1,0:T(4,128)(2,1)S(1)} %get-tuple-element.19), channel_id=1, source_target_pairs={{0,8},{1,9},{2,10},{3,11},{4,12},{5,13},{6,14},{7,15},{8,0},{9,1},... | collective-permute-start | bytes 49160 | tf_op jit(solution)/shard_map/ppermute | solution.py:101
  30.3 4.2 %collective-permute-start.13 = (bf16[4,2048]{1,0:T(4,128)(2,1)S(1)}, bf16[4,2048]{1,0:T(4,128)(2,1)S(1)}, u32[]{:S(2)}, u32[]{:S(2)}) collective-permute-start(bf16[4,2048]{1,0:T(4,128)(2,1)S(1)} %get-tuple-element.20), channel_id=1, source_target_pairs={{0,4},{1,5},{2,6},{3,7},{4,0},{5,1},{6,2},{7,3},{8,12},{9,13},{10,... | collective-permute-start | bytes 49160 | tf_op jit(solution)/shard_map/ppermute | solution.py:101

commit v4 on v3

--- a/solution.py
+++ b/solution.py
@@ -1,3 +1,5 @@
+import functools
+
 import jax
 import jax.numpy as jnp
 from jax import lax
@@ -8,6 +10,7 @@
 VMEM = pl.BlockSpec(memory_space=pltpu.VMEM)
 GRANT = 8 * 2**20
 RADIX = 4
+TALL = 128
 
 
 def call(kernel, out_shape, args, flops=0, moved=2**18):
@@ -21,10 +24,26 @@
     )(*args)
 
 
-def normalise_kernel(rows_ref, out_ref):
-    rows = rows_ref[0]
-    scale = lax.rsqrt(jnp.mean(rows * rows, axis=1, keepdims=True) + 1e-05)
-    out_ref[...] = (rows * scale).astype(jnp.bfloat16)
+def dot(rows, weights):
+    count = rows.shape[0]
+    short = -count % TALL
+    if short:
+        rows = jnp.concatenate([rows, jnp.zeros((short, rows.shape[1]), rows.dtype)], axis=0)
+    return jnp.dot(rows, weights, preferred_element_type=jnp.float32)[:count]
+
+
+def scaled(rows):
+    return rows * lax.rsqrt(jnp.mean(rows * rows, axis=1, keepdims=True) + 1e-05)
+
+
+def own_kernel(rows_ref, out_ref):
+    out_ref[...] = scaled(rows_ref[0])
+
+
+def normalise_kernel(order, own_ref, *refs):
+    *block_refs, out_ref = refs
+    rows = [own_ref[...]] + [scaled(block_refs[order.index(j)][0]) for j in sorted(order)]
+    out_ref[...] = jnp.concatenate(rows, axis=0).astype(jnp.bfloat16)
 
 
 def stack_kernel(*refs):
@@ -36,12 +55,12 @@
 def encode_kernel(*refs):
     *block_refs, enc_ref, bias_ref, limit_ref, codes_ref = refs
     rows = jnp.concatenate([ref[...] for ref in block_refs], axis=0)
-    pre = jnp.dot(rows, enc_ref[0], preferred_element_type=jnp.float32) + bias_ref[...]
+    pre = dot(rows, enc_ref[0]) + bias_ref[...]
     codes_ref[...] = (pre * jax.nn.sigmoid((pre - limit_ref[...]) / 0.1)).astype(jnp.bfloat16)
 
 
 def decode_kernel(codes_ref, dec_ref, own_ref):
-    own_ref[...] = jnp.dot(codes_ref[...], dec_ref[0], preferred_element_type=jnp.float32)
+    own_ref[...] = dot(codes_ref[...], dec_ref[0])
 
 
 def cut(total, part_refs):
@@ -59,7 +78,7 @@
 
     @pl.when(jnp.logical_not(first))
     def _():
-        carried = jnp.dot(before_ref[...], dec_ref[0], preferred_element_type=jnp.float32)
+        carried = dot(before_ref[...], dec_ref[0])
         cut(own_ref[...] + carried, part_refs)
 
 
@@ -105,11 +124,18 @@
 
     arrived_dec = onward(dec_next)
 
-    line = call(normalise_kernel, shape((block, depth), half), (source,), 2**36, 2**27)
-    for at, (stride, radix) in enumerate(reversed(steps)):
-        blocks = [line] + [swap(line, stride * j) for j in range(1, radix)]
-        if at < len(steps) - 1:
-            line = call(stack_kernel, shape((radix * line.shape[0], depth), half), blocks, 2**34)
+    *others, (stride, radix) = steps
+    order = [radix - 1, *range(1, radix - 1)] if radix > 1 else []
+    blocks = [swap(source, stride * j) for j in order]
+    own = call(own_kernel, shape((block, depth), full), (source,), 2**36, 2**27)
+    size = radix * block
+    kernel = functools.partial(normalise_kernel, order)
+    blocks = [call(kernel, shape((size, depth), half), [own] + blocks, 2**34)]
+    for stride, radix in reversed(others):
+        if len(blocks) > 1:
+            blocks = [call(stack_kernel, shape((size, depth), half), blocks, 2**34)]
+        blocks += [swap(blocks[0], stride * j) for j in range(1, radix)]
+        size *= radix
 
     codes = call(encode_kernel, shape((rows, width), half), (*blocks, w_enc, b_enc, threshold), work)
     before = onward(codes)
@@ -122,7 +148,7 @@
         if at < len(steps) - 1:
             following = steps[at + 1][1]
             size //= following
-            kernel = lambda *refs, count=radix: split_kernel(count, *refs)
+            kernel = functools.partial(split_kernel, radix)
             parts = call(kernel, (shape((size, depth), half),) * following, blocks)
     return call(finish_kernel, shape(target.shape, full), (*blocks, target))
 

time: 35.3 us -> 34.6 us (0.980)
    ppermute x2, starting transfers between devices: 0.52 us -> 0.07 us  [onward(): lax.ppermute(value, 'layer', [(i, (i + 1) % layers) for i in range(layers)])]
    ppermute x12, waiting for transfers between devices: 13.4 us -> 12.9 us  [swap(): return lax.ppermute(value, 'feat', [(i, i ^ flip) for i in range(feats)])]
  transfers between devices with their start and end apart: 14 -> 14, of which waited for: 11 -> 11; matrix products, arithmetic and copies ran while one was open for 0% -> 0% of each run, Pallas kernels for 7% -> 6%
where the time goes in v4:
time: 34.6 us; the launch traced here: 34.4 us
  starting transfers between devices  17.2 us (50%)
  waiting for transfers between devices  13.4 us (39%)
  Pallas kernels  2.9 us (8%)
  local copies, waits for them, and re-layouts  0.81 us (2%)
    ppermute x12, starting transfers between devices, swap(): return lax.ppermute(value, 'feat', [(i, i ^ flip) for i in range(feats)])  17.2 us
    ppermute x12, waiting for transfers between devices, swap(): return lax.ppermute(value, 'feat', [(i, i ^ flip) for i in range(feats)])  12.9 us
    pallas_call x7, Pallas kernels, call(): pl.pallas_call(kernel, out_shape=out_shape, in_specs=[VMEM] * len(args),...  2.9 us
    unnamed x12, local copies, waits for them, and re-layouts  0.81 us
  transfers between devices with their start and end apart: 14, of which 11 were waited for; matrix products, arithmetic and copies ran while one was open for 0% of the time, Pallas kernels for 6%

profile of v4, /device:TPU:0, one launch (start us, length us, event | category | flops | bytes accessed | tf_op | source)
XLA Modules:
  0.0 34.4 jit_solution(4121746036180727002)
XLA Ops:
  0.0 5.0 %collective-permute-start = (f32[1,4,2048]{2,1,0:T(4,128)}, f32[1,4,2048]{2,1,0:T(4,128)S(1)}, u32[]{:S(2)}, u32[]{:S(2)}) collective-permute-start(f32[1,4,2048]{2,1,0:T(4,128)} %rows_ref.1), channel_id=1, source_target_pairs={{0,12},{1,13},{2,14},{3,15},{4,8},{5,9},{6,10},{7,11},{8,4},{9,5},... | collective-permute-start | bytes 98312 | tf_op jit(solution)/shard_map/ppermute | solution.py:120
  5.1 0.6 %collective-permute-start.1 = (f32[1,4,2048]{2,1,0:T(4,128)}, f32[1,4,2048]{2,1,0:T(4,128)S(1)}, u32[]{:S(2)}, u32[]{:S(2)}) collective-permute-start(f32[1,4,2048]{2,1,0:T(4,128)} %rows_ref.1), channel_id=1, source_target_pairs={{0,4},{1,5},{2,6},{3,7},{4,0},{5,1},{6,2},{7,3},{8,12},{9,13},{10,... | collective-permute-start | bytes 98312 | tf_op jit(solution)/shard_map/ppermute | solution.py:120
  5.6 0.8 %copy-done.5 = f32[1,4,2048]{2,1,0:T(4,128)S(1)} copy-done((f32[1,4,2048]{2,1,0:T(4,128)S(1)}, f32[1,4,2048]{2,1,0:T(4,128)}, u32[]{:S(2)}) %copy-start.5) | copy-done | bytes 32792
  6.5 0.6 %collective-permute-done.refs_0_ = f32[1,4,2048]{2,1,0:T(4,128)S(1)} collective-permute-done((f32[1,4,2048]{2,1,0:T(4,128)}, f32[1,4,2048]{2,1,0:T(4,128)S(1)}, u32[]{:S(2)}, u32[]{:S(2)}) %collective-permute-start) | collective-permute-done | bytes 32800 | tf_op jit(solution)/shard_map/ppermute | solution.py:120
  7.2 2.9 %collective-permute-done.2.refs_2_ = f32[1,4,2048]{2,1,0:T(4,128)S(1)} collective-permute-done((f32[1,4,2048]{2,1,0:T(4,128)}, f32[1,4,2048]{2,1,0:T(4,128)S(1)}, u32[]{:S(2)}, u32[]{:S(2)}) %collective-permute-start.2) | collective-permute-done | bytes 32800 | tf_op jit(solution)/shard_map/ppermute | solution.py:120
  10.2 2.5 %collective-permute-start.5 = (bf16[16,2048]{1,0:T(8,128)(2,1)S(1)}, bf16[16,2048]{1,0:T(8,128)(2,1)S(1)}, u32[]{:S(2)}, u32[]{:S(2)}) collective-permute-start(bf16[16,2048]{1,0:T(8,128)(2,1)S(1)} %shard_map.74.refs_0_), channel_id=1, source_target_pairs={{0,3},{1,2},{2,1},{3,0},{4,7},{5,6},{6,5},{7,4},{8,11},{9,10},{10,... | collective-permute-start | bytes 196616 | tf_op jit(solution)/shard_map/ppermute | solution.py:120
  12.7 0.5 %collective-permute-start.4 = (bf16[16,2048]{1,0:T(8,128)(2,1)S(1)}, bf16[16,2048]{1,0:T(8,128)(2,1)S(1)}, u32[]{:S(2)}, u32[]{:S(2)}) collective-permute-start(bf16[16,2048]{1,0:T(8,128)(2,1)S(1)} %shard_map.74.refs_0_), channel_id=1, source_target_pairs={{0,2},{1,3},{2,0},{3,1},{4,6},{5,7},{6,4},{7,5},{8,10},{9,11},{10,... | collective-permute-start | bytes 196616 | tf_op jit(solution)/shard_map/ppermute | solution.py:120
  13.2 0.5 %collective-permute-start.3 = (bf16[16,2048]{1,0:T(8,128)(2,1)S(1)}, bf16[16,2048]{1,0:T(8,128)(2,1)S(1)}, u32[]{:S(2)}, u32[]{:S(2)}) collective-permute-start(bf16[16,2048]{1,0:T(8,128)(2,1)S(1)} %shard_map.74.refs_0_), channel_id=1, source_target_pairs={{0,1},{1,0},{2,3},{3,2},{4,5},{5,4},{6,7},{7,6},{8,9},{9,8},{10,11... | collective-permute-start | bytes 196616 | tf_op jit(solution)/shard_map/ppermute | solution.py:120
  13.8 2.3 %collective-permute-done.5.refs_3_ = bf16[16,2048]{1,0:T(8,128)(2,1)S(1)} collective-permute-done((bf16[16,2048]{1,0:T(8,128)(2,1)S(1)}, bf16[16,2048]{1,0:T(8,128)(2,1)S(1)}, u32[]{:S(2)}, u32[]{:S(2)}) %collective-permute-start.5) | collective-permute-done | bytes 65568 | tf_op jit(solution)/shard_map/ppermute | solution.py:120
  16.0 1.0 %collective-permute-done.4.refs_2_ = bf16[16,2048]{1,0:T(8,128)(2,1)S(1)} collective-permute-done((bf16[16,2048]{1,0:T(8,128)(2,1)S(1)}, bf16[16,2048]{1,0:T(8,128)(2,1)S(1)}, u32[]{:S(2)}, u32[]{:S(2)}) %collective-permute-start.4) | collective-permute-done | bytes 65568 | tf_op jit(solution)/shard_map/ppermute | solution.py:120
  17.0 0.5 %collective-permute-done.3.refs_1_ = bf16[16,2048]{1,0:T(8,128)(2,1)S(1)} collective-permute-done((bf16[16,2048]{1,0:T(8,128)(2,1)S(1)}, bf16[16,2048]{1,0:T(8,128)(2,1)S(1)}, u32[]{:S(2)}, u32[]{:S(2)}) %collective-permute-start.3) | collective-permute-done | bytes 65568 | tf_op jit(solution)/shard_map/ppermute | solution.py:120
  17.5 1.0 %shard_map.75.codes_ref = bf16[64,1536]{1,0:T(8,128)(2,1)S(1)} custom-call(bf16[16,2048]{1,0:T(8,128)(2,1)S(1)} %shard_map.74.refs_0_, bf16[16,2048]{1,0:T(8,128)(2,1)S(1)} %collective-permute-done.3.refs_1_, bf16[16,2048]{1,0:T(8,128)(2,1)S(1)} %collective-permute-done.4.refs_2_, bf16[16,2048]{1,0:T(8,128)(2,1)S(1)} %collective-permute-done.5.refs_3_, ...), custom_call_target="tpu_custom_call" | custom-call | flops 402653184 | bytes 262144 | tf_op jit(solution)/shard_map/pallas_call | solution.py:17
  18.6 1.0 %shard_map.76.own_ref = f32[64,2048]{1,0:T(8,128)S(1)} custom-call(bf16[64,1536]{1,0:T(8,128)(2,1)S(1)} %shard_map.75.codes_ref, bf16[1,1536,2048]{2,1,0:T(8,128)(2,1)S(1)} %copy-done.1), custom_call_target="tpu_custom_call" | custom-call | flops 402653184 | bytes 262144 | tf_op jit(solution)/shard_map/pallas_call | solution.py:17
  20.1 1.6 %collective-permute-start.8 = (bf16[16,2048]{1,0:T(8,128)(2,1)S(1)}, bf16[16,2048]{1,0:T(8,128)(2,1)S(1)}, u32[]{:S(2)}, u32[]{:S(2)}) collective-permute-start(bf16[16,2048]{1,0:T(8,128)(2,1)S(1)} %get-tuple-element.14), channel_id=1, source_target_pairs={{0,3},{1,2},{2,1},{3,0},{4,7},{5,6},{6,5},{7,4},{8,11},{9,10},{10,... | collective-permute-start | bytes 196616 | tf_op jit(solution)/shard_map/ppermute | solution.py:120
  21.6 0.5 %collective-permute-start.9 = (bf16[16,2048]{1,0:T(8,128)(2,1)S(1)}, bf16[16,2048]{1,0:T(8,128)(2,1)S(1)}, u32[]{:S(2)}, u32[]{:S(2)}) collective-permute-start(bf16[16,2048]{1,0:T(8,128)(2,1)S(1)} %get-tuple-element.15), channel_id=1, source_target_pairs={{0,2},{1,3},{2,0},{3,1},{4,6},{5,7},{6,4},{7,5},{8,10},{9,11},{10,... | collective-permute-start | bytes 196616 | tf_op jit(solution)/shard_map/ppermute | solution.py:120
  22.1 1.5 %collective-permute-start.10 = (bf16[16,2048]{1,0:T(8,128)(2,1)S(1)}, bf16[16,2048]{1,0:T(8,128)(2,1)S(1)}, u32[]{:S(2)}, u32[]{:S(2)}) collective-permute-start(bf16[16,2048]{1,0:T(8,128)(2,1)S(1)} %get-tuple-element.16), channel_id=1, source_target_pairs={{0,1},{1,0},{2,3},{3,2},{4,5},{5,4},{6,7},{7,6},{8,9},{9,8},{10,11... | collective-permute-start | bytes 196616 | tf_op jit(solution)/shard_map/ppermute | solution.py:120
  23.6 2.3 %collective-permute-done.8.refs_1_ = bf16[16,2048]{1,0:T(8,128)(2,1)S(1)} collective-permute-done((bf16[16,2048]{1,0:T(8,128)(2,1)S(1)}, bf16[16,2048]{1,0:T(8,128)(2,1)S(1)}, u32[]{:S(2)}, u32[]{:S(2)}) %collective-permute-start.8) | collective-permute-done | bytes 65568 | tf_op jit(solution)/shard_map/ppermute | solution.py:120
  26.0 1.4 %collective-permute-done.9.refs_2_ = bf16[16,2048]{1,0:T(8,128)(2,1)S(1)} collective-permute-done((bf16[16,2048]{1,0:T(8,128)(2,1)S(1)}, bf16[16,2048]{1,0:T(8,128)(2,1)S(1)}, u32[]{:S(2)}, u32[]{:S(2)}) %collective-permute-start.9) | collective-permute-done | bytes 65568 | tf_op jit(solution)/shard_map/ppermute | solution.py:120
  27.5 1.6 %collective-permute-start.11 = (bf16[4,2048]{1,0:T(4,128)(2,1)S(1)}, bf16[4,2048]{1,0:T(4,128)(2,1)S(1)}, u32[]{:S(2)}, u32[]{:S(2)}) collective-permute-start(bf16[4,2048]{1,0:T(4,128)(2,1)S(1)} %get-tuple-element.18), channel_id=1, source_target_pairs={{0,12},{1,13},{2,14},{3,15},{4,8},{5,9},{6,10},{7,11},{8,4},{9,5},... | collective-permute-start | bytes 49160 | tf_op jit(solution)/shard_map/ppermute | solution.py:120
  29.0 0.6 %collective-permute-start.12 = (bf16[4,2048]{1,0:T(4,128)(2,1)S(1)}, bf16[4,2048]{1,0:T(4,128)(2,1)S(1)}, u32[]{:S(2)}, u32[]{:S(2)}) collective-permute-start(bf16[4,2048]{1,0:T(4,128)(2,1)S(1)} %get-tuple-element.19), channel_id=1, source_target_pairs={{0,8},{1,9},{2,10},{3,11},{4,12},{5,13},{6,14},{7,15},{8,0},{9,1},... | collective-permute-start | bytes 49160 | tf_op jit(solution)/shard_map/ppermute | solution.py:120
  29.6 2.3 %collective-permute-start.13 = (bf16[4,2048]{1,0:T(4,128)(2,1)S(1)}, bf16[4,2048]{1,0:T(4,128)(2,1)S(1)}, u32[]{:S(2)}, u32[]{:S(2)}) collective-permute-start(bf16[4,2048]{1,0:T(4,128)(2,1)S(1)} %get-tuple-element.20), channel_id=1, source_target_pairs={{0,4},{1,5},{2,6},{3,7},{4,0},{5,1},{6,2},{7,3},{8,12},{9,13},{10,... | collective-permute-start | bytes 49160 | tf_op jit(solution)/shard_map/ppermute | solution.py:120
  31.9 1.3 %collective-permute-done.11.refs_1_ = bf16[4,2048]{1,0:T(4,128)(2,1)S(1)} collective-permute-done((bf16[4,2048]{1,0:T(4,128)(2,1)S(1)}, bf16[4,2048]{1,0:T(4,128)(2,1)S(1)}, u32[]{:S(2)}, u32[]{:S(2)}) %collective-permute-start.11) | collective-permute-done | bytes 16416 | tf_op jit(solution)/shard_map/ppermute | solution.py:120
  33.2 0.4 %collective-permute-done.12.refs_2_ = bf16[4,2048]{1,0:T(4,128)(2,1)S(1)} collective-permute-done((bf16[4,2048]{1,0:T(4,128)(2,1)S(1)}, bf16[4,2048]{1,0:T(4,128)(2,1)S(1)}, u32[]{:S(2)}, u32[]{:S(2)}) %collective-permute-start.12) | collective-permute-done | bytes 16416 | tf_op jit(solution)/shard_map/ppermute | solution.py:120
  33.8 0.6 %shard_map.79 = f32[1,4,2048]{2,1,0:T(4,128)} custom-call(bf16[4,2048]{1,0:T(4,128)(2,1)S(1)} %get-tuple-element.17.refs_0_, bf16[4,2048]{1,0:T(4,128)(2,1)S(1)} %collective-permute-done.11.refs_1_, bf16[4,2048]{1,0:T(4,128)(2,1)S(1)} %collective-permute-done.12.refs_2_, bf16[4,2048]{1,0:T(4,128)(2,1)S(1)} %collective-permute-done.13.refs_3_, ...), custom_call_target="tpu_custom_call" | custom-call | bytes 262144 | tf_op jit(solution)/shard_map/pallas_call | solution.py:17
  (23 shorter events, 1.0 us)
Async XLA Ops:
  0.0 7.2 %collective-permute-start = (f32[1,4,2048]{2,1,0:T(4,128)}, f32[1,4,2048]{2,1,0:T(4,128)S(1)}, u32[]{:S(2)}, u32[]{:S(2)}) collective-permute-start(f32[1,4,2048]{2,1,0:T(4,128)} %rows_ref.1), channel_id=1, source_target_pairs={{0,12},{1,13},{2,14},{3,15},{4,8},{5,9},{6,10},{7,11},{8,4},{9,5},... | collective-permute-start | bytes 98312 | tf_op jit(solution)/shard_map/ppermute | solution.py:120
  5.0 5.0 %collective-permute-start.2 = (f32[1,4,2048]{2,1,0:T(4,128)}, f32[1,4,2048]{2,1,0:T(4,128)S(1)}, u32[]{:S(2)}, u32[]{:S(2)}) collective-permute-start(f32[1,4,2048]{2,1,0:T(4,128)} %rows_ref.1), channel_id=1, source_target_pairs={{0,8},{1,9},{2,10},{3,11},{4,12},{5,13},{6,14},{7,15},{8,0},{9,1},... | collective-permute-start | bytes 98312 | tf_op jit(solution)/shard_map/ppermute | solution.py:120
  5.1 5.0 %collective-permute-start.1 = (f32[1,4,2048]{2,1,0:T(4,128)}, f32[1,4,2048]{2,1,0:T(4,128)S(1)}, u32[]{:S(2)}, u32[]{:S(2)}) collective-permute-start(f32[1,4,2048]{2,1,0:T(4,128)} %rows_ref.1), channel_id=1, source_target_pairs={{0,4},{1,5},{2,6},{3,7},{4,0},{5,1},{6,2},{7,3},{8,12},{9,13},{10,... | collective-permute-start | bytes 98312 | tf_op jit(solution)/shard_map/ppermute | solution.py:120
  5.6 14.4 %collective-permute-start.7 = (bf16[1,1536,2048]{2,1,0:T(8,128)(2,1)}, bf16[1,1536,2048]{2,1,0:T(8,128)(2,1)S(1)}, u32[]{:S(2)}, u32[]{:S(2)}) collective-permute-start(bf16[1,1536,2048]{2,1,0:T(8,128)(2,1)} %param.12), channel_id=1, source_target_pairs={{0,16},{16,0},{1,17},{17,1},{2,18},{18,2},{3,19},{19,3},{4,20},{20... | collective-permute-start | bytes 18874376 | tf_op jit(solution)/shard_map/ppermute | solution.py:123
  5.6 0.8 %copy-start.5 = (f32[1,4,2048]{2,1,0:T(4,128)S(1)}, f32[1,4,2048]{2,1,0:T(4,128)}, u32[]{:S(2)}) copy-start(f32[1,4,2048]{2,1,0:T(4,128)} %rows_ref.1) | copy-start | bytes 98308
  6.5 11.0 %copy-start = (bf16[1,2048,1536]{2,1,0:T(8,128)(2,1)S(1)}, bf16[1,2048,1536]{2,1,0:T(8,128)(2,1)}, u32[]{:S(2)}) copy-start(bf16[1,2048,1536]{2,1,0:T(8,128)(2,1)} %refs_4_.2) | copy-start | bytes 18874372
  6.5 11.0 %copy-start.3 = (f32[1,1536]{1,0:T(1,128)S(1)}, f32[1,1536]{1,0:T(1,128)}, u32[]{:S(2)}) copy-start(f32[1,1536]{1,0:T(1,128)} %refs_5_.1) | copy-start | bytes 18436
  6.5 11.0 %copy-start.4 = (f32[1,1536]{1,0:T(1,128)S(1)}, f32[1,1536]{1,0:T(1,128)}, u32[]{:S(2)}) copy-start(f32[1,1536]{1,0:T(1,128)} %refs_6_.1) | copy-start | bytes 18436
  10.2 8.4 %copy-start.1 = (bf16[1,1536,2048]{2,1,0:T(8,128)(2,1)S(1)}, bf16[1,1536,2048]{2,1,0:T(8,128)(2,1)}, u32[]{:S(2)}) copy-start(bf16[1,1536,2048]{2,1,0:T(8,128)(2,1)} %dec_ref.1) | copy-start | bytes 18874372
  10.2 5.8 %collective-permute-start.5 = (bf16[16,2048]{1,0:T(8,128)(2,1)S(1)}, bf16[16,2048]{1,0:T(8,128)(2,1)S(1)}, u32[]{:S(2)}, u32[]{:S(2)}) collective-permute-start(bf16[16,2048]{1,0:T(8,128)(2,1)S(1)} %shard_map.74.refs_0_), channel_id=1, source_target_pairs={{0,3},{1,2},{2,1},{3,0},{4,7},{5,6},{6,5},{7,4},{8,11},{9,10},{10,... | collective-permute-start | bytes 196616 | tf_op jit(solution)/shard_map/ppermute | solution.py:120
  12.7 4.3 %collective-permute-start.4 = (bf16[16,2048]{1,0:T(8,128)(2,1)S(1)}, bf16[16,2048]{1,0:T(8,128)(2,1)S(1)}, u32[]{:S(2)}, u32[]{:S(2)}) collective-permute-start(bf16[16,2048]{1,0:T(8,128)(2,1)S(1)} %shard_map.74.refs_0_), channel_id=1, source_target_pairs={{0,2},{1,3},{2,0},{3,1},{4,6},{5,7},{6,4},{7,5},{8,10},{9,11},{10,... | collective-permute-start | bytes 196616 | tf_op jit(solution)/shard_map/ppermute | solution.py:120
  13.2 4.3 %collective-permute-start.3 = (bf16[16,2048]{1,0:T(8,128)(2,1)S(1)}, bf16[16,2048]{1,0:T(8,128)(2,1)S(1)}, u32[]{:S(2)}, u32[]{:S(2)}) collective-permute-start(bf16[16,2048]{1,0:T(8,128)(2,1)S(1)} %shard_map.74.refs_0_), channel_id=1, source_target_pairs={{0,1},{1,0},{2,3},{3,2},{4,5},{5,4},{6,7},{7,6},{8,9},{9,8},{10,11... | collective-permute-start | bytes 196616 | tf_op jit(solution)/shard_map/ppermute | solution.py:120
  18.5 15.3 %copy-start.2 = (f32[1,4,2048]{2,1,0:T(4,128)S(1)}, f32[1,4,2048]{2,1,0:T(4,128)}, u32[]{:S(2)}) copy-start(f32[1,4,2048]{2,1,0:T(4,128)} %refs_4_.3) | copy-start | bytes 98308
  18.5 1.5 %collective-permute-start.6 = (bf16[64,1536]{1,0:T(8,128)(2,1)S(1)}, bf16[64,1536]{1,0:T(8,128)(2,1)S(1)}, u32[]{:S(2)}, u32[]{:S(2)}) collective-permute-start(bf16[64,1536]{1,0:T(8,128)(2,1)S(1)} %shard_map.75.codes_ref), channel_id=1, source_target_pairs={{0,16},{16,0},{1,17},{17,1},{2,18},{18,2},{3,19},{19,3},{4,20},{20... | collective-permute-start | bytes 589832 | tf_op jit(solution)/shard_map/ppermute | solution.py:123
  20.1 5.9 %collective-permute-start.8 = (bf16[16,2048]{1,0:T(8,128)(2,1)S(1)}, bf16[16,2048]{1,0:T(8,128)(2,1)S(1)}, u32[]{:S(2)}, u32[]{:S(2)}) collective-permute-start(bf16[16,2048]{1,0:T(8,128)(2,1)S(1)} %get-tuple-element.14), channel_id=1, source_target_pairs={{0,3},{1,2},{2,1},{3,0},{4,7},{5,6},{6,5},{7,4},{8,11},{9,10},{10,... | collective-permute-start | bytes 196616 | tf_op jit(solution)/shard_map/ppermute | solution.py:120
  21.6 5.8 %collective-permute-start.9 = (bf16[16,2048]{1,0:T(8,128)(2,1)S(1)}, bf16[16,2048]{1,0:T(8,128)(2,1)S(1)}, u32[]{:S(2)}, u32[]{:S(2)}) collective-permute-start(bf16[16,2048]{1,0:T(8,128)(2,1)S(1)} %get-tuple-element.15), channel_id=1, source_target_pairs={{0,2},{1,3},{2,0},{3,1},{4,6},{5,7},{6,4},{7,5},{8,10},{9,11},{10,... | collective-permute-start | bytes 196616 | tf_op jit(solution)/shard_map/ppermute | solution.py:120
  22.1 5.3 %collective-permute-start.10 = (bf16[16,2048]{1,0:T(8,128)(2,1)S(1)}, bf16[16,2048]{1,0:T(8,128)(2,1)S(1)}, u32[]{:S(2)}, u32[]{:S(2)}) collective-permute-start(bf16[16,2048]{1,0:T(8,128)(2,1)S(1)} %get-tuple-element.16), channel_id=1, source_target_pairs={{0,1},{1,0},{2,3},{3,2},{4,5},{5,4},{6,7},{7,6},{8,9},{9,8},{10,11... | collective-permute-start | bytes 196616 | tf_op jit(solution)/shard_map/ppermute | solution.py:120
  27.5 5.8 %collective-permute-start.11 = (bf16[4,2048]{1,0:T(4,128)(2,1)S(1)}, bf16[4,2048]{1,0:T(4,128)(2,1)S(1)}, u32[]{:S(2)}, u32[]{:S(2)}) collective-permute-start(bf16[4,2048]{1,0:T(4,128)(2,1)S(1)} %get-tuple-element.18), channel_id=1, source_target_pairs={{0,12},{1,13},{2,14},{3,15},{4,8},{5,9},{6,10},{7,11},{8,4},{9,5},... | collective-permute-start | bytes 49160 | tf_op jit(solution)/shard_map/ppermute | solution.py:120
  29.0 4.7 %collective-permute-start.12 = (bf16[4,2048]{1,0:T(4,128)(2,1)S(1)}, bf16[4,2048]{1,0:T(4,128)(2,1)S(1)}, u32[]{:S(2)}, u32[]{:S(2)}) collective-permute-start(bf16[4,2048]{1,0:T(4,128)(2,1)S(1)} %get-tuple-element.19), channel_id=1, source_target_pairs={{0,8},{1,9},{2,10},{3,11},{4,12},{5,13},{6,14},{7,15},{8,0},{9,1},... | collective-permute-start | bytes 49160 | tf_op jit(solution)/shard_map/ppermute | solution.py:120
  29.6 4.2 %collective-permute-start.13 = (bf16[4,2048]{1,0:T(4,128)(2,1)S(1)}, bf16[4,2048]{1,0:T(4,128)(2,1)S(1)}, u32[]{:S(2)}, u32[]{:S(2)}) collective-permute-start(bf16[4,2048]{1,0:T(4,128)(2,1)S(1)} %get-tuple-element.20), channel_id=1, source_target_pairs={{0,4},{1,5},{2,6},{3,7},{4,0},{5,1},{6,2},{7,3},{8,12},{9,13},{10,... | collective-permute-start | bytes 49160 | tf_op jit(solution)/shard_map/ppermute | solution.py:120

commit v5 on v4

--- a/solution.py
+++ b/solution.py
@@ -2,6 +2,7 @@
 
 import jax
 import jax.numpy as jnp
+import numpy as np
 from jax import lax
 from jax.experimental import pallas as pl
 from jax.experimental.pallas import tpu as pltpu
@@ -69,7 +70,7 @@
         part_ref[...] = total[i * size : (i + 1) * size].astype(jnp.bfloat16)
 
 
-def join_kernel(own_ref, before_ref, dec_ref, *part_refs):
+def join_kernel(places, own_ref, before_ref, dec_ref, *part_refs):
     first = lax.axis_index("layer") == 0
 
     @pl.when(first)
@@ -79,6 +80,8 @@
     @pl.when(jnp.logical_not(first))
     def _():
         carried = dot(before_ref[...], dec_ref[0])
+        block = carried.shape[0] // len(places)
+        carried = jnp.concatenate([carried[i * block : (i + 1) * block] for i in places], axis=0)
         cut(own_ref[...] + carried, part_refs)
 
 
@@ -116,40 +119,50 @@
     shape = jax.ShapeDtypeStruct
     steps = digits(feats)
 
-    def swap(value, flip):
-        return lax.ppermute(value, "feat", [(i, i ^ flip) for i in range(feats)])
+    radices = [radix for _, radix in steps]
+    turned = radices == radices[::-1]
+    strides = [[stride for stride, _ in steps]] * 2
+    if turned:
+        strides = [strides[0], strides[0][::-1]]
+    places = np.arange(feats).reshape(radices)
+    places = [int(i) for i in (places.T if turned else places).ravel()]
+
+    def swap(value, stage, j):
+        flips = [strides[k % 2][stage] * j for k in range(layers)]
+        pairs = [(k * feats + i, k * feats + (i ^ flips[k])) for k in range(layers) for i in range(feats)]
+        return lax.ppermute(value, ("layer", "feat"), pairs)
 
     def onward(value):
         return lax.ppermute(value, "layer", [(i, (i + 1) % layers) for i in range(layers)])
 
     arrived_dec = onward(dec_next)
 
-    *others, (stride, radix) = steps
+    last, radix = len(steps) - 1, radices[-1]
     order = [radix - 1, *range(1, radix - 1)] if radix > 1 else []
-    blocks = [swap(source, stride * j) for j in order]
+    blocks = [swap(source, last, j) for j in order]
     own = call(own_kernel, shape((block, depth), full), (source,), 2**36, 2**27)
     size = radix * block
     kernel = functools.partial(normalise_kernel, order)
     blocks = [call(kernel, shape((size, depth), half), [own] + blocks, 2**34)]
-    for stride, radix in reversed(others):
+    for stage in reversed(range(last)):
         if len(blocks) > 1:
             blocks = [call(stack_kernel, shape((size, depth), half), blocks, 2**34)]
-        blocks += [swap(blocks[0], stride * j) for j in range(1, radix)]
-        size *= radix
+        blocks += [swap(blocks[0], stage, j) for j in range(1, radices[stage])]
+        size *= radices[stage]
 
     codes = call(encode_kernel, shape((rows, width), half), (*blocks, w_enc, b_enc, threshold), work)
     before = onward(codes)
     own = call(decode_kernel, shape((rows, depth), full), (codes, dec_self), work)
 
-    size = rows // steps[0][1]
-    parts = call(join_kernel, (shape((size, depth), half),) * steps[0][1], (own, before, arrived_dec), work)
-    for at, (stride, radix) in enumerate(steps):
-        blocks = [parts[0]] + [swap(parts[j], stride * j) for j in reversed(range(1, radix))]
-        if at < len(steps) - 1:
-            following = steps[at + 1][1]
-            size //= following
+    size = rows // radices[0]
+    kernel = functools.partial(join_kernel, places)
+    parts = call(kernel, (shape((size, depth), half),) * radices[0], (own, before, arrived_dec), work)
+    for stage, radix in enumerate(radices):
+        blocks = [parts[0]] + [swap(parts[j], stage, j) for j in reversed(range(1, radix))]
+        if stage < last:
+            size //= radices[stage + 1]
             kernel = functools.partial(split_kernel, radix)
-            parts = call(kernel, (shape((size, depth), half),) * following, blocks)
+            parts = call(kernel, (shape((size, depth), half),) * radices[stage + 1], blocks)
     return call(finish_kernel, shape(target.shape, full), (*blocks, target))
 
 

time: 34.6 us -> 33.6 us (0.971)
  waiting for transfers between devices: 13.4 us -> 12.4 us
    ppermute x12, waiting for transfers between devices: 12.9 us -> 11.9 us  [swap(): return lax.ppermute(value, ('layer', 'feat'), pairs)]
  transfers between devices with their start and end apart: 14 -> 14, of which waited for: 11 -> 11; matrix products, arithmetic and copies ran while one was open for 0% -> 0% of each run, Pallas kernels for 6% -> 7%
where the time goes in v5:
time: 33.6 us; the launch traced here: 33.4 us
  starting transfers between devices  17.2 us (51%)
  waiting for transfers between devices  12.4 us (37%)
  Pallas kernels  2.9 us (9%)
  local copies, waits for them, and re-layouts  0.81 us (2%)
    ppermute x12, starting transfers between devices, swap(): return lax.ppermute(value, ('layer', 'feat'), pairs)  17.2 us
    ppermute x12, waiting for transfers between devices, swap(): return lax.ppermute(value, ('layer', 'feat'), pairs)  11.9 us
    pallas_call x7, Pallas kernels, call(): pl.pallas_call(kernel, out_shape=out_shape, in_specs=[VMEM] * len(args),...  2.9 us
    unnamed x12, local copies, waits for them, and re-layouts  0.81 us
  transfers between devices with their start and end apart: 14, of which 11 were waited for; matrix products, arithmetic and copies ran while one was open for 0% of the time, Pallas kernels for 7%

profile of v5, /device:TPU:0, one launch (start us, length us, event | category | flops | bytes accessed | tf_op | source)
XLA Modules:
  0.0 33.4 jit_solution(12882131124036388745)
XLA Ops:
  0.0 5.0 %collective-permute-start = (f32[1,4,2048]{2,1,0:T(4,128)}, f32[1,4,2048]{2,1,0:T(4,128)S(1)}, u32[]{:S(2)}, u32[]{:S(2)}) collective-permute-start(f32[1,4,2048]{2,1,0:T(4,128)} %rows_ref.1), channel_id=1, source_target_pairs={{0,12},{1,13},{2,14},{3,15},{4,8},{5,9},{6,10},{7,11},{8,4},{9,5},... | collective-permute-start | bytes 98312 | tf_op jit(solution)/shard_map/ppermute | solution.py:133
  5.1 0.6 %collective-permute-start.1 = (f32[1,4,2048]{2,1,0:T(4,128)}, f32[1,4,2048]{2,1,0:T(4,128)S(1)}, u32[]{:S(2)}, u32[]{:S(2)}) collective-permute-start(f32[1,4,2048]{2,1,0:T(4,128)} %rows_ref.1), channel_id=1, source_target_pairs={{0,4},{1,5},{2,6},{3,7},{4,0},{5,1},{6,2},{7,3},{8,12},{9,13},{10,... | collective-permute-start | bytes 98312 | tf_op jit(solution)/shard_map/ppermute | solution.py:133
  5.6 0.8 %copy-done.5 = f32[1,4,2048]{2,1,0:T(4,128)S(1)} copy-done((f32[1,4,2048]{2,1,0:T(4,128)S(1)}, f32[1,4,2048]{2,1,0:T(4,128)}, u32[]{:S(2)}) %copy-start.5) | copy-done | bytes 32792
  6.5 0.6 %collective-permute-done.refs_0_ = f32[1,4,2048]{2,1,0:T(4,128)S(1)} collective-permute-done((f32[1,4,2048]{2,1,0:T(4,128)}, f32[1,4,2048]{2,1,0:T(4,128)S(1)}, u32[]{:S(2)}, u32[]{:S(2)}) %collective-permute-start) | collective-permute-done | bytes 32800 | tf_op jit(solution)/shard_map/ppermute | solution.py:133
  7.2 2.9 %collective-permute-done.2.refs_2_ = f32[1,4,2048]{2,1,0:T(4,128)S(1)} collective-permute-done((f32[1,4,2048]{2,1,0:T(4,128)}, f32[1,4,2048]{2,1,0:T(4,128)S(1)}, u32[]{:S(2)}, u32[]{:S(2)}) %collective-permute-start.2) | collective-permute-done | bytes 32800 | tf_op jit(solution)/shard_map/ppermute | solution.py:133
  10.2 2.5 %collective-permute-start.5 = (bf16[16,2048]{1,0:T(8,128)(2,1)S(1)}, bf16[16,2048]{1,0:T(8,128)(2,1)S(1)}, u32[]{:S(2)}, u32[]{:S(2)}) collective-permute-start(bf16[16,2048]{1,0:T(8,128)(2,1)S(1)} %shard_map.74.refs_0_), channel_id=1, source_target_pairs={{0,3},{1,2},{2,1},{3,0},{4,7},{5,6},{6,5},{7,4},{8,11},{9,10},{10,... | collective-permute-start | bytes 196616 | tf_op jit(solution)/shard_map/ppermute | solution.py:133
  12.7 0.5 %collective-permute-start.4 = (bf16[16,2048]{1,0:T(8,128)(2,1)S(1)}, bf16[16,2048]{1,0:T(8,128)(2,1)S(1)}, u32[]{:S(2)}, u32[]{:S(2)}) collective-permute-start(bf16[16,2048]{1,0:T(8,128)(2,1)S(1)} %shard_map.74.refs_0_), channel_id=1, source_target_pairs={{0,2},{1,3},{2,0},{3,1},{4,6},{5,7},{6,4},{7,5},{8,10},{9,11},{10,... | collective-permute-start | bytes 196616 | tf_op jit(solution)/shard_map/ppermute | solution.py:133
  13.2 0.5 %collective-permute-start.3 = (bf16[16,2048]{1,0:T(8,128)(2,1)S(1)}, bf16[16,2048]{1,0:T(8,128)(2,1)S(1)}, u32[]{:S(2)}, u32[]{:S(2)}) collective-permute-start(bf16[16,2048]{1,0:T(8,128)(2,1)S(1)} %shard_map.74.refs_0_), channel_id=1, source_target_pairs={{0,1},{1,0},{2,3},{3,2},{4,5},{5,4},{6,7},{7,6},{8,9},{9,8},{10,11... | collective-permute-start | bytes 196616 | tf_op jit(solution)/shard_map/ppermute | solution.py:133
  13.8 1.7 %collective-permute-done.5.refs_3_ = bf16[16,2048]{1,0:T(8,128)(2,1)S(1)} collective-permute-done((bf16[16,2048]{1,0:T(8,128)(2,1)S(1)}, bf16[16,2048]{1,0:T(8,128)(2,1)S(1)}, u32[]{:S(2)}, u32[]{:S(2)}) %collective-permute-start.5) | collective-permute-done | bytes 65568 | tf_op jit(solution)/shard_map/ppermute | solution.py:133
  15.4 1.5 %collective-permute-done.4.refs_2_ = bf16[16,2048]{1,0:T(8,128)(2,1)S(1)} collective-permute-done((bf16[16,2048]{1,0:T(8,128)(2,1)S(1)}, bf16[16,2048]{1,0:T(8,128)(2,1)S(1)}, u32[]{:S(2)}, u32[]{:S(2)}) %collective-permute-start.4) | collective-permute-done | bytes 65568 | tf_op jit(solution)/shard_map/ppermute | solution.py:133
  17.0 0.5 %collective-permute-done.3.refs_1_ = bf16[16,2048]{1,0:T(8,128)(2,1)S(1)} collective-permute-done((bf16[16,2048]{1,0:T(8,128)(2,1)S(1)}, bf16[16,2048]{1,0:T(8,128)(2,1)S(1)}, u32[]{:S(2)}, u32[]{:S(2)}) %collective-permute-start.3) | collective-permute-done | bytes 65568 | tf_op jit(solution)/shard_map/ppermute | solution.py:133
  17.5 1.0 %shard_map.75.codes_ref = bf16[64,1536]{1,0:T(8,128)(2,1)S(1)} custom-call(bf16[16,2048]{1,0:T(8,128)(2,1)S(1)} %shard_map.74.refs_0_, bf16[16,2048]{1,0:T(8,128)(2,1)S(1)} %collective-permute-done.3.refs_1_, bf16[16,2048]{1,0:T(8,128)(2,1)S(1)} %collective-permute-done.4.refs_2_, bf16[16,2048]{1,0:T(8,128)(2,1)S(1)} %collective-permute-done.5.refs_3_, ...), custom_call_target="tpu_custom_call" | custom-call | flops 402653184 | bytes 262144 | tf_op jit(solution)/shard_map/pallas_call | solution.py:18
  18.6 1.0 %shard_map.76.own_ref = f32[64,2048]{1,0:T(8,128)S(1)} custom-call(bf16[64,1536]{1,0:T(8,128)(2,1)S(1)} %shard_map.75.codes_ref, bf16[1,1536,2048]{2,1,0:T(8,128)(2,1)S(1)} %copy-done.1), custom_call_target="tpu_custom_call" | custom-call | flops 402653184 | bytes 262144 | tf_op jit(solution)/shard_map/pallas_call | solution.py:18
  20.1 1.6 %collective-permute-start.8 = (bf16[16,2048]{1,0:T(8,128)(2,1)S(1)}, bf16[16,2048]{1,0:T(8,128)(2,1)S(1)}, u32[]{:S(2)}, u32[]{:S(2)}) collective-permute-start(bf16[16,2048]{1,0:T(8,128)(2,1)S(1)} %get-tuple-element.14), channel_id=1, source_target_pairs={{0,3},{1,2},{2,1},{3,0},{4,7},{5,6},{6,5},{7,4},{8,11},{9,10},{10,... | collective-permute-start | bytes 196616 | tf_op jit(solution)/shard_map/ppermute | solution.py:133
  21.6 0.5 %collective-permute-start.9 = (bf16[16,2048]{1,0:T(8,128)(2,1)S(1)}, bf16[16,2048]{1,0:T(8,128)(2,1)S(1)}, u32[]{:S(2)}, u32[]{:S(2)}) collective-permute-start(bf16[16,2048]{1,0:T(8,128)(2,1)S(1)} %get-tuple-element.15), channel_id=1, source_target_pairs={{0,2},{1,3},{2,0},{3,1},{4,6},{5,7},{6,4},{7,5},{8,10},{9,11},{10,... | collective-permute-start | bytes 196616 | tf_op jit(solution)/shard_map/ppermute | solution.py:133
  22.1 1.5 %collective-permute-start.10 = (bf16[16,2048]{1,0:T(8,128)(2,1)S(1)}, bf16[16,2048]{1,0:T(8,128)(2,1)S(1)}, u32[]{:S(2)}, u32[]{:S(2)}) collective-permute-start(bf16[16,2048]{1,0:T(8,128)(2,1)S(1)} %get-tuple-element.16), channel_id=1, source_target_pairs={{0,1},{1,0},{2,3},{3,2},{4,5},{5,4},{6,7},{7,6},{8,9},{9,8},{10,11... | collective-permute-start | bytes 196616 | tf_op jit(solution)/shard_map/ppermute | solution.py:133
  23.6 1.7 %collective-permute-done.8.refs_1_ = bf16[16,2048]{1,0:T(8,128)(2,1)S(1)} collective-permute-done((bf16[16,2048]{1,0:T(8,128)(2,1)S(1)}, bf16[16,2048]{1,0:T(8,128)(2,1)S(1)}, u32[]{:S(2)}, u32[]{:S(2)}) %collective-permute-start.8) | collective-permute-done | bytes 65568 | tf_op jit(solution)/shard_map/ppermute | solution.py:133
  25.3 0.7 %collective-permute-done.9.refs_2_ = bf16[16,2048]{1,0:T(8,128)(2,1)S(1)} collective-permute-done((bf16[16,2048]{1,0:T(8,128)(2,1)S(1)}, bf16[16,2048]{1,0:T(8,128)(2,1)S(1)}, u32[]{:S(2)}, u32[]{:S(2)}) %collective-permute-start.9) | collective-permute-done | bytes 65568 | tf_op jit(solution)/shard_map/ppermute | solution.py:133
  26.4 1.6 %collective-permute-start.11 = (bf16[4,2048]{1,0:T(4,128)(2,1)S(1)}, bf16[4,2048]{1,0:T(4,128)(2,1)S(1)}, u32[]{:S(2)}, u32[]{:S(2)}) collective-permute-start(bf16[4,2048]{1,0:T(4,128)(2,1)S(1)} %get-tuple-element.18), channel_id=1, source_target_pairs={{0,12},{1,13},{2,14},{3,15},{4,8},{5,9},{6,10},{7,11},{8,4},{9,5},... | collective-permute-start | bytes 49160 | tf_op jit(solution)/shard_map/ppermute | solution.py:133
  28.0 0.6 %collective-permute-start.12 = (bf16[4,2048]{1,0:T(4,128)(2,1)S(1)}, bf16[4,2048]{1,0:T(4,128)(2,1)S(1)}, u32[]{:S(2)}, u32[]{:S(2)}) collective-permute-start(bf16[4,2048]{1,0:T(4,128)(2,1)S(1)} %get-tuple-element.19), channel_id=1, source_target_pairs={{0,8},{1,9},{2,10},{3,11},{4,12},{5,13},{6,14},{7,15},{8,0},{9,1},... | collective-permute-start | bytes 49160 | tf_op jit(solution)/shard_map/ppermute | solution.py:133
  28.6 2.3 %collective-permute-start.13 = (bf16[4,2048]{1,0:T(4,128)(2,1)S(1)}, bf16[4,2048]{1,0:T(4,128)(2,1)S(1)}, u32[]{:S(2)}, u32[]{:S(2)}) collective-permute-start(bf16[4,2048]{1,0:T(4,128)(2,1)S(1)} %get-tuple-element.20), channel_id=1, source_target_pairs={{0,4},{1,5},{2,6},{3,7},{4,0},{5,1},{6,2},{7,3},{8,12},{9,13},{10,... | collective-permute-start | bytes 49160 | tf_op jit(solution)/shard_map/ppermute | solution.py:133
  30.9 1.1 %collective-permute-done.11.refs_1_ = bf16[4,2048]{1,0:T(4,128)(2,1)S(1)} collective-permute-done((bf16[4,2048]{1,0:T(4,128)(2,1)S(1)}, bf16[4,2048]{1,0:T(4,128)(2,1)S(1)}, u32[]{:S(2)}, u32[]{:S(2)}) %collective-permute-start.11) | collective-permute-done | bytes 16416 | tf_op jit(solution)/shard_map/ppermute | solution.py:133
  32.1 0.7 %collective-permute-done.12.refs_2_ = bf16[4,2048]{1,0:T(4,128)(2,1)S(1)} collective-permute-done((bf16[4,2048]{1,0:T(4,128)(2,1)S(1)}, bf16[4,2048]{1,0:T(4,128)(2,1)S(1)}, u32[]{:S(2)}, u32[]{:S(2)}) %collective-permute-start.12) | collective-permute-done | bytes 16416 | tf_op jit(solution)/shard_map/ppermute | solution.py:133
  32.8 0.6 %shard_map.79 = f32[1,4,2048]{2,1,0:T(4,128)} custom-call(bf16[4,2048]{1,0:T(4,128)(2,1)S(1)} %get-tuple-element.17.refs_0_, bf16[4,2048]{1,0:T(4,128)(2,1)S(1)} %collective-permute-done.11.refs_1_, bf16[4,2048]{1,0:T(4,128)(2,1)S(1)} %collective-permute-done.12.refs_2_, bf16[4,2048]{1,0:T(4,128)(2,1)S(1)} %collective-permute-done.13.refs_3_, ...), custom_call_target="tpu_custom_call" | custom-call | bytes 262144 | tf_op jit(solution)/shard_map/pallas_call | solution.py:18
  (23 shorter events, 1.3 us)
Async XLA Ops:
  0.0 7.2 %collective-permute-start = (f32[1,4,2048]{2,1,0:T(4,128)}, f32[1,4,2048]{2,1,0:T(4,128)S(1)}, u32[]{:S(2)}, u32[]{:S(2)}) collective-permute-start(f32[1,4,2048]{2,1,0:T(4,128)} %rows_ref.1), channel_id=1, source_target_pairs={{0,12},{1,13},{2,14},{3,15},{4,8},{5,9},{6,10},{7,11},{8,4},{9,5},... | collective-permute-start | bytes 98312 | tf_op jit(solution)/shard_map/ppermute | solution.py:133
  5.0 5.0 %collective-permute-start.2 = (f32[1,4,2048]{2,1,0:T(4,128)}, f32[1,4,2048]{2,1,0:T(4,128)S(1)}, u32[]{:S(2)}, u32[]{:S(2)}) collective-permute-start(f32[1,4,2048]{2,1,0:T(4,128)} %rows_ref.1), channel_id=1, source_target_pairs={{0,8},{1,9},{2,10},{3,11},{4,12},{5,13},{6,14},{7,15},{8,0},{9,1},... | collective-permute-start | bytes 98312 | tf_op jit(solution)/shard_map/ppermute | solution.py:133
  5.1 5.0 %collective-permute-start.1 = (f32[1,4,2048]{2,1,0:T(4,128)}, f32[1,4,2048]{2,1,0:T(4,128)S(1)}, u32[]{:S(2)}, u32[]{:S(2)}) collective-permute-start(f32[1,4,2048]{2,1,0:T(4,128)} %rows_ref.1), channel_id=1, source_target_pairs={{0,4},{1,5},{2,6},{3,7},{4,0},{5,1},{6,2},{7,3},{8,12},{9,13},{10,... | collective-permute-start | bytes 98312 | tf_op jit(solution)/shard_map/ppermute | solution.py:133
  5.6 14.4 %collective-permute-start.7 = (bf16[1,1536,2048]{2,1,0:T(8,128)(2,1)}, bf16[1,1536,2048]{2,1,0:T(8,128)(2,1)S(1)}, u32[]{:S(2)}, u32[]{:S(2)}) collective-permute-start(bf16[1,1536,2048]{2,1,0:T(8,128)(2,1)} %param.12), channel_id=1, source_target_pairs={{0,16},{16,0},{1,17},{17,1},{2,18},{18,2},{3,19},{19,3},{4,20},{20... | collective-permute-start | bytes 18874376 | tf_op jit(solution)/shard_map/ppermute | solution.py:136
  5.6 0.8 %copy-start.5 = (f32[1,4,2048]{2,1,0:T(4,128)S(1)}, f32[1,4,2048]{2,1,0:T(4,128)}, u32[]{:S(2)}) copy-start(f32[1,4,2048]{2,1,0:T(4,128)} %rows_ref.1) | copy-start | bytes 98308
  6.5 11.0 %copy-start = (bf16[1,2048,1536]{2,1,0:T(8,128)(2,1)S(1)}, bf16[1,2048,1536]{2,1,0:T(8,128)(2,1)}, u32[]{:S(2)}) copy-start(bf16[1,2048,1536]{2,1,0:T(8,128)(2,1)} %refs_4_.2) | copy-start | bytes 18874372
  6.5 11.0 %copy-start.3 = (f32[1,1536]{1,0:T(1,128)S(1)}, f32[1,1536]{1,0:T(1,128)}, u32[]{:S(2)}) copy-start(f32[1,1536]{1,0:T(1,128)} %refs_5_.1) | copy-start | bytes 18436
  6.5 11.0 %copy-start.4 = (f32[1,1536]{1,0:T(1,128)S(1)}, f32[1,1536]{1,0:T(1,128)}, u32[]{:S(2)}) copy-start(f32[1,1536]{1,0:T(1,128)} %refs_6_.1) | copy-start | bytes 18436
  10.2 8.4 %copy-start.1 = (bf16[1,1536,2048]{2,1,0:T(8,128)(2,1)S(1)}, bf16[1,1536,2048]{2,1,0:T(8,128)(2,1)}, u32[]{:S(2)}) copy-start(bf16[1,1536,2048]{2,1,0:T(8,128)(2,1)} %dec_ref.1) | copy-start | bytes 18874372
  10.2 5.2 %collective-permute-start.5 = (bf16[16,2048]{1,0:T(8,128)(2,1)S(1)}, bf16[16,2048]{1,0:T(8,128)(2,1)S(1)}, u32[]{:S(2)}, u32[]{:S(2)}) collective-permute-start(bf16[16,2048]{1,0:T(8,128)(2,1)S(1)} %shard_map.74.refs_0_), channel_id=1, source_target_pairs={{0,3},{1,2},{2,1},{3,0},{4,7},{5,6},{6,5},{7,4},{8,11},{9,10},{10,... | collective-permute-start | bytes 196616 | tf_op jit(solution)/shard_map/ppermute | solution.py:133
  12.7 4.3 %collective-permute-start.4 = (bf16[16,2048]{1,0:T(8,128)(2,1)S(1)}, bf16[16,2048]{1,0:T(8,128)(2,1)S(1)}, u32[]{:S(2)}, u32[]{:S(2)}) collective-permute-start(bf16[16,2048]{1,0:T(8,128)(2,1)S(1)} %shard_map.74.refs_0_), channel_id=1, source_target_pairs={{0,2},{1,3},{2,0},{3,1},{4,6},{5,7},{6,4},{7,5},{8,10},{9,11},{10,... | collective-permute-start | bytes 196616 | tf_op jit(solution)/shard_map/ppermute | solution.py:133
  13.2 4.3 %collective-permute-start.3 = (bf16[16,2048]{1,0:T(8,128)(2,1)S(1)}, bf16[16,2048]{1,0:T(8,128)(2,1)S(1)}, u32[]{:S(2)}, u32[]{:S(2)}) collective-permute-start(bf16[16,2048]{1,0:T(8,128)(2,1)S(1)} %shard_map.74.refs_0_), channel_id=1, source_target_pairs={{0,1},{1,0},{2,3},{3,2},{4,5},{5,4},{6,7},{7,6},{8,9},{9,8},{10,11... | collective-permute-start | bytes 196616 | tf_op jit(solution)/shard_map/ppermute | solution.py:133
  18.5 14.3 %copy-start.2 = (f32[1,4,2048]{2,1,0:T(4,128)S(1)}, f32[1,4,2048]{2,1,0:T(4,128)}, u32[]{:S(2)}) copy-start(f32[1,4,2048]{2,1,0:T(4,128)} %refs_4_.3) | copy-start | bytes 98308
  18.5 1.5 %collective-permute-start.6 = (bf16[64,1536]{1,0:T(8,128)(2,1)S(1)}, bf16[64,1536]{1,0:T(8,128)(2,1)S(1)}, u32[]{:S(2)}, u32[]{:S(2)}) collective-permute-start(bf16[64,1536]{1,0:T(8,128)(2,1)S(1)} %shard_map.75.codes_ref), channel_id=1, source_target_pairs={{0,16},{16,0},{1,17},{17,1},{2,18},{18,2},{3,19},{19,3},{4,20},{20... | collective-permute-start | bytes 589832 | tf_op jit(solution)/shard_map/ppermute | solution.py:136
  20.1 5.2 %collective-permute-start.8 = (bf16[16,2048]{1,0:T(8,128)(2,1)S(1)}, bf16[16,2048]{1,0:T(8,128)(2,1)S(1)}, u32[]{:S(2)}, u32[]{:S(2)}) collective-permute-start(bf16[16,2048]{1,0:T(8,128)(2,1)S(1)} %get-tuple-element.14), channel_id=1, source_target_pairs={{0,3},{1,2},{2,1},{3,0},{4,7},{5,6},{6,5},{7,4},{8,11},{9,10},{10,... | collective-permute-start | bytes 196616 | tf_op jit(solution)/shard_map/ppermute | solution.py:133
  21.6 4.4 %collective-permute-start.9 = (bf16[16,2048]{1,0:T(8,128)(2,1)S(1)}, bf16[16,2048]{1,0:T(8,128)(2,1)S(1)}, u32[]{:S(2)}, u32[]{:S(2)}) collective-permute-start(bf16[16,2048]{1,0:T(8,128)(2,1)S(1)} %get-tuple-element.15), channel_id=1, source_target_pairs={{0,2},{1,3},{2,0},{3,1},{4,6},{5,7},{6,4},{7,5},{8,10},{9,11},{10,... | collective-permute-start | bytes 196616 | tf_op jit(solution)/shard_map/ppermute | solution.py:133
  22.1 4.3 %collective-permute-start.10 = (bf16[16,2048]{1,0:T(8,128)(2,1)S(1)}, bf16[16,2048]{1,0:T(8,128)(2,1)S(1)}, u32[]{:S(2)}, u32[]{:S(2)}) collective-permute-start(bf16[16,2048]{1,0:T(8,128)(2,1)S(1)} %get-tuple-element.16), channel_id=1, source_target_pairs={{0,1},{1,0},{2,3},{3,2},{4,5},{5,4},{6,7},{7,6},{8,9},{9,8},{10,11... | collective-permute-start | bytes 196616 | tf_op jit(solution)/shard_map/ppermute | solution.py:133
  26.4 5.6 %collective-permute-start.11 = (bf16[4,2048]{1,0:T(4,128)(2,1)S(1)}, bf16[4,2048]{1,0:T(4,128)(2,1)S(1)}, u32[]{:S(2)}, u32[]{:S(2)}) collective-permute-start(bf16[4,2048]{1,0:T(4,128)(2,1)S(1)} %get-tuple-element.18), channel_id=1, source_target_pairs={{0,12},{1,13},{2,14},{3,15},{4,8},{5,9},{6,10},{7,11},{8,4},{9,5},... | collective-permute-start | bytes 49160 | tf_op jit(solution)/shard_map/ppermute | solution.py:133
  28.0 4.7 %collective-permute-start.12 = (bf16[4,2048]{1,0:T(4,128)(2,1)S(1)}, bf16[4,2048]{1,0:T(4,128)(2,1)S(1)}, u32[]{:S(2)}, u32[]{:S(2)}) collective-permute-start(bf16[4,2048]{1,0:T(4,128)(2,1)S(1)} %get-tuple-element.19), channel_id=1, source_target_pairs={{0,8},{1,9},{2,10},{3,11},{4,12},{5,13},{6,14},{7,15},{8,0},{9,1},... | collective-permute-start | bytes 49160 | tf_op jit(solution)/shard_map/ppermute | solution.py:133
  28.6 4.2 %collective-permute-start.13 = (bf16[4,2048]{1,0:T(4,128)(2,1)S(1)}, bf16[4,2048]{1,0:T(4,128)(2,1)S(1)}, u32[]{:S(2)}, u32[]{:S(2)}) collective-permute-start(bf16[4,2048]{1,0:T(4,128)(2,1)S(1)} %get-tuple-element.20), channel_id=1, source_target_pairs={{0,4},{1,5},{2,6},{3,7},{4,0},{5,1},{6,2},{7,3},{8,12},{9,13},{10,... | collective-permute-start | bytes 49160 | tf_op jit(solution)/shard_map/ppermute | solution.py:133

commit v6 on v5

--- a/solution.py
+++ b/solution.py
@@ -14,10 +14,11 @@
 TALL = 128
 
 
-def call(kernel, out_shape, args, flops=0, moved=2**18):
+def call(kernel, out_shape, args, flops=0, moved=2**18, aliases=()):
     return pl.pallas_call(
         kernel,
         out_shape=out_shape,
+        input_output_aliases=dict(aliases),
         in_specs=[VMEM] * len(args),
         out_specs=jax.tree.map(lambda _: VMEM, out_shape),
         compiler_params=pltpu.CompilerParams(vmem_limit_bytes=GRANT),
@@ -60,8 +61,10 @@
     codes_ref[...] = (pre * jax.nn.sigmoid((pre - limit_ref[...]) / 0.1)).astype(jnp.bfloat16)
 
 
-def decode_kernel(codes_ref, dec_ref, own_ref):
-    own_ref[...] = dot(codes_ref[...], dec_ref[0])
+def decode_kernel(codes_ref, dec_ref, own_ref, *part_refs):
+    own = dot(codes_ref[...], dec_ref[0])
+    own_ref[...] = own
+    cut(own, part_refs)
 
 
 def cut(total, part_refs):
@@ -70,14 +73,10 @@
         part_ref[...] = total[i * size : (i + 1) * size].astype(jnp.bfloat16)
 
 
-def join_kernel(places, own_ref, before_ref, dec_ref, *part_refs):
-    first = lax.axis_index("layer") == 0
+def join_kernel(places, own_ref, before_ref, dec_ref, *refs):
+    part_refs = refs[len(refs) // 2 :]
 
-    @pl.when(first)
-    def _():
-        cut(own_ref[...], part_refs)
-
-    @pl.when(jnp.logical_not(first))
+    @pl.when(lax.axis_index("layer") > 0)
     def _():
         carried = dot(before_ref[...], dec_ref[0])
         block = carried.shape[0] // len(places)
@@ -87,6 +86,16 @@
 
 def added(block_refs):
     return sum(ref[...].astype(jnp.float32) for ref in block_refs)
+
+
+def gather_up_kernel(*refs):
+    *block_refs, out_ref = refs
+    out_ref[...] = added(block_refs)
+
+
+def add_kernel(*refs):
+    *block_refs, out_ref = refs
+    out_ref[...] = added(block_refs)
 
 
 def split_kernel(count, *refs):
@@ -152,16 +161,20 @@
 
     codes = call(encode_kernel, shape((rows, width), half), (*blocks, w_enc, b_enc, threshold), work)
     before = onward(codes)
-    own = call(decode_kernel, shape((rows, depth), full), (codes, dec_self), work)
-
     size = rows // radices[0]
+    pieces = (shape((size, depth), half),) * radices[0]
+    own, *parts = call(decode_kernel, (shape((rows, depth), full), *pieces), (codes, dec_self), work)
     kernel = functools.partial(join_kernel, places)
-    parts = call(kernel, (shape((size, depth), half),) * radices[0], (own, before, arrived_dec), work)
+    operands = (own, before, arrived_dec, *parts)
+    parts = call(kernel, pieces, operands, work, aliases=[(3 + i, i) for i in range(radices[0])])
     for stage, radix in enumerate(radices):
         blocks = [parts[0]] + [swap(parts[j], stage, j) for j in reversed(range(1, radix))]
+        if len(blocks) > 2:
+            sofar = call(add_kernel, shape(parts[0].shape, full), blocks[:2])
+            blocks = [sofar] + blocks[2:]
         if stage < last:
             size //= radices[stage + 1]
-            kernel = functools.partial(split_kernel, radix)
+            kernel = functools.partial(split_kernel, len(blocks))
             parts = call(kernel, (shape((size, depth), half),) * radices[stage + 1], blocks)
     return call(finish_kernel, shape(target.shape, full), (*blocks, target))
 

time: 33.6 us -> 33.5 us (level)
    pallas_call x7 -> x9, Pallas kernels: 2.9 us -> 2.89 us  [call(): pl.pallas_call(kernel, out_shape=out_shape, input_output_aliases=dict(ali...]
where the time goes in v6:
time: 33.5 us; the launch traced here: 33.3 us
  starting transfers between devices  17.2 us (51%)
  waiting for transfers between devices  12.3 us (37%)
  Pallas kernels  2.89 us (9%)
  local copies, waits for them, and re-layouts  0.81 us (2%)
    ppermute x12, starting transfers between devices, swap(): return lax.ppermute(value, ('layer', 'feat'), pairs)  17.1 us
    ppermute x12, waiting for transfers between devices, swap(): return lax.ppermute(value, ('layer', 'feat'), pairs)  11.9 us
    pallas_call x9, Pallas kernels, call(): pl.pallas_call(kernel, out_shape=out_shape, input_output_aliases=dict(ali...  2.89 us
    unnamed x12, local copies, waits for them, and re-layouts  0.81 us
  transfers between devices with their start and end apart: 14, of which 11 were waited for; matrix products, arithmetic and copies ran while one was open for 0% of the time, Pallas kernels for 7%

profile of v6, /device:TPU:0, one launch (start us, length us, event | category | flops | bytes accessed | tf_op | source)
XLA Modules:
  0.0 33.3 jit_solution(2626324498171334785)
XLA Ops:
  0.0 5.0 %collective-permute-start = (f32[1,4,2048]{2,1,0:T(4,128)}, f32[1,4,2048]{2,1,0:T(4,128)S(1)}, u32[]{:S(2)}, u32[]{:S(2)}) collective-permute-start(f32[1,4,2048]{2,1,0:T(4,128)} %rows_ref.1), channel_id=1, source_target_pairs={{0,12},{1,13},{2,14},{3,15},{4,8},{5,9},{6,10},{7,11},{8,4},{9,5},... | collective-permute-start | bytes 98312 | tf_op jit(solution)/shard_map/ppermute | solution.py:142
  5.1 0.6 %collective-permute-start.1 = (f32[1,4,2048]{2,1,0:T(4,128)}, f32[1,4,2048]{2,1,0:T(4,128)S(1)}, u32[]{:S(2)}, u32[]{:S(2)}) collective-permute-start(f32[1,4,2048]{2,1,0:T(4,128)} %rows_ref.1), channel_id=1, source_target_pairs={{0,4},{1,5},{2,6},{3,7},{4,0},{5,1},{6,2},{7,3},{8,12},{9,13},{10,... | collective-permute-start | bytes 98312 | tf_op jit(solution)/shard_map/ppermute | solution.py:142
  5.6 0.8 %copy-done.5 = f32[1,4,2048]{2,1,0:T(4,128)S(1)} copy-done((f32[1,4,2048]{2,1,0:T(4,128)S(1)}, f32[1,4,2048]{2,1,0:T(4,128)}, u32[]{:S(2)}) %copy-start.5) | copy-done | bytes 32792
  6.5 0.6 %collective-permute-done.refs_0_ = f32[1,4,2048]{2,1,0:T(4,128)S(1)} collective-permute-done((f32[1,4,2048]{2,1,0:T(4,128)}, f32[1,4,2048]{2,1,0:T(4,128)S(1)}, u32[]{:S(2)}, u32[]{:S(2)}) %collective-permute-start) | collective-permute-done | bytes 32800 | tf_op jit(solution)/shard_map/ppermute | solution.py:142
  7.2 2.9 %collective-permute-done.2.refs_2_ = f32[1,4,2048]{2,1,0:T(4,128)S(1)} collective-permute-done((f32[1,4,2048]{2,1,0:T(4,128)}, f32[1,4,2048]{2,1,0:T(4,128)S(1)}, u32[]{:S(2)}, u32[]{:S(2)}) %collective-permute-start.2) | collective-permute-done | bytes 32800 | tf_op jit(solution)/shard_map/ppermute | solution.py:142
  10.2 2.5 %collective-permute-start.5 = (bf16[16,2048]{1,0:T(8,128)(2,1)S(1)}, bf16[16,2048]{1,0:T(8,128)(2,1)S(1)}, u32[]{:S(2)}, u32[]{:S(2)}) collective-permute-start(bf16[16,2048]{1,0:T(8,128)(2,1)S(1)} %shard_map.74.refs_0_), channel_id=1, source_target_pairs={{0,3},{1,2},{2,1},{3,0},{4,7},{5,6},{6,5},{7,4},{8,11},{9,10},{10,... | collective-permute-start | bytes 196616 | tf_op jit(solution)/shard_map/ppermute | solution.py:142
  12.7 0.5 %collective-permute-start.4 = (bf16[16,2048]{1,0:T(8,128)(2,1)S(1)}, bf16[16,2048]{1,0:T(8,128)(2,1)S(1)}, u32[]{:S(2)}, u32[]{:S(2)}) collective-permute-start(bf16[16,2048]{1,0:T(8,128)(2,1)S(1)} %shard_map.74.refs_0_), channel_id=1, source_target_pairs={{0,2},{1,3},{2,0},{3,1},{4,6},{5,7},{6,4},{7,5},{8,10},{9,11},{10,... | collective-permute-start | bytes 196616 | tf_op jit(solution)/shard_map/ppermute | solution.py:142
  13.2 0.5 %collective-permute-start.3 = (bf16[16,2048]{1,0:T(8,128)(2,1)S(1)}, bf16[16,2048]{1,0:T(8,128)(2,1)S(1)}, u32[]{:S(2)}, u32[]{:S(2)}) collective-permute-start(bf16[16,2048]{1,0:T(8,128)(2,1)S(1)} %shard_map.74.refs_0_), channel_id=1, source_target_pairs={{0,1},{1,0},{2,3},{3,2},{4,5},{5,4},{6,7},{7,6},{8,9},{9,8},{10,11... | collective-permute-start | bytes 196616 | tf_op jit(solution)/shard_map/ppermute | solution.py:142
  13.8 1.7 %collective-permute-done.5.refs_3_ = bf16[16,2048]{1,0:T(8,128)(2,1)S(1)} collective-permute-done((bf16[16,2048]{1,0:T(8,128)(2,1)S(1)}, bf16[16,2048]{1,0:T(8,128)(2,1)S(1)}, u32[]{:S(2)}, u32[]{:S(2)}) %collective-permute-start.5) | collective-permute-done | bytes 65568 | tf_op jit(solution)/shard_map/ppermute | solution.py:142
  15.4 1.5 %collective-permute-done.4.refs_2_ = bf16[16,2048]{1,0:T(8,128)(2,1)S(1)} collective-permute-done((bf16[16,2048]{1,0:T(8,128)(2,1)S(1)}, bf16[16,2048]{1,0:T(8,128)(2,1)S(1)}, u32[]{:S(2)}, u32[]{:S(2)}) %collective-permute-start.4) | collective-permute-done | bytes 65568 | tf_op jit(solution)/shard_map/ppermute | solution.py:142
  17.0 0.5 %collective-permute-done.3.refs_1_ = bf16[16,2048]{1,0:T(8,128)(2,1)S(1)} collective-permute-done((bf16[16,2048]{1,0:T(8,128)(2,1)S(1)}, bf16[16,2048]{1,0:T(8,128)(2,1)S(1)}, u32[]{:S(2)}, u32[]{:S(2)}) %collective-permute-start.3) | collective-permute-done | bytes 65568 | tf_op jit(solution)/shard_map/ppermute | solution.py:142
  17.5 1.0 %shard_map.75.codes_ref = bf16[64,1536]{1,0:T(8,128)(2,1)S(1)} custom-call(bf16[16,2048]{1,0:T(8,128)(2,1)S(1)} %shard_map.74.refs_0_, bf16[16,2048]{1,0:T(8,128)(2,1)S(1)} %collective-permute-done.3.refs_1_, bf16[16,2048]{1,0:T(8,128)(2,1)S(1)} %collective-permute-done.4.refs_2_, bf16[16,2048]{1,0:T(8,128)(2,1)S(1)} %collective-permute-done.5.refs_3_, ...), custom_call_target="tpu_custom_call" | custom-call | flops 402653184 | bytes 262144 | tf_op jit(solution)/shard_map/pallas_call | solution.py:18
  18.6 1.0 %shard_map.76 = (f32[64,2048]{1,0:T(8,128)S(1)}, bf16[16,2048]{1,0:T(8,128)(2,1)S(1)}, bf16[16,2048]{1,0:T(8,128)(2,1)S(1)}, bf16[16,2048]{1,0:T(8,128)(2,1)S(1)}, bf16[16,2048]{1,0:T(8,128)(2,1)S(1)}) custom-call(bf16[64,1536]{1,0:T(8,128)(2,1)S(1)} %shard_map.75.codes_ref, bf16[1,1536,2048]{2,1,0:T(8,128)(2,1)S(1)} %copy-done), custom_call_target="tpu_custom_call" | custom-call | flops 402653184 | bytes 262144 | tf_op jit(solution)/shard_map/pallas_call | solution.py:18
  20.0 1.5 %collective-permute-start.8 = (bf16[16,2048]{1,0:T(8,128)(2,1)S(1)}, bf16[16,2048]{1,0:T(8,128)(2,1)S(1)}, u32[]{:S(2)}, u32[]{:S(2)}) collective-permute-start(bf16[16,2048]{1,0:T(8,128)(2,1)S(1)} %get-tuple-element.24), channel_id=1, source_target_pairs={{0,3},{1,2},{2,1},{3,0},{4,7},{5,6},{6,5},{7,4},{8,11},{9,10},{10,... | collective-permute-start | bytes 196616 | tf_op jit(solution)/shard_map/ppermute | solution.py:142
  21.5 0.5 %collective-permute-start.9 = (bf16[16,2048]{1,0:T(8,128)(2,1)S(1)}, bf16[16,2048]{1,0:T(8,128)(2,1)S(1)}, u32[]{:S(2)}, u32[]{:S(2)}) collective-permute-start(bf16[16,2048]{1,0:T(8,128)(2,1)S(1)} %get-tuple-element.25), channel_id=1, source_target_pairs={{0,2},{1,3},{2,0},{3,1},{4,6},{5,7},{6,4},{7,5},{8,10},{9,11},{10,... | collective-permute-start | bytes 196616 | tf_op jit(solution)/shard_map/ppermute | solution.py:142
  22.0 1.5 %collective-permute-start.10 = (bf16[16,2048]{1,0:T(8,128)(2,1)S(1)}, bf16[16,2048]{1,0:T(8,128)(2,1)S(1)}, u32[]{:S(2)}, u32[]{:S(2)}) collective-permute-start(bf16[16,2048]{1,0:T(8,128)(2,1)S(1)} %get-tuple-element.26), channel_id=1, source_target_pairs={{0,1},{1,0},{2,3},{3,2},{4,5},{5,4},{6,7},{7,6},{8,9},{9,8},{10,11... | collective-permute-start | bytes 196616 | tf_op jit(solution)/shard_map/ppermute | solution.py:142
  23.5 1.7 %collective-permute-done.8.refs_1_ = bf16[16,2048]{1,0:T(8,128)(2,1)S(1)} collective-permute-done((bf16[16,2048]{1,0:T(8,128)(2,1)S(1)}, bf16[16,2048]{1,0:T(8,128)(2,1)S(1)}, u32[]{:S(2)}, u32[]{:S(2)}) %collective-permute-start.8) | collective-permute-done | bytes 65568 | tf_op jit(solution)/shard_map/ppermute | solution.py:142
  25.2 0.7 %collective-permute-done.9.refs_1_ = bf16[16,2048]{1,0:T(8,128)(2,1)S(1)} collective-permute-done((bf16[16,2048]{1,0:T(8,128)(2,1)S(1)}, bf16[16,2048]{1,0:T(8,128)(2,1)S(1)}, u32[]{:S(2)}, u32[]{:S(2)}) %collective-permute-start.9) | collective-permute-done | bytes 65568 | tf_op jit(solution)/shard_map/ppermute | solution.py:142
  26.3 1.6 %collective-permute-start.11 = (bf16[4,2048]{1,0:T(4,128)(2,1)S(1)}, bf16[4,2048]{1,0:T(4,128)(2,1)S(1)}, u32[]{:S(2)}, u32[]{:S(2)}) collective-permute-start(bf16[4,2048]{1,0:T(4,128)(2,1)S(1)} %get-tuple-element.28), channel_id=1, source_target_pairs={{0,12},{1,13},{2,14},{3,15},{4,8},{5,9},{6,10},{7,11},{8,4},{9,5},... | collective-permute-start | bytes 49160 | tf_op jit(solution)/shard_map/ppermute | solution.py:142
  27.9 0.6 %collective-permute-start.12 = (bf16[4,2048]{1,0:T(4,128)(2,1)S(1)}, bf16[4,2048]{1,0:T(4,128)(2,1)S(1)}, u32[]{:S(2)}, u32[]{:S(2)}) collective-permute-start(bf16[4,2048]{1,0:T(4,128)(2,1)S(1)} %get-tuple-element.29), channel_id=1, source_target_pairs={{0,8},{1,9},{2,10},{3,11},{4,12},{5,13},{6,14},{7,15},{8,0},{9,1},... | collective-permute-start | bytes 49160 | tf_op jit(solution)/shard_map/ppermute | solution.py:142
  28.5 2.3 %collective-permute-start.13 = (bf16[4,2048]{1,0:T(4,128)(2,1)S(1)}, bf16[4,2048]{1,0:T(4,128)(2,1)S(1)}, u32[]{:S(2)}, u32[]{:S(2)}) collective-permute-start(bf16[4,2048]{1,0:T(4,128)(2,1)S(1)} %get-tuple-element.30), channel_id=1, source_target_pairs={{0,4},{1,5},{2,6},{3,7},{4,0},{5,1},{6,2},{7,3},{8,12},{9,13},{10,... | collective-permute-start | bytes 49160 | tf_op jit(solution)/shard_map/ppermute | solution.py:142
  30.8 1.1 %collective-permute-done.11.refs_1_ = bf16[4,2048]{1,0:T(4,128)(2,1)S(1)} collective-permute-done((bf16[4,2048]{1,0:T(4,128)(2,1)S(1)}, bf16[4,2048]{1,0:T(4,128)(2,1)S(1)}, u32[]{:S(2)}, u32[]{:S(2)}) %collective-permute-start.11) | collective-permute-done | bytes 16416 | tf_op jit(solution)/shard_map/ppermute | solution.py:142
  31.9 0.7 %collective-permute-done.12.refs_1_ = bf16[4,2048]{1,0:T(4,128)(2,1)S(1)} collective-permute-done((bf16[4,2048]{1,0:T(4,128)(2,1)S(1)}, bf16[4,2048]{1,0:T(4,128)(2,1)S(1)}, u32[]{:S(2)}, u32[]{:S(2)}) %collective-permute-start.12) | collective-permute-done | bytes 16416 | tf_op jit(solution)/shard_map/ppermute | solution.py:142
  32.7 0.6 %shard_map.81 = f32[1,4,2048]{2,1,0:T(4,128)} custom-call(f32[4,2048]{1,0:T(4,128)S(1)} %shard_map.80.refs_0_, bf16[4,2048]{1,0:T(4,128)(2,1)S(1)} %collective-permute-done.12.refs_1_, bf16[4,2048]{1,0:T(4,128)(2,1)S(1)} %collective-permute-done.13.refs_2_, f32[1,4,2048]{2,1,0:T(4,128)S(1)} %copy-done.2), custom_call_target="tpu_custom_call" | custom-call | bytes 262144 | tf_op jit(solution)/shard_map/pallas_call | solution.py:18
  (25 shorter events, 1.2 us)
Async XLA Ops:
  0.0 7.2 %collective-permute-start = (f32[1,4,2048]{2,1,0:T(4,128)}, f32[1,4,2048]{2,1,0:T(4,128)S(1)}, u32[]{:S(2)}, u32[]{:S(2)}) collective-permute-start(f32[1,4,2048]{2,1,0:T(4,128)} %rows_ref.1), channel_id=1, source_target_pairs={{0,12},{1,13},{2,14},{3,15},{4,8},{5,9},{6,10},{7,11},{8,4},{9,5},... | collective-permute-start | bytes 98312 | tf_op jit(solution)/shard_map/ppermute | solution.py:142
  5.0 5.0 %collective-permute-start.2 = (f32[1,4,2048]{2,1,0:T(4,128)}, f32[1,4,2048]{2,1,0:T(4,128)S(1)}, u32[]{:S(2)}, u32[]{:S(2)}) collective-permute-start(f32[1,4,2048]{2,1,0:T(4,128)} %rows_ref.1), channel_id=1, source_target_pairs={{0,8},{1,9},{2,10},{3,11},{4,12},{5,13},{6,14},{7,15},{8,0},{9,1},... | collective-permute-start | bytes 98312 | tf_op jit(solution)/shard_map/ppermute | solution.py:142
  5.1 5.0 %collective-permute-start.1 = (f32[1,4,2048]{2,1,0:T(4,128)}, f32[1,4,2048]{2,1,0:T(4,128)S(1)}, u32[]{:S(2)}, u32[]{:S(2)}) collective-permute-start(f32[1,4,2048]{2,1,0:T(4,128)} %rows_ref.1), channel_id=1, source_target_pairs={{0,4},{1,5},{2,6},{3,7},{4,0},{5,1},{6,2},{7,3},{8,12},{9,13},{10,... | collective-permute-start | bytes 98312 | tf_op jit(solution)/shard_map/ppermute | solution.py:142
  5.6 14.4 %collective-permute-start.7 = (bf16[1,1536,2048]{2,1,0:T(8,128)(2,1)}, bf16[1,1536,2048]{2,1,0:T(8,128)(2,1)S(1)}, u32[]{:S(2)}, u32[]{:S(2)}) collective-permute-start(bf16[1,1536,2048]{2,1,0:T(8,128)(2,1)} %param.12), channel_id=1, source_target_pairs={{0,16},{16,0},{1,17},{17,1},{2,18},{18,2},{3,19},{19,3},{4,20},{20... | collective-permute-start | bytes 18874376 | tf_op jit(solution)/shard_map/ppermute | solution.py:145
  5.6 0.8 %copy-start.5 = (f32[1,4,2048]{2,1,0:T(4,128)S(1)}, f32[1,4,2048]{2,1,0:T(4,128)}, u32[]{:S(2)}) copy-start(f32[1,4,2048]{2,1,0:T(4,128)} %rows_ref.1) | copy-start | bytes 98308
  6.5 11.0 %copy-start.1 = (bf16[1,2048,1536]{2,1,0:T(8,128)(2,1)S(1)}, bf16[1,2048,1536]{2,1,0:T(8,128)(2,1)}, u32[]{:S(2)}) copy-start(bf16[1,2048,1536]{2,1,0:T(8,128)(2,1)} %refs_4_.1) | copy-start | bytes 18874372
  6.5 11.0 %copy-start.3 = (f32[1,1536]{1,0:T(1,128)S(1)}, f32[1,1536]{1,0:T(1,128)}, u32[]{:S(2)}) copy-start(f32[1,1536]{1,0:T(1,128)} %refs_5_.1) | copy-start | bytes 18436
  6.5 11.0 %copy-start.4 = (f32[1,1536]{1,0:T(1,128)S(1)}, f32[1,1536]{1,0:T(1,128)}, u32[]{:S(2)}) copy-start(f32[1,1536]{1,0:T(1,128)} %refs_6_.1) | copy-start | bytes 18436
  10.2 8.4 %copy-start = (bf16[1,1536,2048]{2,1,0:T(8,128)(2,1)S(1)}, bf16[1,1536,2048]{2,1,0:T(8,128)(2,1)}, u32[]{:S(2)}) copy-start(bf16[1,1536,2048]{2,1,0:T(8,128)(2,1)} %dec_ref.1) | copy-start | bytes 18874372
  10.2 5.2 %collective-permute-start.5 = (bf16[16,2048]{1,0:T(8,128)(2,1)S(1)}, bf16[16,2048]{1,0:T(8,128)(2,1)S(1)}, u32[]{:S(2)}, u32[]{:S(2)}) collective-permute-start(bf16[16,2048]{1,0:T(8,128)(2,1)S(1)} %shard_map.74.refs_0_), channel_id=1, source_target_pairs={{0,3},{1,2},{2,1},{3,0},{4,7},{5,6},{6,5},{7,4},{8,11},{9,10},{10,... | collective-permute-start | bytes 196616 | tf_op jit(solution)/shard_map/ppermute | solution.py:142
  12.7 4.3 %collective-permute-start.4 = (bf16[16,2048]{1,0:T(8,128)(2,1)S(1)}, bf16[16,2048]{1,0:T(8,128)(2,1)S(1)}, u32[]{:S(2)}, u32[]{:S(2)}) collective-permute-start(bf16[16,2048]{1,0:T(8,128)(2,1)S(1)} %shard_map.74.refs_0_), channel_id=1, source_target_pairs={{0,2},{1,3},{2,0},{3,1},{4,6},{5,7},{6,4},{7,5},{8,10},{9,11},{10,... | collective-permute-start | bytes 196616 | tf_op jit(solution)/shard_map/ppermute | solution.py:142
  13.2 4.3 %collective-permute-start.3 = (bf16[16,2048]{1,0:T(8,128)(2,1)S(1)}, bf16[16,2048]{1,0:T(8,128)(2,1)S(1)}, u32[]{:S(2)}, u32[]{:S(2)}) collective-permute-start(bf16[16,2048]{1,0:T(8,128)(2,1)S(1)} %shard_map.74.refs_0_), channel_id=1, source_target_pairs={{0,1},{1,0},{2,3},{3,2},{4,5},{5,4},{6,7},{7,6},{8,9},{9,8},{10,11... | collective-permute-start | bytes 196616 | tf_op jit(solution)/shard_map/ppermute | solution.py:142
  18.5 14.2 %copy-start.2 = (f32[1,4,2048]{2,1,0:T(4,128)S(1)}, f32[1,4,2048]{2,1,0:T(4,128)}, u32[]{:S(2)}) copy-start(f32[1,4,2048]{2,1,0:T(4,128)} %refs_3_.1) | copy-start | bytes 98308
  18.5 1.5 %collective-permute-start.6 = (bf16[64,1536]{1,0:T(8,128)(2,1)S(1)}, bf16[64,1536]{1,0:T(8,128)(2,1)S(1)}, u32[]{:S(2)}, u32[]{:S(2)}) collective-permute-start(bf16[64,1536]{1,0:T(8,128)(2,1)S(1)} %shard_map.75.codes_ref), channel_id=1, source_target_pairs={{0,16},{16,0},{1,17},{17,1},{2,18},{18,2},{3,19},{19,3},{4,20},{20... | collective-permute-start | bytes 589832 | tf_op jit(solution)/shard_map/ppermute | solution.py:145
  20.0 5.2 %collective-permute-start.8 = (bf16[16,2048]{1,0:T(8,128)(2,1)S(1)}, bf16[16,2048]{1,0:T(8,128)(2,1)S(1)}, u32[]{:S(2)}, u32[]{:S(2)}) collective-permute-start(bf16[16,2048]{1,0:T(8,128)(2,1)S(1)} %get-tuple-element.24), channel_id=1, source_target_pairs={{0,3},{1,2},{2,1},{3,0},{4,7},{5,6},{6,5},{7,4},{8,11},{9,10},{10,... | collective-permute-start | bytes 196616 | tf_op jit(solution)/shard_map/ppermute | solution.py:142
  21.5 4.4 %collective-permute-start.9 = (bf16[16,2048]{1,0:T(8,128)(2,1)S(1)}, bf16[16,2048]{1,0:T(8,128)(2,1)S(1)}, u32[]{:S(2)}, u32[]{:S(2)}) collective-permute-start(bf16[16,2048]{1,0:T(8,128)(2,1)S(1)} %get-tuple-element.25), channel_id=1, source_target_pairs={{0,2},{1,3},{2,0},{3,1},{4,6},{5,7},{6,4},{7,5},{8,10},{9,11},{10,... | collective-permute-start | bytes 196616 | tf_op jit(solution)/shard_map/ppermute | solution.py:142
  22.0 4.3 %collective-permute-start.10 = (bf16[16,2048]{1,0:T(8,128)(2,1)S(1)}, bf16[16,2048]{1,0:T(8,128)(2,1)S(1)}, u32[]{:S(2)}, u32[]{:S(2)}) collective-permute-start(bf16[16,2048]{1,0:T(8,128)(2,1)S(1)} %get-tuple-element.26), channel_id=1, source_target_pairs={{0,1},{1,0},{2,3},{3,2},{4,5},{5,4},{6,7},{7,6},{8,9},{9,8},{10,11... | collective-permute-start | bytes 196616 | tf_op jit(solution)/shard_map/ppermute | solution.py:142
  26.3 5.6 %collective-permute-start.11 = (bf16[4,2048]{1,0:T(4,128)(2,1)S(1)}, bf16[4,2048]{1,0:T(4,128)(2,1)S(1)}, u32[]{:S(2)}, u32[]{:S(2)}) collective-permute-start(bf16[4,2048]{1,0:T(4,128)(2,1)S(1)} %get-tuple-element.28), channel_id=1, source_target_pairs={{0,12},{1,13},{2,14},{3,15},{4,8},{5,9},{6,10},{7,11},{8,4},{9,5},... | collective-permute-start | bytes 49160 | tf_op jit(solution)/shard_map/ppermute | solution.py:142
  27.9 4.7 %collective-permute-start.12 = (bf16[4,2048]{1,0:T(4,128)(2,1)S(1)}, bf16[4,2048]{1,0:T(4,128)(2,1)S(1)}, u32[]{:S(2)}, u32[]{:S(2)}) collective-permute-start(bf16[4,2048]{1,0:T(4,128)(2,1)S(1)} %get-tuple-element.29), channel_id=1, source_target_pairs={{0,8},{1,9},{2,10},{3,11},{4,12},{5,13},{6,14},{7,15},{8,0},{9,1},... | collective-permute-start | bytes 49160 | tf_op jit(solution)/shard_map/ppermute | solution.py:142
  28.5 4.2 %collective-permute-start.13 = (bf16[4,2048]{1,0:T(4,128)(2,1)S(1)}, bf16[4,2048]{1,0:T(4,128)(2,1)S(1)}, u32[]{:S(2)}, u32[]{:S(2)}) collective-permute-start(bf16[4,2048]{1,0:T(4,128)(2,1)S(1)} %get-tuple-element.30), channel_id=1, source_target_pairs={{0,4},{1,5},{2,6},{3,7},{4,0},{5,1},{6,2},{7,3},{8,12},{9,13},{10,... | collective-permute-start | bytes 49160 | tf_op jit(solution)/shard_map/ppermute | solution.py:142

commit v7 on v5

--- a/solution.py
+++ b/solution.py
@@ -14,10 +14,11 @@
 TALL = 128
 
 
-def call(kernel, out_shape, args, flops=0, moved=2**18):
+def call(kernel, out_shape, args, flops=0, moved=2**18, aliases=()):
     return pl.pallas_call(
         kernel,
         out_shape=out_shape,
+        input_output_aliases=dict(aliases),
         in_specs=[VMEM] * len(args),
         out_specs=jax.tree.map(lambda _: VMEM, out_shape),
         compiler_params=pltpu.CompilerParams(vmem_limit_bytes=GRANT),
@@ -54,14 +55,21 @@
 
 
 def encode_kernel(*refs):
-    *block_refs, enc_ref, bias_ref, limit_ref, codes_ref = refs
+    *block_refs, enc_ref, bias_ref, limit_ref, dec_ref, codes_ref, own_ref = refs
     rows = jnp.concatenate([ref[...] for ref in block_refs], axis=0)
     pre = dot(rows, enc_ref[0]) + bias_ref[...]
-    codes_ref[...] = (pre * jax.nn.sigmoid((pre - limit_ref[...]) / 0.1)).astype(jnp.bfloat16)
+    codes = (pre * jax.nn.sigmoid((pre - limit_ref[...]) / 0.1)).astype(jnp.bfloat16)
+    codes_ref[...] = codes
+
+    @pl.when(lax.axis_index("layer") % 2 == 1)
+    def _():
+        own_ref[...] = dot(codes, dec_ref[0])
 
 
-def decode_kernel(codes_ref, dec_ref, own_ref):
-    own_ref[...] = dot(codes_ref[...], dec_ref[0])
+def decode_kernel(codes_ref, dec_ref, early_ref, own_ref):
+    @pl.when(lax.axis_index("layer") % 2 == 0)
+    def _():
+        own_ref[...] = dot(codes_ref[...], dec_ref[0])
 
 
 def cut(total, part_refs):
@@ -150,9 +158,9 @@
         blocks += [swap(blocks[0], stage, j) for j in range(1, radices[stage])]
         size *= radices[stage]
 
-    codes = call(encode_kernel, shape((rows, width), half), (*blocks, w_enc, b_enc, threshold), work)
+    codes, early = call(encode_kernel, (shape((rows, width), half), shape((rows, depth), full)), (*blocks, w_enc, b_enc, threshold, dec_self), work)
     before = onward(codes)
-    own = call(decode_kernel, shape((rows, depth), full), (codes, dec_self), work)
+    own = call(decode_kernel, shape((rows, depth), full), (codes, dec_self, early), work, aliases=[(2, 0)])
 
     size = rows // radices[0]
     kernel = functools.partial(join_kernel, places)

time: 33.6 us -> 33.6 us (level)
  transfers between devices with their start and end apart: 14 -> 14, of which waited for: 11 -> 12; matrix products, arithmetic and copies ran while one was open for 0% -> 0% of each run, Pallas kernels for 7% -> 7%
where the time goes in v7:
time: 33.6 us; the launch traced here: 33.4 us
  starting transfers between devices  17.2 us (51%)
  waiting for transfers between devices  12.3 us (37%)
  Pallas kernels  2.92 us (9%)
  local copies, waits for them, and re-layouts  0.81 us (2%)
    ppermute x12, starting transfers between devices, swap(): return lax.ppermute(value, ('layer', 'feat'), pairs)  17.2 us
    ppermute x12, waiting for transfers between devices, swap(): return lax.ppermute(value, ('layer', 'feat'), pairs)  11.9 us
    pallas_call x7, Pallas kernels, call(): pl.pallas_call(kernel, out_shape=out_shape, input_output_aliases=dict(ali...  2.92 us
    unnamed x12, local copies, waits for them, and re-layouts  0.81 us
  transfers between devices with their start and end apart: 14, of which 12 were waited for; matrix products, arithmetic and copies ran while one was open for 0% of the time, Pallas kernels for 7%

profile of v7, /device:TPU:0, one launch (start us, length us, event | category | flops | bytes accessed | tf_op | source)
XLA Modules:
  0.0 33.4 jit_solution(2788235442439853764)
XLA Ops:
  0.0 5.0 %collective-permute-start = (f32[1,4,2048]{2,1,0:T(4,128)}, f32[1,4,2048]{2,1,0:T(4,128)S(1)}, u32[]{:S(2)}, u32[]{:S(2)}) collective-permute-start(f32[1,4,2048]{2,1,0:T(4,128)} %rows_ref.1), channel_id=1, source_target_pairs={{0,12},{1,13},{2,14},{3,15},{4,8},{5,9},{6,10},{7,11},{8,4},{9,5},... | collective-permute-start | bytes 98312 | tf_op jit(solution)/shard_map/ppermute | solution.py:141
  5.1 0.6 %collective-permute-start.1 = (f32[1,4,2048]{2,1,0:T(4,128)}, f32[1,4,2048]{2,1,0:T(4,128)S(1)}, u32[]{:S(2)}, u32[]{:S(2)}) collective-permute-start(f32[1,4,2048]{2,1,0:T(4,128)} %rows_ref.1), channel_id=1, source_target_pairs={{0,4},{1,5},{2,6},{3,7},{4,0},{5,1},{6,2},{7,3},{8,12},{9,13},{10,... | collective-permute-start | bytes 98312 | tf_op jit(solution)/shard_map/ppermute | solution.py:141
  5.6 0.8 %copy-done.5 = f32[1,4,2048]{2,1,0:T(4,128)S(1)} copy-done((f32[1,4,2048]{2,1,0:T(4,128)S(1)}, f32[1,4,2048]{2,1,0:T(4,128)}, u32[]{:S(2)}) %copy-start.5) | copy-done | bytes 32792
  6.5 0.6 %collective-permute-done.refs_0_ = f32[1,4,2048]{2,1,0:T(4,128)S(1)} collective-permute-done((f32[1,4,2048]{2,1,0:T(4,128)}, f32[1,4,2048]{2,1,0:T(4,128)S(1)}, u32[]{:S(2)}, u32[]{:S(2)}) %collective-permute-start) | collective-permute-done | bytes 32800 | tf_op jit(solution)/shard_map/ppermute | solution.py:141
  7.2 2.9 %collective-permute-done.2.refs_2_ = f32[1,4,2048]{2,1,0:T(4,128)S(1)} collective-permute-done((f32[1,4,2048]{2,1,0:T(4,128)}, f32[1,4,2048]{2,1,0:T(4,128)S(1)}, u32[]{:S(2)}, u32[]{:S(2)}) %collective-permute-start.2) | collective-permute-done | bytes 32800 | tf_op jit(solution)/shard_map/ppermute | solution.py:141
  10.2 2.5 %collective-permute-start.5 = (bf16[16,2048]{1,0:T(8,128)(2,1)S(1)}, bf16[16,2048]{1,0:T(8,128)(2,1)S(1)}, u32[]{:S(2)}, u32[]{:S(2)}) collective-permute-start(bf16[16,2048]{1,0:T(8,128)(2,1)S(1)} %shard_map.74.refs_0_), channel_id=1, source_target_pairs={{0,3},{1,2},{2,1},{3,0},{4,7},{5,6},{6,5},{7,4},{8,11},{9,10},{10,... | collective-permute-start | bytes 196616 | tf_op jit(solution)/shard_map/ppermute | solution.py:141
  12.7 0.5 %collective-permute-start.4 = (bf16[16,2048]{1,0:T(8,128)(2,1)S(1)}, bf16[16,2048]{1,0:T(8,128)(2,1)S(1)}, u32[]{:S(2)}, u32[]{:S(2)}) collective-permute-start(bf16[16,2048]{1,0:T(8,128)(2,1)S(1)} %shard_map.74.refs_0_), channel_id=1, source_target_pairs={{0,2},{1,3},{2,0},{3,1},{4,6},{5,7},{6,4},{7,5},{8,10},{9,11},{10,... | collective-permute-start | bytes 196616 | tf_op jit(solution)/shard_map/ppermute | solution.py:141
  13.2 0.5 %collective-permute-start.3 = (bf16[16,2048]{1,0:T(8,128)(2,1)S(1)}, bf16[16,2048]{1,0:T(8,128)(2,1)S(1)}, u32[]{:S(2)}, u32[]{:S(2)}) collective-permute-start(bf16[16,2048]{1,0:T(8,128)(2,1)S(1)} %shard_map.74.refs_0_), channel_id=1, source_target_pairs={{0,1},{1,0},{2,3},{3,2},{4,5},{5,4},{6,7},{7,6},{8,9},{9,8},{10,11... | collective-permute-start | bytes 196616 | tf_op jit(solution)/shard_map/ppermute | solution.py:141
  13.8 1.7 %collective-permute-done.5.refs_3_ = bf16[16,2048]{1,0:T(8,128)(2,1)S(1)} collective-permute-done((bf16[16,2048]{1,0:T(8,128)(2,1)S(1)}, bf16[16,2048]{1,0:T(8,128)(2,1)S(1)}, u32[]{:S(2)}, u32[]{:S(2)}) %collective-permute-start.5) | collective-permute-done | bytes 65568 | tf_op jit(solution)/shard_map/ppermute | solution.py:141
  15.4 1.5 %collective-permute-done.4.refs_2_ = bf16[16,2048]{1,0:T(8,128)(2,1)S(1)} collective-permute-done((bf16[16,2048]{1,0:T(8,128)(2,1)S(1)}, bf16[16,2048]{1,0:T(8,128)(2,1)S(1)}, u32[]{:S(2)}, u32[]{:S(2)}) %collective-permute-start.4) | collective-permute-done | bytes 65568 | tf_op jit(solution)/shard_map/ppermute | solution.py:141
  17.0 0.5 %collective-permute-done.3.refs_1_ = bf16[16,2048]{1,0:T(8,128)(2,1)S(1)} collective-permute-done((bf16[16,2048]{1,0:T(8,128)(2,1)S(1)}, bf16[16,2048]{1,0:T(8,128)(2,1)S(1)}, u32[]{:S(2)}, u32[]{:S(2)}) %collective-permute-start.3) | collective-permute-done | bytes 65568 | tf_op jit(solution)/shard_map/ppermute | solution.py:141
  17.5 1.0 %shard_map.75 = (bf16[64,1536]{1,0:T(8,128)(2,1)S(1)}, f32[64,2048]{1,0:T(8,128)S(1)}) custom-call(bf16[16,2048]{1,0:T(8,128)(2,1)S(1)} %shard_map.74.refs_0_, bf16[16,2048]{1,0:T(8,128)(2,1)S(1)} %collective-permute-done.3.refs_1_, bf16[16,2048]{1,0:T(8,128)(2,1)S(1)} %collective-permute-done.4.refs_2_, ...), custom_call_target="tpu_custom_call" | custom-call | flops 402653184 | bytes 262144 | tf_op jit(solution)/shard_map/pallas_call | solution.py:18
  18.6 1.0 %shard_map.76.own_ref = f32[64,2048]{1,0:T(8,128)S(1)} custom-call(bf16[64,1536]{1,0:T(8,128)(2,1)S(1)} %get-tuple-element.15.codes_ref, bf16[1,1536,2048]{2,1,0:T(8,128)(2,1)S(1)} %copy-done, f32[64,2048]{1,0:T(8,128)S(1)} %get-tuple-element.16.early_ref), custom_call_target="tpu_custom_call", output_to_operand_aliasing={{}: (2, {})} | custom-call | flops 402653184 | bytes 262144 | tf_op jit(solution)/shard_map/pallas_call | solution.py:18
  20.1 1.6 %collective-permute-start.8 = (bf16[16,2048]{1,0:T(8,128)(2,1)S(1)}, bf16[16,2048]{1,0:T(8,128)(2,1)S(1)}, u32[]{:S(2)}, u32[]{:S(2)}) collective-permute-start(bf16[16,2048]{1,0:T(8,128)(2,1)S(1)} %get-tuple-element.18), channel_id=1, source_target_pairs={{0,3},{1,2},{2,1},{3,0},{4,7},{5,6},{6,5},{7,4},{8,11},{9,10},{10,... | collective-permute-start | bytes 196616 | tf_op jit(solution)/shard_map/ppermute | solution.py:141
  21.6 0.5 %collective-permute-start.9 = (bf16[16,2048]{1,0:T(8,128)(2,1)S(1)}, bf16[16,2048]{1,0:T(8,128)(2,1)S(1)}, u32[]{:S(2)}, u32[]{:S(2)}) collective-permute-start(bf16[16,2048]{1,0:T(8,128)(2,1)S(1)} %get-tuple-element.19), channel_id=1, source_target_pairs={{0,2},{1,3},{2,0},{3,1},{4,6},{5,7},{6,4},{7,5},{8,10},{9,11},{10,... | collective-permute-start | bytes 196616 | tf_op jit(solution)/shard_map/ppermute | solution.py:141
  22.1 1.5 %collective-permute-start.10 = (bf16[16,2048]{1,0:T(8,128)(2,1)S(1)}, bf16[16,2048]{1,0:T(8,128)(2,1)S(1)}, u32[]{:S(2)}, u32[]{:S(2)}) collective-permute-start(bf16[16,2048]{1,0:T(8,128)(2,1)S(1)} %get-tuple-element.20), channel_id=1, source_target_pairs={{0,1},{1,0},{2,3},{3,2},{4,5},{5,4},{6,7},{7,6},{8,9},{9,8},{10,11... | collective-permute-start | bytes 196616 | tf_op jit(solution)/shard_map/ppermute | solution.py:141
  23.6 1.7 %collective-permute-done.8.refs_1_ = bf16[16,2048]{1,0:T(8,128)(2,1)S(1)} collective-permute-done((bf16[16,2048]{1,0:T(8,128)(2,1)S(1)}, bf16[16,2048]{1,0:T(8,128)(2,1)S(1)}, u32[]{:S(2)}, u32[]{:S(2)}) %collective-permute-start.8) | collective-permute-done | bytes 65568 | tf_op jit(solution)/shard_map/ppermute | solution.py:141
  25.3 0.7 %collective-permute-done.9.refs_2_ = bf16[16,2048]{1,0:T(8,128)(2,1)S(1)} collective-permute-done((bf16[16,2048]{1,0:T(8,128)(2,1)S(1)}, bf16[16,2048]{1,0:T(8,128)(2,1)S(1)}, u32[]{:S(2)}, u32[]{:S(2)}) %collective-permute-start.9) | collective-permute-done | bytes 65568 | tf_op jit(solution)/shard_map/ppermute | solution.py:141
  26.4 1.5 %collective-permute-start.11 = (bf16[4,2048]{1,0:T(4,128)(2,1)S(1)}, bf16[4,2048]{1,0:T(4,128)(2,1)S(1)}, u32[]{:S(2)}, u32[]{:S(2)}) collective-permute-start(bf16[4,2048]{1,0:T(4,128)(2,1)S(1)} %get-tuple-element.22), channel_id=1, source_target_pairs={{0,12},{1,13},{2,14},{3,15},{4,8},{5,9},{6,10},{7,11},{8,4},{9,5},... | collective-permute-start | bytes 49160 | tf_op jit(solution)/shard_map/ppermute | solution.py:141
  28.0 0.6 %collective-permute-start.12 = (bf16[4,2048]{1,0:T(4,128)(2,1)S(1)}, bf16[4,2048]{1,0:T(4,128)(2,1)S(1)}, u32[]{:S(2)}, u32[]{:S(2)}) collective-permute-start(bf16[4,2048]{1,0:T(4,128)(2,1)S(1)} %get-tuple-element.23), channel_id=1, source_target_pairs={{0,8},{1,9},{2,10},{3,11},{4,12},{5,13},{6,14},{7,15},{8,0},{9,1},... | collective-permute-start | bytes 49160 | tf_op jit(solution)/shard_map/ppermute | solution.py:141
  28.6 2.3 %collective-permute-start.13 = (bf16[4,2048]{1,0:T(4,128)(2,1)S(1)}, bf16[4,2048]{1,0:T(4,128)(2,1)S(1)}, u32[]{:S(2)}, u32[]{:S(2)}) collective-permute-start(bf16[4,2048]{1,0:T(4,128)(2,1)S(1)} %get-tuple-element.24), channel_id=1, source_target_pairs={{0,4},{1,5},{2,6},{3,7},{4,0},{5,1},{6,2},{7,3},{8,12},{9,13},{10,... | collective-permute-start | bytes 49160 | tf_op jit(solution)/shard_map/ppermute | solution.py:141
  30.9 1.1 %collective-permute-done.11.refs_1_ = bf16[4,2048]{1,0:T(4,128)(2,1)S(1)} collective-permute-done((bf16[4,2048]{1,0:T(4,128)(2,1)S(1)}, bf16[4,2048]{1,0:T(4,128)(2,1)S(1)}, u32[]{:S(2)}, u32[]{:S(2)}) %collective-permute-start.11) | collective-permute-done | bytes 16416 | tf_op jit(solution)/shard_map/ppermute | solution.py:141
  32.1 0.7 %collective-permute-done.12.refs_2_ = bf16[4,2048]{1,0:T(4,128)(2,1)S(1)} collective-permute-done((bf16[4,2048]{1,0:T(4,128)(2,1)S(1)}, bf16[4,2048]{1,0:T(4,128)(2,1)S(1)}, u32[]{:S(2)}, u32[]{:S(2)}) %collective-permute-start.12) | collective-permute-done | bytes 16416 | tf_op jit(solution)/shard_map/ppermute | solution.py:141
  32.8 0.6 %shard_map.79 = f32[1,4,2048]{2,1,0:T(4,128)} custom-call(bf16[4,2048]{1,0:T(4,128)(2,1)S(1)} %get-tuple-element.21.refs_0_, bf16[4,2048]{1,0:T(4,128)(2,1)S(1)} %collective-permute-done.11.refs_1_, bf16[4,2048]{1,0:T(4,128)(2,1)S(1)} %collective-permute-done.12.refs_2_, bf16[4,2048]{1,0:T(4,128)(2,1)S(1)} %collective-permute-done.13.refs_3_, ...), custom_call_target="tpu_custom_call" | custom-call | bytes 262144 | tf_op jit(solution)/shard_map/pallas_call | solution.py:18
  (23 shorter events, 1.3 us)
Async XLA Ops:
  0.0 7.2 %collective-permute-start = (f32[1,4,2048]{2,1,0:T(4,128)}, f32[1,4,2048]{2,1,0:T(4,128)S(1)}, u32[]{:S(2)}, u32[]{:S(2)}) collective-permute-start(f32[1,4,2048]{2,1,0:T(4,128)} %rows_ref.1), channel_id=1, source_target_pairs={{0,12},{1,13},{2,14},{3,15},{4,8},{5,9},{6,10},{7,11},{8,4},{9,5},... | collective-permute-start | bytes 98312 | tf_op jit(solution)/shard_map/ppermute | solution.py:141
  5.0 5.0 %collective-permute-start.2 = (f32[1,4,2048]{2,1,0:T(4,128)}, f32[1,4,2048]{2,1,0:T(4,128)S(1)}, u32[]{:S(2)}, u32[]{:S(2)}) collective-permute-start(f32[1,4,2048]{2,1,0:T(4,128)} %rows_ref.1), channel_id=1, source_target_pairs={{0,8},{1,9},{2,10},{3,11},{4,12},{5,13},{6,14},{7,15},{8,0},{9,1},... | collective-permute-start | bytes 98312 | tf_op jit(solution)/shard_map/ppermute | solution.py:141
  5.1 5.0 %collective-permute-start.1 = (f32[1,4,2048]{2,1,0:T(4,128)}, f32[1,4,2048]{2,1,0:T(4,128)S(1)}, u32[]{:S(2)}, u32[]{:S(2)}) collective-permute-start(f32[1,4,2048]{2,1,0:T(4,128)} %rows_ref.1), channel_id=1, source_target_pairs={{0,4},{1,5},{2,6},{3,7},{4,0},{5,1},{6,2},{7,3},{8,12},{9,13},{10,... | collective-permute-start | bytes 98312 | tf_op jit(solution)/shard_map/ppermute | solution.py:141
  5.6 14.4 %collective-permute-start.7 = (bf16[1,1536,2048]{2,1,0:T(8,128)(2,1)}, bf16[1,1536,2048]{2,1,0:T(8,128)(2,1)S(1)}, u32[]{:S(2)}, u32[]{:S(2)}) collective-permute-start(bf16[1,1536,2048]{2,1,0:T(8,128)(2,1)} %param.12), channel_id=1, source_target_pairs={{0,16},{16,0},{1,17},{17,1},{2,18},{18,2},{3,19},{19,3},{4,20},{20... | collective-permute-start | bytes 18874376 | tf_op jit(solution)/shard_map/ppermute | solution.py:144
  5.6 0.8 %copy-start.5 = (f32[1,4,2048]{2,1,0:T(4,128)S(1)}, f32[1,4,2048]{2,1,0:T(4,128)}, u32[]{:S(2)}) copy-start(f32[1,4,2048]{2,1,0:T(4,128)} %rows_ref.1) | copy-start | bytes 98308
  6.5 11.0 %copy-start = (bf16[1,1536,2048]{2,1,0:T(8,128)(2,1)S(1)}, bf16[1,1536,2048]{2,1,0:T(8,128)(2,1)}, u32[]{:S(2)}) copy-start(bf16[1,1536,2048]{2,1,0:T(8,128)(2,1)} %dec_ref.1) | copy-start | bytes 18874372
  6.5 11.0 %copy-start.1 = (bf16[1,2048,1536]{2,1,0:T(8,128)(2,1)S(1)}, bf16[1,2048,1536]{2,1,0:T(8,128)(2,1)}, u32[]{:S(2)}) copy-start(bf16[1,2048,1536]{2,1,0:T(8,128)(2,1)} %refs_4_.2) | copy-start | bytes 18874372
  6.5 11.0 %copy-start.3 = (f32[1,1536]{1,0:T(1,128)S(1)}, f32[1,1536]{1,0:T(1,128)}, u32[]{:S(2)}) copy-start(f32[1,1536]{1,0:T(1,128)} %refs_5_.1) | copy-start | bytes 18436
  6.5 11.0 %copy-start.4 = (f32[1,1536]{1,0:T(1,128)S(1)}, f32[1,1536]{1,0:T(1,128)}, u32[]{:S(2)}) copy-start(f32[1,1536]{1,0:T(1,128)} %refs_6_.1) | copy-start | bytes 18436
  10.2 5.2 %collective-permute-start.5 = (bf16[16,2048]{1,0:T(8,128)(2,1)S(1)}, bf16[16,2048]{1,0:T(8,128)(2,1)S(1)}, u32[]{:S(2)}, u32[]{:S(2)}) collective-permute-start(bf16[16,2048]{1,0:T(8,128)(2,1)S(1)} %shard_map.74.refs_0_), channel_id=1, source_target_pairs={{0,3},{1,2},{2,1},{3,0},{4,7},{5,6},{6,5},{7,4},{8,11},{9,10},{10,... | collective-permute-start | bytes 196616 | tf_op jit(solution)/shard_map/ppermute | solution.py:141
  12.7 4.3 %collective-permute-start.4 = (bf16[16,2048]{1,0:T(8,128)(2,1)S(1)}, bf16[16,2048]{1,0:T(8,128)(2,1)S(1)}, u32[]{:S(2)}, u32[]{:S(2)}) collective-permute-start(bf16[16,2048]{1,0:T(8,128)(2,1)S(1)} %shard_map.74.refs_0_), channel_id=1, source_target_pairs={{0,2},{1,3},{2,0},{3,1},{4,6},{5,7},{6,4},{7,5},{8,10},{9,11},{10,... | collective-permute-start | bytes 196616 | tf_op jit(solution)/shard_map/ppermute | solution.py:141
  13.2 4.3 %collective-permute-start.3 = (bf16[16,2048]{1,0:T(8,128)(2,1)S(1)}, bf16[16,2048]{1,0:T(8,128)(2,1)S(1)}, u32[]{:S(2)}, u32[]{:S(2)}) collective-permute-start(bf16[16,2048]{1,0:T(8,128)(2,1)S(1)} %shard_map.74.refs_0_), channel_id=1, source_target_pairs={{0,1},{1,0},{2,3},{3,2},{4,5},{5,4},{6,7},{7,6},{8,9},{9,8},{10,11... | collective-permute-start | bytes 196616 | tf_op jit(solution)/shard_map/ppermute | solution.py:141
  18.5 1.5 %collective-permute-start.6 = (bf16[64,1536]{1,0:T(8,128)(2,1)S(1)}, bf16[64,1536]{1,0:T(8,128)(2,1)S(1)}, u32[]{:S(2)}, u32[]{:S(2)}) collective-permute-start(bf16[64,1536]{1,0:T(8,128)(2,1)S(1)} %get-tuple-element.15.codes_ref), channel_id=1, source_target_pairs={{0,16},{16,0},{1,17},{17,1},{2,18},{18,2},{3,19},{19,3},{4,20},{20... | collective-permute-start | bytes 589832 | tf_op jit(solution)/shard_map/ppermute | solution.py:144
  18.6 14.2 %copy-start.2 = (f32[1,4,2048]{2,1,0:T(4,128)S(1)}, f32[1,4,2048]{2,1,0:T(4,128)}, u32[]{:S(2)}) copy-start(f32[1,4,2048]{2,1,0:T(4,128)} %refs_4_.3) | copy-start | bytes 98308
  20.1 5.2 %collective-permute-start.8 = (bf16[16,2048]{1,0:T(8,128)(2,1)S(1)}, bf16[16,2048]{1,0:T(8,128)(2,1)S(1)}, u32[]{:S(2)}, u32[]{:S(2)}) collective-permute-start(bf16[16,2048]{1,0:T(8,128)(2,1)S(1)} %get-tuple-element.18), channel_id=1, source_target_pairs={{0,3},{1,2},{2,1},{3,0},{4,7},{5,6},{6,5},{7,4},{8,11},{9,10},{10,... | collective-permute-start | bytes 196616 | tf_op jit(solution)/shard_map/ppermute | solution.py:141
  21.6 4.4 %collective-permute-start.9 = (bf16[16,2048]{1,0:T(8,128)(2,1)S(1)}, bf16[16,2048]{1,0:T(8,128)(2,1)S(1)}, u32[]{:S(2)}, u32[]{:S(2)}) collective-permute-start(bf16[16,2048]{1,0:T(8,128)(2,1)S(1)} %get-tuple-element.19), channel_id=1, source_target_pairs={{0,2},{1,3},{2,0},{3,1},{4,6},{5,7},{6,4},{7,5},{8,10},{9,11},{10,... | collective-permute-start | bytes 196616 | tf_op jit(solution)/shard_map/ppermute | solution.py:141
  22.1 4.3 %collective-permute-start.10 = (bf16[16,2048]{1,0:T(8,128)(2,1)S(1)}, bf16[16,2048]{1,0:T(8,128)(2,1)S(1)}, u32[]{:S(2)}, u32[]{:S(2)}) collective-permute-start(bf16[16,2048]{1,0:T(8,128)(2,1)S(1)} %get-tuple-element.20), channel_id=1, source_target_pairs={{0,1},{1,0},{2,3},{3,2},{4,5},{5,4},{6,7},{7,6},{8,9},{9,8},{10,11... | collective-permute-start | bytes 196616 | tf_op jit(solution)/shard_map/ppermute | solution.py:141
  26.4 5.6 %collective-permute-start.11 = (bf16[4,2048]{1,0:T(4,128)(2,1)S(1)}, bf16[4,2048]{1,0:T(4,128)(2,1)S(1)}, u32[]{:S(2)}, u32[]{:S(2)}) collective-permute-start(bf16[4,2048]{1,0:T(4,128)(2,1)S(1)} %get-tuple-element.22), channel_id=1, source_target_pairs={{0,12},{1,13},{2,14},{3,15},{4,8},{5,9},{6,10},{7,11},{8,4},{9,5},... | collective-permute-start | bytes 49160 | tf_op jit(solution)/shard_map/ppermute | solution.py:141
  28.0 4.7 %collective-permute-start.12 = (bf16[4,2048]{1,0:T(4,128)(2,1)S(1)}, bf16[4,2048]{1,0:T(4,128)(2,1)S(1)}, u32[]{:S(2)}, u32[]{:S(2)}) collective-permute-start(bf16[4,2048]{1,0:T(4,128)(2,1)S(1)} %get-tuple-element.23), channel_id=1, source_target_pairs={{0,8},{1,9},{2,10},{3,11},{4,12},{5,13},{6,14},{7,15},{8,0},{9,1},... | collective-permute-start | bytes 49160 | tf_op jit(solution)/shard_map/ppermute | solution.py:141
  28.6 4.2 %collective-permute-start.13 = (bf16[4,2048]{1,0:T(4,128)(2,1)S(1)}, bf16[4,2048]{1,0:T(4,128)(2,1)S(1)}, u32[]{:S(2)}, u32[]{:S(2)}) collective-permute-start(bf16[4,2048]{1,0:T(4,128)(2,1)S(1)} %get-tuple-element.24), channel_id=1, source_target_pairs={{0,4},{1,5},{2,6},{3,7},{4,0},{5,1},{6,2},{7,3},{8,12},{9,13},{10,... | collective-permute-start | bytes 49160 | tf_op jit(solution)/shard_map/ppermute | solution.py:141

commit v8 on v5

--- a/solution.py
+++ b/solution.py
@@ -43,7 +43,8 @@
 
 def normalise_kernel(order, own_ref, *refs):
     *block_refs, out_ref = refs
-    rows = [own_ref[...]] + [scaled(block_refs[order.index(j)][0]) for j in sorted(order)]
+    arrived = [ref[...] if i == 0 else scaled(ref[0]) for i, ref in enumerate(block_refs)]
+    rows = [own_ref[...]] + [arrived[order.index(j)] for j in sorted(order)]
     out_ref[...] = jnp.concatenate(rows, axis=0).astype(jnp.bfloat16)
 
 
@@ -141,6 +142,7 @@
     order = [radix - 1, *range(1, radix - 1)] if radix > 1 else []
     blocks = [swap(source, last, j) for j in order]
     own = call(own_kernel, shape((block, depth), full), (source,), 2**36, 2**27)
+    blocks[:1] = [call(own_kernel, shape((block, depth), full), (rows_of,)) for rows_of in blocks[:1]]
     size = radix * block
     kernel = functools.partial(normalise_kernel, order)
     blocks = [call(kernel, shape((size, depth), half), [own] + blocks, 2**34)]

time: 33.6 us -> 33.6 us (level)
    pallas_call x7 -> x8, Pallas kernels: 2.9 us -> 3 us  [call(): pl.pallas_call(kernel, out_shape=out_shape, in_specs=[VMEM] * len(args),...]
    unnamed x12 -> x16, local copies, waits for them, and re-layouts: 0.81 us -> 0.82 us
where the time goes in v8:
time: 33.6 us; the launch traced here: 33.4 us
  starting transfers between devices  17.2 us (51%)
  waiting for transfers between devices  12.2 us (36%)
  Pallas kernels  3 us (9%)
  local copies, waits for them, and re-layouts  0.82 us (2%)
    ppermute x12, starting transfers between devices, swap(): return lax.ppermute(value, ('layer', 'feat'), pairs)  17.2 us
    ppermute x12, waiting for transfers between devices, swap(): return lax.ppermute(value, ('layer', 'feat'), pairs)  11.8 us
    pallas_call x8, Pallas kernels, call(): pl.pallas_call(kernel, out_shape=out_shape, in_specs=[VMEM] * len(args),...  3 us
    unnamed x16, local copies, waits for them, and re-layouts  0.82 us
  transfers between devices with their start and end apart: 14, of which 11 were waited for; matrix products, arithmetic and copies ran while one was open for 0% of the time, Pallas kernels for 7%

profile of v8, /device:TPU:0, one launch (start us, length us, event | category | flops | bytes accessed | tf_op | source)
XLA Modules:
  0.0 33.4 jit_solution(11146681421491613683)
XLA Ops:
  0.0 5.0 %collective-permute-start = (f32[1,4,2048]{2,1,0:T(4,128)}, f32[1,4,2048]{2,1,0:T(4,128)S(1)}, u32[]{:S(2)}, u32[]{:S(2)}) collective-permute-start(f32[1,4,2048]{2,1,0:T(4,128)} %rows_ref.1), channel_id=1, source_target_pairs={{0,12},{1,13},{2,14},{3,15},{4,8},{5,9},{6,10},{7,11},{8,4},{9,5},... | collective-permute-start | bytes 98312 | tf_op jit(solution)/shard_map/ppermute | solution.py:134
  5.1 0.6 %collective-permute-start.1 = (f32[1,4,2048]{2,1,0:T(4,128)}, f32[1,4,2048]{2,1,0:T(4,128)S(1)}, u32[]{:S(2)}, u32[]{:S(2)}) collective-permute-start(f32[1,4,2048]{2,1,0:T(4,128)} %rows_ref.1), channel_id=1, source_target_pairs={{0,4},{1,5},{2,6},{3,7},{4,0},{5,1},{6,2},{7,3},{8,12},{9,13},{10,... | collective-permute-start | bytes 98312 | tf_op jit(solution)/shard_map/ppermute | solution.py:134
  5.6 0.8 %copy-done.3 = f32[1,4,2048]{2,1,0:T(4,128)S(1)} copy-done((f32[1,4,2048]{2,1,0:T(4,128)S(1)}, f32[1,4,2048]{2,1,0:T(4,128)}, u32[]{:S(2)}) %copy-start.3) | copy-done | bytes 32792
  6.5 0.6 %collective-permute-done.rows_ref = f32[1,4,2048]{2,1,0:T(4,128)S(1)} collective-permute-done((f32[1,4,2048]{2,1,0:T(4,128)}, f32[1,4,2048]{2,1,0:T(4,128)S(1)}, u32[]{:S(2)}, u32[]{:S(2)}) %collective-permute-start) | collective-permute-done | bytes 32800 | tf_op jit(solution)/shard_map/ppermute | solution.py:134
  7.3 2.8 %collective-permute-done.2.refs_2_ = f32[1,4,2048]{2,1,0:T(4,128)S(1)} collective-permute-done((f32[1,4,2048]{2,1,0:T(4,128)}, f32[1,4,2048]{2,1,0:T(4,128)S(1)}, u32[]{:S(2)}, u32[]{:S(2)}) %collective-permute-start.2) | collective-permute-done | bytes 32800 | tf_op jit(solution)/shard_map/ppermute | solution.py:134
  10.2 2.5 %collective-permute-start.5 = (bf16[16,2048]{1,0:T(8,128)(2,1)S(1)}, bf16[16,2048]{1,0:T(8,128)(2,1)S(1)}, u32[]{:S(2)}, u32[]{:S(2)}) collective-permute-start(bf16[16,2048]{1,0:T(8,128)(2,1)S(1)} %shard_map.75.refs_0_), channel_id=1, source_target_pairs={{0,3},{1,2},{2,1},{3,0},{4,7},{5,6},{6,5},{7,4},{8,11},{9,10},{10,... | collective-permute-start | bytes 196616 | tf_op jit(solution)/shard_map/ppermute | solution.py:134
  12.7 0.5 %collective-permute-start.4 = (bf16[16,2048]{1,0:T(8,128)(2,1)S(1)}, bf16[16,2048]{1,0:T(8,128)(2,1)S(1)}, u32[]{:S(2)}, u32[]{:S(2)}) collective-permute-start(bf16[16,2048]{1,0:T(8,128)(2,1)S(1)} %shard_map.75.refs_0_), channel_id=1, source_target_pairs={{0,2},{1,3},{2,0},{3,1},{4,6},{5,7},{6,4},{7,5},{8,10},{9,11},{10,... | collective-permute-start | bytes 196616 | tf_op jit(solution)/shard_map/ppermute | solution.py:134
  13.2 0.5 %collective-permute-start.3 = (bf16[16,2048]{1,0:T(8,128)(2,1)S(1)}, bf16[16,2048]{1,0:T(8,128)(2,1)S(1)}, u32[]{:S(2)}, u32[]{:S(2)}) collective-permute-start(bf16[16,2048]{1,0:T(8,128)(2,1)S(1)} %shard_map.75.refs_0_), channel_id=1, source_target_pairs={{0,1},{1,0},{2,3},{3,2},{4,5},{5,4},{6,7},{7,6},{8,9},{9,8},{10,11... | collective-permute-start | bytes 196616 | tf_op jit(solution)/shard_map/ppermute | solution.py:134
  13.8 1.7 %collective-permute-done.5.refs_3_ = bf16[16,2048]{1,0:T(8,128)(2,1)S(1)} collective-permute-done((bf16[16,2048]{1,0:T(8,128)(2,1)S(1)}, bf16[16,2048]{1,0:T(8,128)(2,1)S(1)}, u32[]{:S(2)}, u32[]{:S(2)}) %collective-permute-start.5) | collective-permute-done | bytes 65568 | tf_op jit(solution)/shard_map/ppermute | solution.py:134
  15.4 1.5 %collective-permute-done.4.refs_2_ = bf16[16,2048]{1,0:T(8,128)(2,1)S(1)} collective-permute-done((bf16[16,2048]{1,0:T(8,128)(2,1)S(1)}, bf16[16,2048]{1,0:T(8,128)(2,1)S(1)}, u32[]{:S(2)}, u32[]{:S(2)}) %collective-permute-start.4) | collective-permute-done | bytes 65568 | tf_op jit(solution)/shard_map/ppermute | solution.py:134
  17.0 0.5 %collective-permute-done.3.refs_1_ = bf16[16,2048]{1,0:T(8,128)(2,1)S(1)} collective-permute-done((bf16[16,2048]{1,0:T(8,128)(2,1)S(1)}, bf16[16,2048]{1,0:T(8,128)(2,1)S(1)}, u32[]{:S(2)}, u32[]{:S(2)}) %collective-permute-start.3) | collective-permute-done | bytes 65568 | tf_op jit(solution)/shard_map/ppermute | solution.py:134
  17.5 1.0 %shard_map.76.codes_ref = bf16[64,1536]{1,0:T(8,128)(2,1)S(1)} custom-call(bf16[16,2048]{1,0:T(8,128)(2,1)S(1)} %shard_map.75.refs_0_, bf16[16,2048]{1,0:T(8,128)(2,1)S(1)} %collective-permute-done.3.refs_1_, bf16[16,2048]{1,0:T(8,128)(2,1)S(1)} %collective-permute-done.4.refs_2_, bf16[16,2048]{1,0:T(8,128)(2,1)S(1)} %collective-permute-done.5.refs_3_, ...), custom_call_target="tpu_custom_call" | custom-call | flops 402653184 | bytes 262144 | tf_op jit(solution)/shard_map/pallas_call | solution.py:18
  18.6 1.0 %shard_map.77.own_ref = f32[64,2048]{1,0:T(8,128)S(1)} custom-call(bf16[64,1536]{1,0:T(8,128)(2,1)S(1)} %shard_map.76.codes_ref, bf16[1,1536,2048]{2,1,0:T(8,128)(2,1)S(1)} %bitcast.3), custom_call_target="tpu_custom_call" | custom-call | flops 402653184 | bytes 262144 | tf_op jit(solution)/shard_map/pallas_call | solution.py:18
  20.1 1.6 %collective-permute-start.8 = (bf16[16,2048]{1,0:T(8,128)(2,1)S(1)}, bf16[16,2048]{1,0:T(8,128)(2,1)S(1)}, u32[]{:S(2)}, u32[]{:S(2)}) collective-permute-start(bf16[16,2048]{1,0:T(8,128)(2,1)S(1)} %get-tuple-element.14), channel_id=1, source_target_pairs={{0,3},{1,2},{2,1},{3,0},{4,7},{5,6},{6,5},{7,4},{8,11},{9,10},{10,... | collective-permute-start | bytes 196616 | tf_op jit(solution)/shard_map/ppermute | solution.py:134
  21.6 0.5 %collective-permute-start.9 = (bf16[16,2048]{1,0:T(8,128)(2,1)S(1)}, bf16[16,2048]{1,0:T(8,128)(2,1)S(1)}, u32[]{:S(2)}, u32[]{:S(2)}) collective-permute-start(bf16[16,2048]{1,0:T(8,128)(2,1)S(1)} %get-tuple-element.15), channel_id=1, source_target_pairs={{0,2},{1,3},{2,0},{3,1},{4,6},{5,7},{6,4},{7,5},{8,10},{9,11},{10,... | collective-permute-start | bytes 196616 | tf_op jit(solution)/shard_map/ppermute | solution.py:134
  22.1 1.5 %collective-permute-start.10 = (bf16[16,2048]{1,0:T(8,128)(2,1)S(1)}, bf16[16,2048]{1,0:T(8,128)(2,1)S(1)}, u32[]{:S(2)}, u32[]{:S(2)}) collective-permute-start(bf16[16,2048]{1,0:T(8,128)(2,1)S(1)} %get-tuple-element.16), channel_id=1, source_target_pairs={{0,1},{1,0},{2,3},{3,2},{4,5},{5,4},{6,7},{7,6},{8,9},{9,8},{10,11... | collective-permute-start | bytes 196616 | tf_op jit(solution)/shard_map/ppermute | solution.py:134
  23.6 1.7 %collective-permute-done.8.refs_1_ = bf16[16,2048]{1,0:T(8,128)(2,1)S(1)} collective-permute-done((bf16[16,2048]{1,0:T(8,128)(2,1)S(1)}, bf16[16,2048]{1,0:T(8,128)(2,1)S(1)}, u32[]{:S(2)}, u32[]{:S(2)}) %collective-permute-start.8) | collective-permute-done | bytes 65568 | tf_op jit(solution)/shard_map/ppermute | solution.py:134
  25.3 0.7 %collective-permute-done.9.refs_2_ = bf16[16,2048]{1,0:T(8,128)(2,1)S(1)} collective-permute-done((bf16[16,2048]{1,0:T(8,128)(2,1)S(1)}, bf16[16,2048]{1,0:T(8,128)(2,1)S(1)}, u32[]{:S(2)}, u32[]{:S(2)}) %collective-permute-start.9) | collective-permute-done | bytes 65568 | tf_op jit(solution)/shard_map/ppermute | solution.py:134
  26.4 1.6 %collective-permute-start.11 = (bf16[4,2048]{1,0:T(4,128)(2,1)S(1)}, bf16[4,2048]{1,0:T(4,128)(2,1)S(1)}, u32[]{:S(2)}, u32[]{:S(2)}) collective-permute-start(bf16[4,2048]{1,0:T(4,128)(2,1)S(1)} %get-tuple-element.18), channel_id=1, source_target_pairs={{0,12},{1,13},{2,14},{3,15},{4,8},{5,9},{6,10},{7,11},{8,4},{9,5},... | collective-permute-start | bytes 49160 | tf_op jit(solution)/shard_map/ppermute | solution.py:134
  28.0 0.6 %collective-permute-start.12 = (bf16[4,2048]{1,0:T(4,128)(2,1)S(1)}, bf16[4,2048]{1,0:T(4,128)(2,1)S(1)}, u32[]{:S(2)}, u32[]{:S(2)}) collective-permute-start(bf16[4,2048]{1,0:T(4,128)(2,1)S(1)} %get-tuple-element.19), channel_id=1, source_target_pairs={{0,8},{1,9},{2,10},{3,11},{4,12},{5,13},{6,14},{7,15},{8,0},{9,1},... | collective-permute-start | bytes 49160 | tf_op jit(solution)/shard_map/ppermute | solution.py:134
  28.6 2.3 %collective-permute-start.13 = (bf16[4,2048]{1,0:T(4,128)(2,1)S(1)}, bf16[4,2048]{1,0:T(4,128)(2,1)S(1)}, u32[]{:S(2)}, u32[]{:S(2)}) collective-permute-start(bf16[4,2048]{1,0:T(4,128)(2,1)S(1)} %get-tuple-element.20), channel_id=1, source_target_pairs={{0,4},{1,5},{2,6},{3,7},{4,0},{5,1},{6,2},{7,3},{8,12},{9,13},{10,... | collective-permute-start | bytes 49160 | tf_op jit(solution)/shard_map/ppermute | solution.py:134
  30.9 1.1 %collective-permute-done.11.refs_1_ = bf16[4,2048]{1,0:T(4,128)(2,1)S(1)} collective-permute-done((bf16[4,2048]{1,0:T(4,128)(2,1)S(1)}, bf16[4,2048]{1,0:T(4,128)(2,1)S(1)}, u32[]{:S(2)}, u32[]{:S(2)}) %collective-permute-start.11) | collective-permute-done | bytes 16416 | tf_op jit(solution)/shard_map/ppermute | solution.py:134
  32.1 0.7 %collective-permute-done.12.refs_2_ = bf16[4,2048]{1,0:T(4,128)(2,1)S(1)} collective-permute-done((bf16[4,2048]{1,0:T(4,128)(2,1)S(1)}, bf16[4,2048]{1,0:T(4,128)(2,1)S(1)}, u32[]{:S(2)}, u32[]{:S(2)}) %collective-permute-start.12) | collective-permute-done | bytes 16416 | tf_op jit(solution)/shard_map/ppermute | solution.py:134
  32.8 0.6 %shard_map.80 = f32[1,4,2048]{2,1,0:T(4,128)} custom-call(bf16[4,2048]{1,0:T(4,128)(2,1)S(1)} %get-tuple-element.17.refs_0_, bf16[4,2048]{1,0:T(4,128)(2,1)S(1)} %collective-permute-done.11.refs_1_, bf16[4,2048]{1,0:T(4,128)(2,1)S(1)} %collective-permute-done.12.refs_2_, bf16[4,2048]{1,0:T(4,128)(2,1)S(1)} %collective-permute-done.13.refs_3_, ...), custom_call_target="tpu_custom_call" | custom-call | bytes 262144 | tf_op jit(solution)/shard_map/pallas_call | solution.py:18
  (30 shorter events, 1.3 us)
Async XLA Ops:
  0.0 7.2 %collective-permute-start = (f32[1,4,2048]{2,1,0:T(4,128)}, f32[1,4,2048]{2,1,0:T(4,128)S(1)}, u32[]{:S(2)}, u32[]{:S(2)}) collective-permute-start(f32[1,4,2048]{2,1,0:T(4,128)} %rows_ref.1), channel_id=1, source_target_pairs={{0,12},{1,13},{2,14},{3,15},{4,8},{5,9},{6,10},{7,11},{8,4},{9,5},... | collective-permute-start | bytes 98312 | tf_op jit(solution)/shard_map/ppermute | solution.py:134
  5.0 5.0 %collective-permute-start.2 = (f32[1,4,2048]{2,1,0:T(4,128)}, f32[1,4,2048]{2,1,0:T(4,128)S(1)}, u32[]{:S(2)}, u32[]{:S(2)}) collective-permute-start(f32[1,4,2048]{2,1,0:T(4,128)} %rows_ref.1), channel_id=1, source_target_pairs={{0,8},{1,9},{2,10},{3,11},{4,12},{5,13},{6,14},{7,15},{8,0},{9,1},... | collective-permute-start | bytes 98312 | tf_op jit(solution)/shard_map/ppermute | solution.py:134
  5.1 5.0 %collective-permute-start.1 = (f32[1,4,2048]{2,1,0:T(4,128)}, f32[1,4,2048]{2,1,0:T(4,128)S(1)}, u32[]{:S(2)}, u32[]{:S(2)}) collective-permute-start(f32[1,4,2048]{2,1,0:T(4,128)} %rows_ref.1), channel_id=1, source_target_pairs={{0,4},{1,5},{2,6},{3,7},{4,0},{5,1},{6,2},{7,3},{8,12},{9,13},{10,... | collective-permute-start | bytes 98312 | tf_op jit(solution)/shard_map/ppermute | solution.py:134
  5.6 14.4 %collective-permute-start.7 = (bf16[1,1536,2048]{2,1,0:T(8,128)(2,1)}, bf16[1,1536,2048]{2,1,0:T(8,128)(2,1)S(1)}, u32[]{:S(2)}, u32[]{:S(2)}) collective-permute-start(bf16[1,1536,2048]{2,1,0:T(8,128)(2,1)} %param.12), channel_id=1, source_target_pairs={{0,16},{16,0},{1,17},{17,1},{2,18},{18,2},{3,19},{19,3},{4,20},{20... | collective-permute-start | bytes 18874376 | tf_op jit(solution)/shard_map/ppermute | solution.py:137
  5.6 0.8 %copy-start.3 = (f32[1,4,2048]{2,1,0:T(4,128)S(1)}, f32[1,4,2048]{2,1,0:T(4,128)}, u32[]{:S(2)}) copy-start(f32[1,4,2048]{2,1,0:T(4,128)} %rows_ref.1) | copy-start | bytes 98308
  7.2 10.3 %slice-start = ((s8[6291456]{0:T(1024)(128)(4,1)}), s8[4194304]{0:T(1024)(128)(4,1)S(1)}, s32[]{:S(2)}) async-start(s8[6291456]{0:T(1024)(128)(4,1)} %bitcast), calls=%async_computation | async-start | bytes 8388608
  7.2 11.5 %slice-start.2 = ((s8[6291456]{0:T(1024)(128)(4,1)}), s8[4194304]{0:T(1024)(128)(4,1)S(1)}, s32[]{:S(2)}) async-start(s8[6291456]{0:T(1024)(128)(4,1)} %bitcast.2), calls=%async_computation.2 | async-start | bytes 8388608
  7.3 10.2 %slice-start.1 = ((s8[6291456]{0:T(1024)(128)(4,1)}), s8[2097152]{0:T(1024)(128)(4,1)S(1)}, s32[]{:S(2)}) async-start(s8[6291456]{0:T(1024)(128)(4,1)} %bitcast), calls=%async_computation.1 | async-start | bytes 4194304
  7.3 10.2 %copy-start.1 = (f32[1,1536]{1,0:T(1,128)S(1)}, f32[1,1536]{1,0:T(1,128)}, u32[]{:S(2)}) copy-start(f32[1,1536]{1,0:T(1,128)} %refs_5_.1) | copy-start | bytes 18436
  7.3 10.2 %copy-start.2 = (f32[1,1536]{1,0:T(1,128)S(1)}, f32[1,1536]{1,0:T(1,128)}, u32[]{:S(2)}) copy-start(f32[1,1536]{1,0:T(1,128)} %refs_6_.1) | copy-start | bytes 18436
  7.3 11.3 %slice-start.3 = ((s8[6291456]{0:T(1024)(128)(4,1)}), s8[2097152]{0:T(1024)(128)(4,1)S(1)}, s32[]{:S(2)}) async-start(s8[6291456]{0:T(1024)(128)(4,1)} %bitcast.2), calls=%async_computation.3 | async-start | bytes 4194304
  10.2 5.2 %collective-permute-start.5 = (bf16[16,2048]{1,0:T(8,128)(2,1)S(1)}, bf16[16,2048]{1,0:T(8,128)(2,1)S(1)}, u32[]{:S(2)}, u32[]{:S(2)}) collective-permute-start(bf16[16,2048]{1,0:T(8,128)(2,1)S(1)} %shard_map.75.refs_0_), channel_id=1, source_target_pairs={{0,3},{1,2},{2,1},{3,0},{4,7},{5,6},{6,5},{7,4},{8,11},{9,10},{10,... | collective-permute-start | bytes 196616 | tf_op jit(solution)/shard_map/ppermute | solution.py:134
  12.7 4.3 %collective-permute-start.4 = (bf16[16,2048]{1,0:T(8,128)(2,1)S(1)}, bf16[16,2048]{1,0:T(8,128)(2,1)S(1)}, u32[]{:S(2)}, u32[]{:S(2)}) collective-permute-start(bf16[16,2048]{1,0:T(8,128)(2,1)S(1)} %shard_map.75.refs_0_), channel_id=1, source_target_pairs={{0,2},{1,3},{2,0},{3,1},{4,6},{5,7},{6,4},{7,5},{8,10},{9,11},{10,... | collective-permute-start | bytes 196616 | tf_op jit(solution)/shard_map/ppermute | solution.py:134
  13.2 4.3 %collective-permute-start.3 = (bf16[16,2048]{1,0:T(8,128)(2,1)S(1)}, bf16[16,2048]{1,0:T(8,128)(2,1)S(1)}, u32[]{:S(2)}, u32[]{:S(2)}) collective-permute-start(bf16[16,2048]{1,0:T(8,128)(2,1)S(1)} %shard_map.75.refs_0_), channel_id=1, source_target_pairs={{0,1},{1,0},{2,3},{3,2},{4,5},{5,4},{6,7},{7,6},{8,9},{9,8},{10,11... | collective-permute-start | bytes 196616 | tf_op jit(solution)/shard_map/ppermute | solution.py:134
  18.5 14.3 %copy-start = (f32[1,4,2048]{2,1,0:T(4,128)S(1)}, f32[1,4,2048]{2,1,0:T(4,128)}, u32[]{:S(2)}) copy-start(f32[1,4,2048]{2,1,0:T(4,128)} %refs_4_.3) | copy-start | bytes 98308
  18.5 1.5 %collective-permute-start.6 = (bf16[64,1536]{1,0:T(8,128)(2,1)S(1)}, bf16[64,1536]{1,0:T(8,128)(2,1)S(1)}, u32[]{:S(2)}, u32[]{:S(2)}) collective-permute-start(bf16[64,1536]{1,0:T(8,128)(2,1)S(1)} %shard_map.76.codes_ref), channel_id=1, source_target_pairs={{0,16},{16,0},{1,17},{17,1},{2,18},{18,2},{3,19},{19,3},{4,20},{20... | collective-permute-start | bytes 589832 | tf_op jit(solution)/shard_map/ppermute | solution.py:137
  20.1 5.2 %collective-permute-start.8 = (bf16[16,2048]{1,0:T(8,128)(2,1)S(1)}, bf16[16,2048]{1,0:T(8,128)(2,1)S(1)}, u32[]{:S(2)}, u32[]{:S(2)}) collective-permute-start(bf16[16,2048]{1,0:T(8,128)(2,1)S(1)} %get-tuple-element.14), channel_id=1, source_target_pairs={{0,3},{1,2},{2,1},{3,0},{4,7},{5,6},{6,5},{7,4},{8,11},{9,10},{10,... | collective-permute-start | bytes 196616 | tf_op jit(solution)/shard_map/ppermute | solution.py:134
  21.6 4.4 %collective-permute-start.9 = (bf16[16,2048]{1,0:T(8,128)(2,1)S(1)}, bf16[16,2048]{1,0:T(8,128)(2,1)S(1)}, u32[]{:S(2)}, u32[]{:S(2)}) collective-permute-start(bf16[16,2048]{1,0:T(8,128)(2,1)S(1)} %get-tuple-element.15), channel_id=1, source_target_pairs={{0,2},{1,3},{2,0},{3,1},{4,6},{5,7},{6,4},{7,5},{8,10},{9,11},{10,... | collective-permute-start | bytes 196616 | tf_op jit(solution)/shard_map/ppermute | solution.py:134
  22.1 4.3 %collective-permute-start.10 = (bf16[16,2048]{1,0:T(8,128)(2,1)S(1)}, bf16[16,2048]{1,0:T(8,128)(2,1)S(1)}, u32[]{:S(2)}, u32[]{:S(2)}) collective-permute-start(bf16[16,2048]{1,0:T(8,128)(2,1)S(1)} %get-tuple-element.16), channel_id=1, source_target_pairs={{0,1},{1,0},{2,3},{3,2},{4,5},{5,4},{6,7},{7,6},{8,9},{9,8},{10,11... | collective-permute-start | bytes 196616 | tf_op jit(solution)/shard_map/ppermute | solution.py:134
  26.4 5.6 %collective-permute-start.11 = (bf16[4,2048]{1,0:T(4,128)(2,1)S(1)}, bf16[4,2048]{1,0:T(4,128)(2,1)S(1)}, u32[]{:S(2)}, u32[]{:S(2)}) collective-permute-start(bf16[4,2048]{1,0:T(4,128)(2,1)S(1)} %get-tuple-element.18), channel_id=1, source_target_pairs={{0,12},{1,13},{2,14},{3,15},{4,8},{5,9},{6,10},{7,11},{8,4},{9,5},... | collective-permute-start | bytes 49160 | tf_op jit(solution)/shard_map/ppermute | solution.py:134
  28.0 4.7 %collective-permute-start.12 = (bf16[4,2048]{1,0:T(4,128)(2,1)S(1)}, bf16[4,2048]{1,0:T(4,128)(2,1)S(1)}, u32[]{:S(2)}, u32[]{:S(2)}) collective-permute-start(bf16[4,2048]{1,0:T(4,128)(2,1)S(1)} %get-tuple-element.19), channel_id=1, source_target_pairs={{0,8},{1,9},{2,10},{3,11},{4,12},{5,13},{6,14},{7,15},{8,0},{9,1},... | collective-permute-start | bytes 49160 | tf_op jit(solution)/shard_map/ppermute | solution.py:134
  28.6 4.2 %collective-permute-start.13 = (bf16[4,2048]{1,0:T(4,128)(2,1)S(1)}, bf16[4,2048]{1,0:T(4,128)(2,1)S(1)}, u32[]{:S(2)}, u32[]{:S(2)}) collective-permute-start(bf16[4,2048]{1,0:T(4,128)(2,1)S(1)} %get-tuple-element.20), channel_id=1, source_target_pairs={{0,4},{1,5},{2,6},{3,7},{4,0},{5,1},{6,2},{7,3},{8,12},{9,13},{10,... | collective-permute-start | bytes 49160 | tf_op jit(solution)/shard_map/ppermute | solution.py:134

commit v9 on v6

--- a/solution.py
+++ b/solution.py
@@ -14,11 +14,11 @@
 TALL = 128
 
 
-def call(kernel, out_shape, args, flops=0, moved=2**18, aliases=()):
+def call(kernel, out_shape, args, flops=0, moved=2**18, aliases={}):
     return pl.pallas_call(
         kernel,
         out_shape=out_shape,
-        input_output_aliases=dict(aliases),
+        input_output_aliases=aliases,
         in_specs=[VMEM] * len(args),
         out_specs=jax.tree.map(lambda _: VMEM, out_shape),
         compiler_params=pltpu.CompilerParams(vmem_limit_bytes=GRANT),
@@ -62,9 +62,15 @@
 
 
 def decode_kernel(codes_ref, dec_ref, own_ref, *part_refs):
-    own = dot(codes_ref[...], dec_ref[0])
-    own_ref[...] = own
-    cut(own, part_refs)
+    first = lax.axis_index("layer") == 0
+
+    @pl.when(first)
+    def _():
+        cut(dot(codes_ref[...], dec_ref[0]), part_refs)
+
+    @pl.when(jnp.logical_not(first))
+    def _():
+        own_ref[...] = dot(codes_ref[...], dec_ref[0])
 
 
 def cut(total, part_refs):
@@ -89,11 +95,6 @@
 
 
 def gather_up_kernel(*refs):
-    *block_refs, out_ref = refs
-    out_ref[...] = added(block_refs)
-
-
-def add_kernel(*refs):
     *block_refs, out_ref = refs
     out_ref[...] = added(block_refs)
 
@@ -165,16 +166,12 @@
     pieces = (shape((size, depth), half),) * radices[0]
     own, *parts = call(decode_kernel, (shape((rows, depth), full), *pieces), (codes, dec_self), work)
     kernel = functools.partial(join_kernel, places)
-    operands = (own, before, arrived_dec, *parts)
-    parts = call(kernel, pieces, operands, work, aliases=[(3 + i, i) for i in range(radices[0])])
+    parts = call(kernel, pieces, (own, before, arrived_dec, *parts), work, aliases={3 + i: i for i in range(radices[0])})
     for stage, radix in enumerate(radices):
         blocks = [parts[0]] + [swap(parts[j], stage, j) for j in reversed(range(1, radix))]
-        if len(blocks) > 2:
-            sofar = call(add_kernel, shape(parts[0].shape, full), blocks[:2])
-            blocks = [sofar] + blocks[2:]
         if stage < last:
             size //= radices[stage + 1]
-            kernel = functools.partial(split_kernel, len(blocks))
+            kernel = functools.partial(split_kernel, radix)
             parts = call(kernel, (shape((size, depth), half),) * radices[stage + 1], blocks)
     return call(finish_kernel, shape(target.shape, full), (*blocks, target))
 

time: 33.5 us -> 33.5 us (level)
    pallas_call x9 -> x7, Pallas kernels: 2.89 us -> 2.89 us  [call(): pl.pallas_call(kernel, out_shape=out_shape, input_output_aliases=aliases,...]
where the time goes in v9:
time: 33.5 us; the launch traced here: 33.3 us
  starting transfers between devices  17.2 us (51%)
  waiting for transfers between devices  12.4 us (37%)
  Pallas kernels  2.89 us (9%)
  local copies, waits for them, and re-layouts  0.81 us (2%)
    ppermute x12, starting transfers between devices, swap(): return lax.ppermute(value, ('layer', 'feat'), pairs)  17.1 us
    ppermute x12, waiting for transfers between devices, swap(): return lax.ppermute(value, ('layer', 'feat'), pairs)  11.9 us
    pallas_call x7, Pallas kernels, call(): pl.pallas_call(kernel, out_shape=out_shape, input_output_aliases=aliases,...  2.89 us
    unnamed x12, local copies, waits for them, and re-layouts  0.81 us
  transfers between devices with their start and end apart: 14, of which 11 were waited for; matrix products, arithmetic and copies ran while one was open for 0% of the time, Pallas kernels for 7%

profile of v9, /device:TPU:0, one launch (start us, length us, event | category | flops | bytes accessed | tf_op | source)
XLA Modules:
  0.0 33.3 jit_solution(8117912183946782944)
XLA Ops:
  0.0 5.0 %collective-permute-start = (f32[1,4,2048]{2,1,0:T(4,128)}, f32[1,4,2048]{2,1,0:T(4,128)S(1)}, u32[]{:S(2)}, u32[]{:S(2)}) collective-permute-start(f32[1,4,2048]{2,1,0:T(4,128)} %rows_ref.1), channel_id=1, source_target_pairs={{0,12},{1,13},{2,14},{3,15},{4,8},{5,9},{6,10},{7,11},{8,4},{9,5},... | collective-permute-start | bytes 98312 | tf_op jit(solution)/shard_map/ppermute | solution.py:143
  5.1 0.6 %collective-permute-start.1 = (f32[1,4,2048]{2,1,0:T(4,128)}, f32[1,4,2048]{2,1,0:T(4,128)S(1)}, u32[]{:S(2)}, u32[]{:S(2)}) collective-permute-start(f32[1,4,2048]{2,1,0:T(4,128)} %rows_ref.1), channel_id=1, source_target_pairs={{0,4},{1,5},{2,6},{3,7},{4,0},{5,1},{6,2},{7,3},{8,12},{9,13},{10,... | collective-permute-start | bytes 98312 | tf_op jit(solution)/shard_map/ppermute | solution.py:143
  5.6 0.8 %copy-done.5 = f32[1,4,2048]{2,1,0:T(4,128)S(1)} copy-done((f32[1,4,2048]{2,1,0:T(4,128)S(1)}, f32[1,4,2048]{2,1,0:T(4,128)}, u32[]{:S(2)}) %copy-start.5) | copy-done | bytes 32792
  6.5 0.6 %collective-permute-done.refs_0_ = f32[1,4,2048]{2,1,0:T(4,128)S(1)} collective-permute-done((f32[1,4,2048]{2,1,0:T(4,128)}, f32[1,4,2048]{2,1,0:T(4,128)S(1)}, u32[]{:S(2)}, u32[]{:S(2)}) %collective-permute-start) | collective-permute-done | bytes 32800 | tf_op jit(solution)/shard_map/ppermute | solution.py:143
  7.2 2.9 %collective-permute-done.2.refs_2_ = f32[1,4,2048]{2,1,0:T(4,128)S(1)} collective-permute-done((f32[1,4,2048]{2,1,0:T(4,128)}, f32[1,4,2048]{2,1,0:T(4,128)S(1)}, u32[]{:S(2)}, u32[]{:S(2)}) %collective-permute-start.2) | collective-permute-done | bytes 32800 | tf_op jit(solution)/shard_map/ppermute | solution.py:143
  10.2 2.5 %collective-permute-start.5 = (bf16[16,2048]{1,0:T(8,128)(2,1)S(1)}, bf16[16,2048]{1,0:T(8,128)(2,1)S(1)}, u32[]{:S(2)}, u32[]{:S(2)}) collective-permute-start(bf16[16,2048]{1,0:T(8,128)(2,1)S(1)} %shard_map.74.refs_0_), channel_id=1, source_target_pairs={{0,3},{1,2},{2,1},{3,0},{4,7},{5,6},{6,5},{7,4},{8,11},{9,10},{10,... | collective-permute-start | bytes 196616 | tf_op jit(solution)/shard_map/ppermute | solution.py:143
  12.7 0.5 %collective-permute-start.4 = (bf16[16,2048]{1,0:T(8,128)(2,1)S(1)}, bf16[16,2048]{1,0:T(8,128)(2,1)S(1)}, u32[]{:S(2)}, u32[]{:S(2)}) collective-permute-start(bf16[16,2048]{1,0:T(8,128)(2,1)S(1)} %shard_map.74.refs_0_), channel_id=1, source_target_pairs={{0,2},{1,3},{2,0},{3,1},{4,6},{5,7},{6,4},{7,5},{8,10},{9,11},{10,... | collective-permute-start | bytes 196616 | tf_op jit(solution)/shard_map/ppermute | solution.py:143
  13.2 0.5 %collective-permute-start.3 = (bf16[16,2048]{1,0:T(8,128)(2,1)S(1)}, bf16[16,2048]{1,0:T(8,128)(2,1)S(1)}, u32[]{:S(2)}, u32[]{:S(2)}) collective-permute-start(bf16[16,2048]{1,0:T(8,128)(2,1)S(1)} %shard_map.74.refs_0_), channel_id=1, source_target_pairs={{0,1},{1,0},{2,3},{3,2},{4,5},{5,4},{6,7},{7,6},{8,9},{9,8},{10,11... | collective-permute-start | bytes 196616 | tf_op jit(solution)/shard_map/ppermute | solution.py:143
  13.8 1.7 %collective-permute-done.5.refs_3_ = bf16[16,2048]{1,0:T(8,128)(2,1)S(1)} collective-permute-done((bf16[16,2048]{1,0:T(8,128)(2,1)S(1)}, bf16[16,2048]{1,0:T(8,128)(2,1)S(1)}, u32[]{:S(2)}, u32[]{:S(2)}) %collective-permute-start.5) | collective-permute-done | bytes 65568 | tf_op jit(solution)/shard_map/ppermute | solution.py:143
  15.4 1.5 %collective-permute-done.4.refs_2_ = bf16[16,2048]{1,0:T(8,128)(2,1)S(1)} collective-permute-done((bf16[16,2048]{1,0:T(8,128)(2,1)S(1)}, bf16[16,2048]{1,0:T(8,128)(2,1)S(1)}, u32[]{:S(2)}, u32[]{:S(2)}) %collective-permute-start.4) | collective-permute-done | bytes 65568 | tf_op jit(solution)/shard_map/ppermute | solution.py:143
  17.0 0.5 %collective-permute-done.3.refs_1_ = bf16[16,2048]{1,0:T(8,128)(2,1)S(1)} collective-permute-done((bf16[16,2048]{1,0:T(8,128)(2,1)S(1)}, bf16[16,2048]{1,0:T(8,128)(2,1)S(1)}, u32[]{:S(2)}, u32[]{:S(2)}) %collective-permute-start.3) | collective-permute-done | bytes 65568 | tf_op jit(solution)/shard_map/ppermute | solution.py:143
  17.5 1.0 %shard_map.75.codes_ref = bf16[64,1536]{1,0:T(8,128)(2,1)S(1)} custom-call(bf16[16,2048]{1,0:T(8,128)(2,1)S(1)} %shard_map.74.refs_0_, bf16[16,2048]{1,0:T(8,128)(2,1)S(1)} %collective-permute-done.3.refs_1_, bf16[16,2048]{1,0:T(8,128)(2,1)S(1)} %collective-permute-done.4.refs_2_, bf16[16,2048]{1,0:T(8,128)(2,1)S(1)} %collective-permute-done.5.refs_3_, ...), custom_call_target="tpu_custom_call" | custom-call | flops 402653184 | bytes 262144 | tf_op jit(solution)/shard_map/pallas_call | solution.py:18
  18.6 1.0 %shard_map.76 = (f32[64,2048]{1,0:T(8,128)S(1)}, bf16[16,2048]{1,0:T(8,128)(2,1)S(1)}, bf16[16,2048]{1,0:T(8,128)(2,1)S(1)}, bf16[16,2048]{1,0:T(8,128)(2,1)S(1)}, bf16[16,2048]{1,0:T(8,128)(2,1)S(1)}) custom-call(bf16[64,1536]{1,0:T(8,128)(2,1)S(1)} %shard_map.75.codes_ref, bf16[1,1536,2048]{2,1,0:T(8,128)(2,1)S(1)} %copy-done), custom_call_target="tpu_custom_call" | custom-call | flops 402653184 | bytes 262144 | tf_op jit(solution)/shard_map/pallas_call | solution.py:18
  20.0 1.5 %collective-permute-start.8 = (bf16[16,2048]{1,0:T(8,128)(2,1)S(1)}, bf16[16,2048]{1,0:T(8,128)(2,1)S(1)}, u32[]{:S(2)}, u32[]{:S(2)}) collective-permute-start(bf16[16,2048]{1,0:T(8,128)(2,1)S(1)} %get-tuple-element.24), channel_id=1, source_target_pairs={{0,3},{1,2},{2,1},{3,0},{4,7},{5,6},{6,5},{7,4},{8,11},{9,10},{10,... | collective-permute-start | bytes 196616 | tf_op jit(solution)/shard_map/ppermute | solution.py:143
  21.5 0.5 %collective-permute-start.9 = (bf16[16,2048]{1,0:T(8,128)(2,1)S(1)}, bf16[16,2048]{1,0:T(8,128)(2,1)S(1)}, u32[]{:S(2)}, u32[]{:S(2)}) collective-permute-start(bf16[16,2048]{1,0:T(8,128)(2,1)S(1)} %get-tuple-element.25), channel_id=1, source_target_pairs={{0,2},{1,3},{2,0},{3,1},{4,6},{5,7},{6,4},{7,5},{8,10},{9,11},{10,... | collective-permute-start | bytes 196616 | tf_op jit(solution)/shard_map/ppermute | solution.py:143
  22.0 1.5 %collective-permute-start.10 = (bf16[16,2048]{1,0:T(8,128)(2,1)S(1)}, bf16[16,2048]{1,0:T(8,128)(2,1)S(1)}, u32[]{:S(2)}, u32[]{:S(2)}) collective-permute-start(bf16[16,2048]{1,0:T(8,128)(2,1)S(1)} %get-tuple-element.26), channel_id=1, source_target_pairs={{0,1},{1,0},{2,3},{3,2},{4,5},{5,4},{6,7},{7,6},{8,9},{9,8},{10,11... | collective-permute-start | bytes 196616 | tf_op jit(solution)/shard_map/ppermute | solution.py:143
  23.5 1.7 %collective-permute-done.8.refs_1_ = bf16[16,2048]{1,0:T(8,128)(2,1)S(1)} collective-permute-done((bf16[16,2048]{1,0:T(8,128)(2,1)S(1)}, bf16[16,2048]{1,0:T(8,128)(2,1)S(1)}, u32[]{:S(2)}, u32[]{:S(2)}) %collective-permute-start.8) | collective-permute-done | bytes 65568 | tf_op jit(solution)/shard_map/ppermute | solution.py:143
  25.2 0.7 %collective-permute-done.9.refs_2_ = bf16[16,2048]{1,0:T(8,128)(2,1)S(1)} collective-permute-done((bf16[16,2048]{1,0:T(8,128)(2,1)S(1)}, bf16[16,2048]{1,0:T(8,128)(2,1)S(1)}, u32[]{:S(2)}, u32[]{:S(2)}) %collective-permute-start.9) | collective-permute-done | bytes 65568 | tf_op jit(solution)/shard_map/ppermute | solution.py:143
  26.3 1.6 %collective-permute-start.11 = (bf16[4,2048]{1,0:T(4,128)(2,1)S(1)}, bf16[4,2048]{1,0:T(4,128)(2,1)S(1)}, u32[]{:S(2)}, u32[]{:S(2)}) collective-permute-start(bf16[4,2048]{1,0:T(4,128)(2,1)S(1)} %get-tuple-element.28), channel_id=1, source_target_pairs={{0,12},{1,13},{2,14},{3,15},{4,8},{5,9},{6,10},{7,11},{8,4},{9,5},... | collective-permute-start | bytes 49160 | tf_op jit(solution)/shard_map/ppermute | solution.py:143
  27.9 0.6 %collective-permute-start.12 = (bf16[4,2048]{1,0:T(4,128)(2,1)S(1)}, bf16[4,2048]{1,0:T(4,128)(2,1)S(1)}, u32[]{:S(2)}, u32[]{:S(2)}) collective-permute-start(bf16[4,2048]{1,0:T(4,128)(2,1)S(1)} %get-tuple-element.29), channel_id=1, source_target_pairs={{0,8},{1,9},{2,10},{3,11},{4,12},{5,13},{6,14},{7,15},{8,0},{9,1},... | collective-permute-start | bytes 49160 | tf_op jit(solution)/shard_map/ppermute | solution.py:143
  28.5 2.3 %collective-permute-start.13 = (bf16[4,2048]{1,0:T(4,128)(2,1)S(1)}, bf16[4,2048]{1,0:T(4,128)(2,1)S(1)}, u32[]{:S(2)}, u32[]{:S(2)}) collective-permute-start(bf16[4,2048]{1,0:T(4,128)(2,1)S(1)} %get-tuple-element.30), channel_id=1, source_target_pairs={{0,4},{1,5},{2,6},{3,7},{4,0},{5,1},{6,2},{7,3},{8,12},{9,13},{10,... | collective-permute-start | bytes 49160 | tf_op jit(solution)/shard_map/ppermute | solution.py:143
  30.8 1.1 %collective-permute-done.11.refs_1_ = bf16[4,2048]{1,0:T(4,128)(2,1)S(1)} collective-permute-done((bf16[4,2048]{1,0:T(4,128)(2,1)S(1)}, bf16[4,2048]{1,0:T(4,128)(2,1)S(1)}, u32[]{:S(2)}, u32[]{:S(2)}) %collective-permute-start.11) | collective-permute-done | bytes 16416 | tf_op jit(solution)/shard_map/ppermute | solution.py:143
  32.0 0.7 %collective-permute-done.12.refs_2_ = bf16[4,2048]{1,0:T(4,128)(2,1)S(1)} collective-permute-done((bf16[4,2048]{1,0:T(4,128)(2,1)S(1)}, bf16[4,2048]{1,0:T(4,128)(2,1)S(1)}, u32[]{:S(2)}, u32[]{:S(2)}) %collective-permute-start.12) | collective-permute-done | bytes 16416 | tf_op jit(solution)/shard_map/ppermute | solution.py:143
  32.7 0.6 %shard_map.79 = f32[1,4,2048]{2,1,0:T(4,128)} custom-call(bf16[4,2048]{1,0:T(4,128)(2,1)S(1)} %get-tuple-element.27.refs_0_, bf16[4,2048]{1,0:T(4,128)(2,1)S(1)} %collective-permute-done.11.refs_1_, bf16[4,2048]{1,0:T(4,128)(2,1)S(1)} %collective-permute-done.12.refs_2_, bf16[4,2048]{1,0:T(4,128)(2,1)S(1)} %collective-permute-done.13.refs_3_, ...), custom_call_target="tpu_custom_call" | custom-call | bytes 262144 | tf_op jit(solution)/shard_map/pallas_call | solution.py:18
  (23 shorter events, 1.2 us)
Async XLA Ops:
  0.0 7.2 %collective-permute-start = (f32[1,4,2048]{2,1,0:T(4,128)}, f32[1,4,2048]{2,1,0:T(4,128)S(1)}, u32[]{:S(2)}, u32[]{:S(2)}) collective-permute-start(f32[1,4,2048]{2,1,0:T(4,128)} %rows_ref.1), channel_id=1, source_target_pairs={{0,12},{1,13},{2,14},{3,15},{4,8},{5,9},{6,10},{7,11},{8,4},{9,5},... | collective-permute-start | bytes 98312 | tf_op jit(solution)/shard_map/ppermute | solution.py:143
  5.0 5.0 %collective-permute-start.2 = (f32[1,4,2048]{2,1,0:T(4,128)}, f32[1,4,2048]{2,1,0:T(4,128)S(1)}, u32[]{:S(2)}, u32[]{:S(2)}) collective-permute-start(f32[1,4,2048]{2,1,0:T(4,128)} %rows_ref.1), channel_id=1, source_target_pairs={{0,8},{1,9},{2,10},{3,11},{4,12},{5,13},{6,14},{7,15},{8,0},{9,1},... | collective-permute-start | bytes 98312 | tf_op jit(solution)/shard_map/ppermute | solution.py:143
  5.1 5.0 %collective-permute-start.1 = (f32[1,4,2048]{2,1,0:T(4,128)}, f32[1,4,2048]{2,1,0:T(4,128)S(1)}, u32[]{:S(2)}, u32[]{:S(2)}) collective-permute-start(f32[1,4,2048]{2,1,0:T(4,128)} %rows_ref.1), channel_id=1, source_target_pairs={{0,4},{1,5},{2,6},{3,7},{4,0},{5,1},{6,2},{7,3},{8,12},{9,13},{10,... | collective-permute-start | bytes 98312 | tf_op jit(solution)/shard_map/ppermute | solution.py:143
  5.6 14.4 %collective-permute-start.7 = (bf16[1,1536,2048]{2,1,0:T(8,128)(2,1)}, bf16[1,1536,2048]{2,1,0:T(8,128)(2,1)S(1)}, u32[]{:S(2)}, u32[]{:S(2)}) collective-permute-start(bf16[1,1536,2048]{2,1,0:T(8,128)(2,1)} %param.12), channel_id=1, source_target_pairs={{0,16},{16,0},{1,17},{17,1},{2,18},{18,2},{3,19},{19,3},{4,20},{20... | collective-permute-start | bytes 18874376 | tf_op jit(solution)/shard_map/ppermute | solution.py:146
  5.6 0.8 %copy-start.5 = (f32[1,4,2048]{2,1,0:T(4,128)S(1)}, f32[1,4,2048]{2,1,0:T(4,128)}, u32[]{:S(2)}) copy-start(f32[1,4,2048]{2,1,0:T(4,128)} %rows_ref.1) | copy-start | bytes 98308
  6.5 11.0 %copy-start.1 = (bf16[1,2048,1536]{2,1,0:T(8,128)(2,1)S(1)}, bf16[1,2048,1536]{2,1,0:T(8,128)(2,1)}, u32[]{:S(2)}) copy-start(bf16[1,2048,1536]{2,1,0:T(8,128)(2,1)} %refs_4_.2) | copy-start | bytes 18874372
  6.5 11.0 %copy-start.3 = (f32[1,1536]{1,0:T(1,128)S(1)}, f32[1,1536]{1,0:T(1,128)}, u32[]{:S(2)}) copy-start(f32[1,1536]{1,0:T(1,128)} %refs_5_.1) | copy-start | bytes 18436
  6.5 11.0 %copy-start.4 = (f32[1,1536]{1,0:T(1,128)S(1)}, f32[1,1536]{1,0:T(1,128)}, u32[]{:S(2)}) copy-start(f32[1,1536]{1,0:T(1,128)} %refs_6_.1) | copy-start | bytes 18436
  10.2 8.4 %copy-start = (bf16[1,1536,2048]{2,1,0:T(8,128)(2,1)S(1)}, bf16[1,1536,2048]{2,1,0:T(8,128)(2,1)}, u32[]{:S(2)}) copy-start(bf16[1,1536,2048]{2,1,0:T(8,128)(2,1)} %dec_ref.1) | copy-start | bytes 18874372
  10.2 5.2 %collective-permute-start.5 = (bf16[16,2048]{1,0:T(8,128)(2,1)S(1)}, bf16[16,2048]{1,0:T(8,128)(2,1)S(1)}, u32[]{:S(2)}, u32[]{:S(2)}) collective-permute-start(bf16[16,2048]{1,0:T(8,128)(2,1)S(1)} %shard_map.74.refs_0_), channel_id=1, source_target_pairs={{0,3},{1,2},{2,1},{3,0},{4,7},{5,6},{6,5},{7,4},{8,11},{9,10},{10,... | collective-permute-start | bytes 196616 | tf_op jit(solution)/shard_map/ppermute | solution.py:143
  12.7 4.3 %collective-permute-start.4 = (bf16[16,2048]{1,0:T(8,128)(2,1)S(1)}, bf16[16,2048]{1,0:T(8,128)(2,1)S(1)}, u32[]{:S(2)}, u32[]{:S(2)}) collective-permute-start(bf16[16,2048]{1,0:T(8,128)(2,1)S(1)} %shard_map.74.refs_0_), channel_id=1, source_target_pairs={{0,2},{1,3},{2,0},{3,1},{4,6},{5,7},{6,4},{7,5},{8,10},{9,11},{10,... | collective-permute-start | bytes 196616 | tf_op jit(solution)/shard_map/ppermute | solution.py:143
  13.2 4.3 %collective-permute-start.3 = (bf16[16,2048]{1,0:T(8,128)(2,1)S(1)}, bf16[16,2048]{1,0:T(8,128)(2,1)S(1)}, u32[]{:S(2)}, u32[]{:S(2)}) collective-permute-start(bf16[16,2048]{1,0:T(8,128)(2,1)S(1)} %shard_map.74.refs_0_), channel_id=1, source_target_pairs={{0,1},{1,0},{2,3},{3,2},{4,5},{5,4},{6,7},{7,6},{8,9},{9,8},{10,11... | collective-permute-start | bytes 196616 | tf_op jit(solution)/shard_map/ppermute | solution.py:143
  18.5 14.2 %copy-start.2 = (f32[1,4,2048]{2,1,0:T(4,128)S(1)}, f32[1,4,2048]{2,1,0:T(4,128)}, u32[]{:S(2)}) copy-start(f32[1,4,2048]{2,1,0:T(4,128)} %refs_4_.3) | copy-start | bytes 98308
  18.5 1.5 %collective-permute-start.6 = (bf16[64,1536]{1,0:T(8,128)(2,1)S(1)}, bf16[64,1536]{1,0:T(8,128)(2,1)S(1)}, u32[]{:S(2)}, u32[]{:S(2)}) collective-permute-start(bf16[64,1536]{1,0:T(8,128)(2,1)S(1)} %shard_map.75.codes_ref), channel_id=1, source_target_pairs={{0,16},{16,0},{1,17},{17,1},{2,18},{18,2},{3,19},{19,3},{4,20},{20... | collective-permute-start | bytes 589832 | tf_op jit(solution)/shard_map/ppermute | solution.py:146
  20.0 5.2 %collective-permute-start.8 = (bf16[16,2048]{1,0:T(8,128)(2,1)S(1)}, bf16[16,2048]{1,0:T(8,128)(2,1)S(1)}, u32[]{:S(2)}, u32[]{:S(2)}) collective-permute-start(bf16[16,2048]{1,0:T(8,128)(2,1)S(1)} %get-tuple-element.24), channel_id=1, source_target_pairs={{0,3},{1,2},{2,1},{3,0},{4,7},{5,6},{6,5},{7,4},{8,11},{9,10},{10,... | collective-permute-start | bytes 196616 | tf_op jit(solution)/shard_map/ppermute | solution.py:143
  21.5 4.4 %collective-permute-start.9 = (bf16[16,2048]{1,0:T(8,128)(2,1)S(1)}, bf16[16,2048]{1,0:T(8,128)(2,1)S(1)}, u32[]{:S(2)}, u32[]{:S(2)}) collective-permute-start(bf16[16,2048]{1,0:T(8,128)(2,1)S(1)} %get-tuple-element.25), channel_id=1, source_target_pairs={{0,2},{1,3},{2,0},{3,1},{4,6},{5,7},{6,4},{7,5},{8,10},{9,11},{10,... | collective-permute-start | bytes 196616 | tf_op jit(solution)/shard_map/ppermute | solution.py:143
  22.0 4.3 %collective-permute-start.10 = (bf16[16,2048]{1,0:T(8,128)(2,1)S(1)}, bf16[16,2048]{1,0:T(8,128)(2,1)S(1)}, u32[]{:S(2)}, u32[]{:S(2)}) collective-permute-start(bf16[16,2048]{1,0:T(8,128)(2,1)S(1)} %get-tuple-element.26), channel_id=1, source_target_pairs={{0,1},{1,0},{2,3},{3,2},{4,5},{5,4},{6,7},{7,6},{8,9},{9,8},{10,11... | collective-permute-start | bytes 196616 | tf_op jit(solution)/shard_map/ppermute | solution.py:143
  26.3 5.6 %collective-permute-start.11 = (bf16[4,2048]{1,0:T(4,128)(2,1)S(1)}, bf16[4,2048]{1,0:T(4,128)(2,1)S(1)}, u32[]{:S(2)}, u32[]{:S(2)}) collective-permute-start(bf16[4,2048]{1,0:T(4,128)(2,1)S(1)} %get-tuple-element.28), channel_id=1, source_target_pairs={{0,12},{1,13},{2,14},{3,15},{4,8},{5,9},{6,10},{7,11},{8,4},{9,5},... | collective-permute-start | bytes 49160 | tf_op jit(solution)/shard_map/ppermute | solution.py:143
  27.9 4.7 %collective-permute-start.12 = (bf16[4,2048]{1,0:T(4,128)(2,1)S(1)}, bf16[4,2048]{1,0:T(4,128)(2,1)S(1)}, u32[]{:S(2)}, u32[]{:S(2)}) collective-permute-start(bf16[4,2048]{1,0:T(4,128)(2,1)S(1)} %get-tuple-element.29), channel_id=1, source_target_pairs={{0,8},{1,9},{2,10},{3,11},{4,12},{5,13},{6,14},{7,15},{8,0},{9,1},... | collective-permute-start | bytes 49160 | tf_op jit(solution)/shard_map/ppermute | solution.py:143
  28.5 4.2 %collective-permute-start.13 = (bf16[4,2048]{1,0:T(4,128)(2,1)S(1)}, bf16[4,2048]{1,0:T(4,128)(2,1)S(1)}, u32[]{:S(2)}, u32[]{:S(2)}) collective-permute-start(bf16[4,2048]{1,0:T(4,128)(2,1)S(1)} %get-tuple-element.30), channel_id=1, source_target_pairs={{0,4},{1,5},{2,6},{3,7},{4,0},{5,1},{6,2},{7,3},{8,12},{9,13},{10,... | collective-permute-start | bytes 49160 | tf_op jit(solution)/shard_map/ppermute | solution.py:143

commit v10 on v5

--- a/solution.py
+++ b/solution.py
@@ -140,7 +140,7 @@
     last, radix = len(steps) - 1, radices[-1]
     order = [radix - 1, *range(1, radix - 1)] if radix > 1 else []
     blocks = [swap(source, last, j) for j in order]
-    own = call(own_kernel, shape((block, depth), full), (source,), 2**36, 2**27)
+    own = call(own_kernel, shape((block, depth), full), (source,), 2**34, 2**25)
     size = radix * block
     kernel = functools.partial(normalise_kernel, order)
     blocks = [call(kernel, shape((size, depth), half), [own] + blocks, 2**34)]

time: 33.6 us -> 33.6 us (level)
    ppermute x2, starting transfers between devices: 0.07 us -> 0.52 us  [onward(): lax.ppermute(value, 'layer', [(i, (i + 1) % layers) for i in range(layers)])]
    ppermute x12, starting transfers between devices: 17.2 us -> 16.8 us  [swap(): return lax.ppermute(value, ('layer', 'feat'), pairs)]
    unnamed x12 -> x16, local copies, waits for them, and re-layouts: 0.81 us -> 0.83 us
where the time goes in v10:
time: 33.6 us; the launch traced here: 33.4 us
  starting transfers between devices  17.3 us (51%)
  waiting for transfers between devices  12.3 us (37%)
  Pallas kernels  2.91 us (9%)
  local copies, waits for them, and re-layouts  0.83 us (2%)
    ppermute x12, starting transfers between devices, swap(): return lax.ppermute(value, ('layer', 'feat'), pairs)  16.8 us
    ppermute x12, waiting for transfers between devices, swap(): return lax.ppermute(value, ('layer', 'feat'), pairs)  11.8 us
    pallas_call x7, Pallas kernels, call(): pl.pallas_call(kernel, out_shape=out_shape, in_specs=[VMEM] * len(args),...  2.91 us
    unnamed x16, local copies, waits for them, and re-layouts  0.83 us
  transfers between devices with their start and end apart: 14, of which 11 were waited for; matrix products, arithmetic and copies ran while one was open for 0% of the time, Pallas kernels for 7%

profile of v10, /device:TPU:0, one launch (start us, length us, event | category | flops | bytes accessed | tf_op | source)
XLA Modules:
  0.0 33.4 jit_solution(17107361799032042776)
XLA Ops:
  0.5 4.6 %collective-permute-start = (f32[1,4,2048]{2,1,0:T(4,128)}, f32[1,4,2048]{2,1,0:T(4,128)S(1)}, u32[]{:S(2)}, u32[]{:S(2)}) collective-permute-start(f32[1,4,2048]{2,1,0:T(4,128)} %rows_ref.1), channel_id=1, source_target_pairs={{0,12},{1,13},{2,14},{3,15},{4,8},{5,9},{6,10},{7,11},{8,4},{9,5},... | collective-permute-start | bytes 98312 | tf_op jit(solution)/shard_map/ppermute | solution.py:133
  5.1 0.6 %collective-permute-start.1 = (f32[1,4,2048]{2,1,0:T(4,128)}, f32[1,4,2048]{2,1,0:T(4,128)S(1)}, u32[]{:S(2)}, u32[]{:S(2)}) collective-permute-start(f32[1,4,2048]{2,1,0:T(4,128)} %rows_ref.1), channel_id=1, source_target_pairs={{0,4},{1,5},{2,6},{3,7},{4,0},{5,1},{6,2},{7,3},{8,12},{9,13},{10,... | collective-permute-start | bytes 98312 | tf_op jit(solution)/shard_map/ppermute | solution.py:133
  5.7 0.8 %copy-done.3 = f32[1,4,2048]{2,1,0:T(4,128)S(1)} copy-done((f32[1,4,2048]{2,1,0:T(4,128)S(1)}, f32[1,4,2048]{2,1,0:T(4,128)}, u32[]{:S(2)}) %copy-start.3) | copy-done | bytes 32792
  6.6 0.5 %collective-permute-done.refs_0_ = f32[1,4,2048]{2,1,0:T(4,128)S(1)} collective-permute-done((f32[1,4,2048]{2,1,0:T(4,128)}, f32[1,4,2048]{2,1,0:T(4,128)S(1)}, u32[]{:S(2)}, u32[]{:S(2)}) %collective-permute-start) | collective-permute-done | bytes 32800 | tf_op jit(solution)/shard_map/ppermute | solution.py:133
  7.2 2.9 %collective-permute-done.2.refs_2_ = f32[1,4,2048]{2,1,0:T(4,128)S(1)} collective-permute-done((f32[1,4,2048]{2,1,0:T(4,128)}, f32[1,4,2048]{2,1,0:T(4,128)S(1)}, u32[]{:S(2)}, u32[]{:S(2)}) %collective-permute-start.2) | collective-permute-done | bytes 32800 | tf_op jit(solution)/shard_map/ppermute | solution.py:133
  10.2 2.5 %collective-permute-start.5 = (bf16[16,2048]{1,0:T(8,128)(2,1)S(1)}, bf16[16,2048]{1,0:T(8,128)(2,1)S(1)}, u32[]{:S(2)}, u32[]{:S(2)}) collective-permute-start(bf16[16,2048]{1,0:T(8,128)(2,1)S(1)} %shard_map.74.refs_0_), channel_id=1, source_target_pairs={{0,3},{1,2},{2,1},{3,0},{4,7},{5,6},{6,5},{7,4},{8,11},{9,10},{10,... | collective-permute-start | bytes 196616 | tf_op jit(solution)/shard_map/ppermute | solution.py:133
  12.7 0.5 %collective-permute-start.4 = (bf16[16,2048]{1,0:T(8,128)(2,1)S(1)}, bf16[16,2048]{1,0:T(8,128)(2,1)S(1)}, u32[]{:S(2)}, u32[]{:S(2)}) collective-permute-start(bf16[16,2048]{1,0:T(8,128)(2,1)S(1)} %shard_map.74.refs_0_), channel_id=1, source_target_pairs={{0,2},{1,3},{2,0},{3,1},{4,6},{5,7},{6,4},{7,5},{8,10},{9,11},{10,... | collective-permute-start | bytes 196616 | tf_op jit(solution)/shard_map/ppermute | solution.py:133
  13.2 0.5 %collective-permute-start.3 = (bf16[16,2048]{1,0:T(8,128)(2,1)S(1)}, bf16[16,2048]{1,0:T(8,128)(2,1)S(1)}, u32[]{:S(2)}, u32[]{:S(2)}) collective-permute-start(bf16[16,2048]{1,0:T(8,128)(2,1)S(1)} %shard_map.74.refs_0_), channel_id=1, source_target_pairs={{0,1},{1,0},{2,3},{3,2},{4,5},{5,4},{6,7},{7,6},{8,9},{9,8},{10,11... | collective-permute-start | bytes 196616 | tf_op jit(solution)/shard_map/ppermute | solution.py:133
  13.8 1.7 %collective-permute-done.5.refs_3_ = bf16[16,2048]{1,0:T(8,128)(2,1)S(1)} collective-permute-done((bf16[16,2048]{1,0:T(8,128)(2,1)S(1)}, bf16[16,2048]{1,0:T(8,128)(2,1)S(1)}, u32[]{:S(2)}, u32[]{:S(2)}) %collective-permute-start.5) | collective-permute-done | bytes 65568 | tf_op jit(solution)/shard_map/ppermute | solution.py:133
  15.4 1.5 %collective-permute-done.4.refs_2_ = bf16[16,2048]{1,0:T(8,128)(2,1)S(1)} collective-permute-done((bf16[16,2048]{1,0:T(8,128)(2,1)S(1)}, bf16[16,2048]{1,0:T(8,128)(2,1)S(1)}, u32[]{:S(2)}, u32[]{:S(2)}) %collective-permute-start.4) | collective-permute-done | bytes 65568 | tf_op jit(solution)/shard_map/ppermute | solution.py:133
  17.0 0.5 %collective-permute-done.3.refs_1_ = bf16[16,2048]{1,0:T(8,128)(2,1)S(1)} collective-permute-done((bf16[16,2048]{1,0:T(8,128)(2,1)S(1)}, bf16[16,2048]{1,0:T(8,128)(2,1)S(1)}, u32[]{:S(2)}, u32[]{:S(2)}) %collective-permute-start.3) | collective-permute-done | bytes 65568 | tf_op jit(solution)/shard_map/ppermute | solution.py:133
  17.5 1.0 %shard_map.75.codes_ref = bf16[64,1536]{1,0:T(8,128)(2,1)S(1)} custom-call(bf16[16,2048]{1,0:T(8,128)(2,1)S(1)} %shard_map.74.refs_0_, bf16[16,2048]{1,0:T(8,128)(2,1)S(1)} %collective-permute-done.3.refs_1_, bf16[16,2048]{1,0:T(8,128)(2,1)S(1)} %collective-permute-done.4.refs_2_, bf16[16,2048]{1,0:T(8,128)(2,1)S(1)} %collective-permute-done.5.refs_3_, ...), custom_call_target="tpu_custom_call" | custom-call | flops 402653184 | bytes 262144 | tf_op jit(solution)/shard_map/pallas_call | solution.py:18
  18.6 1.0 %shard_map.76.own_ref = f32[64,2048]{1,0:T(8,128)S(1)} custom-call(bf16[64,1536]{1,0:T(8,128)(2,1)S(1)} %shard_map.75.codes_ref, bf16[1,1536,2048]{2,1,0:T(8,128)(2,1)S(1)} %bitcast.3), custom_call_target="tpu_custom_call" | custom-call | flops 402653184 | bytes 262144 | tf_op jit(solution)/shard_map/pallas_call | solution.py:18
  20.1 1.5 %collective-permute-start.8 = (bf16[16,2048]{1,0:T(8,128)(2,1)S(1)}, bf16[16,2048]{1,0:T(8,128)(2,1)S(1)}, u32[]{:S(2)}, u32[]{:S(2)}) collective-permute-start(bf16[16,2048]{1,0:T(8,128)(2,1)S(1)} %get-tuple-element.14), channel_id=1, source_target_pairs={{0,3},{1,2},{2,1},{3,0},{4,7},{5,6},{6,5},{7,4},{8,11},{9,10},{10,... | collective-permute-start | bytes 196616 | tf_op jit(solution)/shard_map/ppermute | solution.py:133
  21.6 0.5 %collective-permute-start.9 = (bf16[16,2048]{1,0:T(8,128)(2,1)S(1)}, bf16[16,2048]{1,0:T(8,128)(2,1)S(1)}, u32[]{:S(2)}, u32[]{:S(2)}) collective-permute-start(bf16[16,2048]{1,0:T(8,128)(2,1)S(1)} %get-tuple-element.15), channel_id=1, source_target_pairs={{0,2},{1,3},{2,0},{3,1},{4,6},{5,7},{6,4},{7,5},{8,10},{9,11},{10,... | collective-permute-start | bytes 196616 | tf_op jit(solution)/shard_map/ppermute | solution.py:133
  22.1 1.5 %collective-permute-start.10 = (bf16[16,2048]{1,0:T(8,128)(2,1)S(1)}, bf16[16,2048]{1,0:T(8,128)(2,1)S(1)}, u32[]{:S(2)}, u32[]{:S(2)}) collective-permute-start(bf16[16,2048]{1,0:T(8,128)(2,1)S(1)} %get-tuple-element.16), channel_id=1, source_target_pairs={{0,1},{1,0},{2,3},{3,2},{4,5},{5,4},{6,7},{7,6},{8,9},{9,8},{10,11... | collective-permute-start | bytes 196616 | tf_op jit(solution)/shard_map/ppermute | solution.py:133
  23.6 1.7 %collective-permute-done.8.refs_1_ = bf16[16,2048]{1,0:T(8,128)(2,1)S(1)} collective-permute-done((bf16[16,2048]{1,0:T(8,128)(2,1)S(1)}, bf16[16,2048]{1,0:T(8,128)(2,1)S(1)}, u32[]{:S(2)}, u32[]{:S(2)}) %collective-permute-start.8) | collective-permute-done | bytes 65568 | tf_op jit(solution)/shard_map/ppermute | solution.py:133
  25.3 0.7 %collective-permute-done.9.refs_2_ = bf16[16,2048]{1,0:T(8,128)(2,1)S(1)} collective-permute-done((bf16[16,2048]{1,0:T(8,128)(2,1)S(1)}, bf16[16,2048]{1,0:T(8,128)(2,1)S(1)}, u32[]{:S(2)}, u32[]{:S(2)}) %collective-permute-start.9) | collective-permute-done | bytes 65568 | tf_op jit(solution)/shard_map/ppermute | solution.py:133
  26.5 1.6 %collective-permute-start.11 = (bf16[4,2048]{1,0:T(4,128)(2,1)S(1)}, bf16[4,2048]{1,0:T(4,128)(2,1)S(1)}, u32[]{:S(2)}, u32[]{:S(2)}) collective-permute-start(bf16[4,2048]{1,0:T(4,128)(2,1)S(1)} %get-tuple-element.18), channel_id=1, source_target_pairs={{0,12},{1,13},{2,14},{3,15},{4,8},{5,9},{6,10},{7,11},{8,4},{9,5},... | collective-permute-start | bytes 49160 | tf_op jit(solution)/shard_map/ppermute | solution.py:133
  28.0 0.6 %collective-permute-start.12 = (bf16[4,2048]{1,0:T(4,128)(2,1)S(1)}, bf16[4,2048]{1,0:T(4,128)(2,1)S(1)}, u32[]{:S(2)}, u32[]{:S(2)}) collective-permute-start(bf16[4,2048]{1,0:T(4,128)(2,1)S(1)} %get-tuple-element.19), channel_id=1, source_target_pairs={{0,8},{1,9},{2,10},{3,11},{4,12},{5,13},{6,14},{7,15},{8,0},{9,1},... | collective-permute-start | bytes 49160 | tf_op jit(solution)/shard_map/ppermute | solution.py:133
  28.6 2.3 %collective-permute-start.13 = (bf16[4,2048]{1,0:T(4,128)(2,1)S(1)}, bf16[4,2048]{1,0:T(4,128)(2,1)S(1)}, u32[]{:S(2)}, u32[]{:S(2)}) collective-permute-start(bf16[4,2048]{1,0:T(4,128)(2,1)S(1)} %get-tuple-element.20), channel_id=1, source_target_pairs={{0,4},{1,5},{2,6},{3,7},{4,0},{5,1},{6,2},{7,3},{8,12},{9,13},{10,... | collective-permute-start | bytes 49160 | tf_op jit(solution)/shard_map/ppermute | solution.py:133
  30.9 1.1 %collective-permute-done.11.refs_1_ = bf16[4,2048]{1,0:T(4,128)(2,1)S(1)} collective-permute-done((bf16[4,2048]{1,0:T(4,128)(2,1)S(1)}, bf16[4,2048]{1,0:T(4,128)(2,1)S(1)}, u32[]{:S(2)}, u32[]{:S(2)}) %collective-permute-start.11) | collective-permute-done | bytes 16416 | tf_op jit(solution)/shard_map/ppermute | solution.py:133
  32.1 0.7 %collective-permute-done.12.refs_2_ = bf16[4,2048]{1,0:T(4,128)(2,1)S(1)} collective-permute-done((bf16[4,2048]{1,0:T(4,128)(2,1)S(1)}, bf16[4,2048]{1,0:T(4,128)(2,1)S(1)}, u32[]{:S(2)}, u32[]{:S(2)}) %collective-permute-start.12) | collective-permute-done | bytes 16416 | tf_op jit(solution)/shard_map/ppermute | solution.py:133
  32.8 0.6 %shard_map.79 = f32[1,4,2048]{2,1,0:T(4,128)} custom-call(bf16[4,2048]{1,0:T(4,128)(2,1)S(1)} %get-tuple-element.17.refs_0_, bf16[4,2048]{1,0:T(4,128)(2,1)S(1)} %collective-permute-done.11.refs_1_, bf16[4,2048]{1,0:T(4,128)(2,1)S(1)} %collective-permute-done.12.refs_2_, bf16[4,2048]{1,0:T(4,128)(2,1)S(1)} %collective-permute-done.13.refs_3_, ...), custom_call_target="tpu_custom_call" | custom-call | bytes 262144 | tf_op jit(solution)/shard_map/pallas_call | solution.py:18
  (29 shorter events, 1.7 us)
Async XLA Ops:
  0.0 20.1 %collective-permute-start.7 = (bf16[1,1536,2048]{2,1,0:T(8,128)(2,1)}, bf16[1,1536,2048]{2,1,0:T(8,128)(2,1)S(1)}, u32[]{:S(2)}, u32[]{:S(2)}) collective-permute-start(bf16[1,1536,2048]{2,1,0:T(8,128)(2,1)} %param.12), channel_id=1, source_target_pairs={{0,16},{16,0},{1,17},{17,1},{2,18},{18,2},{3,19},{19,3},{4,20},{20... | collective-permute-start | bytes 18874376 | tf_op jit(solution)/shard_map/ppermute | solution.py:136
  0.5 6.7 %collective-permute-start = (f32[1,4,2048]{2,1,0:T(4,128)}, f32[1,4,2048]{2,1,0:T(4,128)S(1)}, u32[]{:S(2)}, u32[]{:S(2)}) collective-permute-start(f32[1,4,2048]{2,1,0:T(4,128)} %rows_ref.1), channel_id=1, source_target_pairs={{0,12},{1,13},{2,14},{3,15},{4,8},{5,9},{6,10},{7,11},{8,4},{9,5},... | collective-permute-start | bytes 98312 | tf_op jit(solution)/shard_map/ppermute | solution.py:133
  5.1 5.0 %collective-permute-start.2 = (f32[1,4,2048]{2,1,0:T(4,128)}, f32[1,4,2048]{2,1,0:T(4,128)S(1)}, u32[]{:S(2)}, u32[]{:S(2)}) collective-permute-start(f32[1,4,2048]{2,1,0:T(4,128)} %rows_ref.1), channel_id=1, source_target_pairs={{0,8},{1,9},{2,10},{3,11},{4,12},{5,13},{6,14},{7,15},{8,0},{9,1},... | collective-permute-start | bytes 98312 | tf_op jit(solution)/shard_map/ppermute | solution.py:133
  5.1 5.0 %collective-permute-start.1 = (f32[1,4,2048]{2,1,0:T(4,128)}, f32[1,4,2048]{2,1,0:T(4,128)S(1)}, u32[]{:S(2)}, u32[]{:S(2)}) collective-permute-start(f32[1,4,2048]{2,1,0:T(4,128)} %rows_ref.1), channel_id=1, source_target_pairs={{0,4},{1,5},{2,6},{3,7},{4,0},{5,1},{6,2},{7,3},{8,12},{9,13},{10,... | collective-permute-start | bytes 98312 | tf_op jit(solution)/shard_map/ppermute | solution.py:133
  5.7 0.8 %copy-start.3 = (f32[1,4,2048]{2,1,0:T(4,128)S(1)}, f32[1,4,2048]{2,1,0:T(4,128)}, u32[]{:S(2)}) copy-start(f32[1,4,2048]{2,1,0:T(4,128)} %rows_ref.1) | copy-start | bytes 98308
  6.5 11.0 %slice-start = ((s8[6291456]{0:T(1024)(128)(4,1)}), s8[4194304]{0:T(1024)(128)(4,1)S(1)}, s32[]{:S(2)}) async-start(s8[6291456]{0:T(1024)(128)(4,1)} %bitcast), calls=%async_computation | async-start | bytes 8388608
  6.5 12.1 %slice-start.2 = ((s8[6291456]{0:T(1024)(128)(4,1)}), s8[4194304]{0:T(1024)(128)(4,1)S(1)}, s32[]{:S(2)}) async-start(s8[6291456]{0:T(1024)(128)(4,1)} %bitcast.2), calls=%async_computation.2 | async-start | bytes 8388608
  6.6 10.9 %slice-start.1 = ((s8[6291456]{0:T(1024)(128)(4,1)}), s8[2097152]{0:T(1024)(128)(4,1)S(1)}, s32[]{:S(2)}) async-start(s8[6291456]{0:T(1024)(128)(4,1)} %bitcast), calls=%async_computation.1 | async-start | bytes 4194304
  6.6 10.9 %copy-start.1 = (f32[1,1536]{1,0:T(1,128)S(1)}, f32[1,1536]{1,0:T(1,128)}, u32[]{:S(2)}) copy-start(f32[1,1536]{1,0:T(1,128)} %refs_5_.1) | copy-start | bytes 18436
  6.6 10.9 %copy-start.2 = (f32[1,1536]{1,0:T(1,128)S(1)}, f32[1,1536]{1,0:T(1,128)}, u32[]{:S(2)}) copy-start(f32[1,1536]{1,0:T(1,128)} %refs_6_.1) | copy-start | bytes 18436
  6.6 12.0 %slice-start.3 = ((s8[6291456]{0:T(1024)(128)(4,1)}), s8[2097152]{0:T(1024)(128)(4,1)S(1)}, s32[]{:S(2)}) async-start(s8[6291456]{0:T(1024)(128)(4,1)} %bitcast.2), calls=%async_computation.3 | async-start | bytes 4194304
  10.2 5.2 %collective-permute-start.5 = (bf16[16,2048]{1,0:T(8,128)(2,1)S(1)}, bf16[16,2048]{1,0:T(8,128)(2,1)S(1)}, u32[]{:S(2)}, u32[]{:S(2)}) collective-permute-start(bf16[16,2048]{1,0:T(8,128)(2,1)S(1)} %shard_map.74.refs_0_), channel_id=1, source_target_pairs={{0,3},{1,2},{2,1},{3,0},{4,7},{5,6},{6,5},{7,4},{8,11},{9,10},{10,... | collective-permute-start | bytes 196616 | tf_op jit(solution)/shard_map/ppermute | solution.py:133
  12.7 4.3 %collective-permute-start.4 = (bf16[16,2048]{1,0:T(8,128)(2,1)S(1)}, bf16[16,2048]{1,0:T(8,128)(2,1)S(1)}, u32[]{:S(2)}, u32[]{:S(2)}) collective-permute-start(bf16[16,2048]{1,0:T(8,128)(2,1)S(1)} %shard_map.74.refs_0_), channel_id=1, source_target_pairs={{0,2},{1,3},{2,0},{3,1},{4,6},{5,7},{6,4},{7,5},{8,10},{9,11},{10,... | collective-permute-start | bytes 196616 | tf_op jit(solution)/shard_map/ppermute | solution.py:133
  13.2 4.3 %collective-permute-start.3 = (bf16[16,2048]{1,0:T(8,128)(2,1)S(1)}, bf16[16,2048]{1,0:T(8,128)(2,1)S(1)}, u32[]{:S(2)}, u32[]{:S(2)}) collective-permute-start(bf16[16,2048]{1,0:T(8,128)(2,1)S(1)} %shard_map.74.refs_0_), channel_id=1, source_target_pairs={{0,1},{1,0},{2,3},{3,2},{4,5},{5,4},{6,7},{7,6},{8,9},{9,8},{10,11... | collective-permute-start | bytes 196616 | tf_op jit(solution)/shard_map/ppermute | solution.py:133
  18.5 14.3 %copy-start = (f32[1,4,2048]{2,1,0:T(4,128)S(1)}, f32[1,4,2048]{2,1,0:T(4,128)}, u32[]{:S(2)}) copy-start(f32[1,4,2048]{2,1,0:T(4,128)} %refs_4_.3) | copy-start | bytes 98308
  18.5 1.5 %collective-permute-start.6 = (bf16[64,1536]{1,0:T(8,128)(2,1)S(1)}, bf16[64,1536]{1,0:T(8,128)(2,1)S(1)}, u32[]{:S(2)}, u32[]{:S(2)}) collective-permute-start(bf16[64,1536]{1,0:T(8,128)(2,1)S(1)} %shard_map.75.codes_ref), channel_id=1, source_target_pairs={{0,16},{16,0},{1,17},{17,1},{2,18},{18,2},{3,19},{19,3},{4,20},{20... | collective-permute-start | bytes 589832 | tf_op jit(solution)/shard_map/ppermute | solution.py:136
  20.1 5.2 %collective-permute-start.8 = (bf16[16,2048]{1,0:T(8,128)(2,1)S(1)}, bf16[16,2048]{1,0:T(8,128)(2,1)S(1)}, u32[]{:S(2)}, u32[]{:S(2)}) collective-permute-start(bf16[16,2048]{1,0:T(8,128)(2,1)S(1)} %get-tuple-element.14), channel_id=1, source_target_pairs={{0,3},{1,2},{2,1},{3,0},{4,7},{5,6},{6,5},{7,4},{8,11},{9,10},{10,... | collective-permute-start | bytes 196616 | tf_op jit(solution)/shard_map/ppermute | solution.py:133
  21.6 4.4 %collective-permute-start.9 = (bf16[16,2048]{1,0:T(8,128)(2,1)S(1)}, bf16[16,2048]{1,0:T(8,128)(2,1)S(1)}, u32[]{:S(2)}, u32[]{:S(2)}) collective-permute-start(bf16[16,2048]{1,0:T(8,128)(2,1)S(1)} %get-tuple-element.15), channel_id=1, source_target_pairs={{0,2},{1,3},{2,0},{3,1},{4,6},{5,7},{6,4},{7,5},{8,10},{9,11},{10,... | collective-permute-start | bytes 196616 | tf_op jit(solution)/shard_map/ppermute | solution.py:133
  22.1 4.3 %collective-permute-start.10 = (bf16[16,2048]{1,0:T(8,128)(2,1)S(1)}, bf16[16,2048]{1,0:T(8,128)(2,1)S(1)}, u32[]{:S(2)}, u32[]{:S(2)}) collective-permute-start(bf16[16,2048]{1,0:T(8,128)(2,1)S(1)} %get-tuple-element.16), channel_id=1, source_target_pairs={{0,1},{1,0},{2,3},{3,2},{4,5},{5,4},{6,7},{7,6},{8,9},{9,8},{10,11... | collective-permute-start | bytes 196616 | tf_op jit(solution)/shard_map/ppermute | solution.py:133
  26.5 5.6 %collective-permute-start.11 = (bf16[4,2048]{1,0:T(4,128)(2,1)S(1)}, bf16[4,2048]{1,0:T(4,128)(2,1)S(1)}, u32[]{:S(2)}, u32[]{:S(2)}) collective-permute-start(bf16[4,2048]{1,0:T(4,128)(2,1)S(1)} %get-tuple-element.18), channel_id=1, source_target_pairs={{0,12},{1,13},{2,14},{3,15},{4,8},{5,9},{6,10},{7,11},{8,4},{9,5},... | collective-permute-start | bytes 49160 | tf_op jit(solution)/shard_map/ppermute | solution.py:133
  28.0 4.7 %collective-permute-start.12 = (bf16[4,2048]{1,0:T(4,128)(2,1)S(1)}, bf16[4,2048]{1,0:T(4,128)(2,1)S(1)}, u32[]{:S(2)}, u32[]{:S(2)}) collective-permute-start(bf16[4,2048]{1,0:T(4,128)(2,1)S(1)} %get-tuple-element.19), channel_id=1, source_target_pairs={{0,8},{1,9},{2,10},{3,11},{4,12},{5,13},{6,14},{7,15},{8,0},{9,1},... | collective-permute-start | bytes 49160 | tf_op jit(solution)/shard_map/ppermute | solution.py:133
  28.6 4.2 %collective-permute-start.13 = (bf16[4,2048]{1,0:T(4,128)(2,1)S(1)}, bf16[4,2048]{1,0:T(4,128)(2,1)S(1)}, u32[]{:S(2)}, u32[]{:S(2)}) collective-permute-start(bf16[4,2048]{1,0:T(4,128)(2,1)S(1)} %get-tuple-element.20), channel_id=1, source_target_pairs={{0,4},{1,5},{2,6},{3,7},{4,0},{5,1},{6,2},{7,3},{8,12},{9,13},{10,... | collective-permute-start | bytes 49160 | tf_op jit(solution)/shard_map/ppermute | solution.py:133
